TPU v7x, 128 devices: a whole 4x4x4 slice. The times are simulated.
128 devices in a mesh: grp: 4 (over x), bulk: 32 (over y, z, core).
Axes of the slice: x: 4, y: 4, z: 4, core: 2. Of those that a mesh axis runs over, the one named last changes fastest.
Arguments:
- embeddings: bfloat16 [49152, 768], P(('grp', 'bulk')), may hold values from -100 to 100
- cluster_ids: int32 [49152], P(('grp', 'bulk')), may hold values from 0 to 255, as said below
Outputs:
- redundancy: float32 [49152], P(('grp', 'bulk'))
Inputs may be any that keep to these rules, and one draw needn't show every extreme that they name: `cluster_ids`: the cluster group of a row is its id // 64; every aligned block of 384 rows holds exactly 96 rows of each cluster group.
All inputs are finite; a program needn't handle non-finite values.
Results may differ from a plain program's by a relative error of at most 0.0015.
Values may be sent and summed in bfloat16 or wider, within the bound.
No kernel may reach another device: no remote copies, remote signals or barrier semaphores. Data moves between devices by JAX's collectives and lax.ppermute only.
A program may use at most 64 MiB of HBM per device.

v0:
```python
import jax
import jax.numpy as jnp
from jax import lax
from jax.sharding import PartitionSpec as P

CL_DEV = 2


TEMP = 0.05


def unit_rows(embeddings):
    values = embeddings.astype(jnp.float32)
    scale = lax.rsqrt(jnp.sum(values * values, axis=1, keepdims=True) + 1e-06)
    return (values * scale).astype(jnp.bfloat16)


def tile_terms(queries, query_ids, keys, key_ids, query_start):
    similarity = lax.dot_general(
        queries, keys, (((1,), (1,)), ((), ())), preferred_element_type=jnp.float32
    )
    rows_here = query_start + jnp.arange(queries.shape[0], dtype=jnp.int32)
    cols_here = jnp.arange(keys.shape[0], dtype=jnp.int32)
    keep = (query_ids[:, None] == key_ids[None, :]) & (rows_here[:, None] != cols_here[None, :])
    return jnp.where(keep, jnp.exp((similarity - 1.0) / TEMP), jnp.float32(0.0))


def pair_sums(queries, query_ids, keys, key_ids, query_start):
    terms = tile_terms(queries, query_ids, keys, key_ids, query_start)
    return (jnp.sum(terms, axis=1), None)


def shards(embeddings, cluster_ids):
    n_grp = lax.axis_size("grp")
    n_bulk = lax.axis_size("bulk")
    rows = embeddings.shape[0]
    width = embeddings.shape[1]
    share = rows // n_grp
    cl_grp = CL_DEV * n_bulk
    units = unit_rows(embeddings)
    order = jnp.argsort(cluster_ids // cl_grp, stable=True)
    outgoing = (units[order].reshape(n_grp, share, width), cluster_ids[order].reshape(n_grp, share))
    queries, query_ids = (
        lax.all_to_all(outgoing[0], "grp", split_axis=0, concat_axis=0, tiled=True),
        lax.all_to_all(outgoing[1], "grp", split_axis=0, concat_axis=0, tiled=True),
    )
    queries = queries.reshape(rows, width)
    query_ids = query_ids.reshape(rows)
    arranged = jnp.arange(rows, dtype=jnp.int32)
    own_start = lax.axis_index("bulk") * rows
    row_sums, unused = pair_sums(
        queries,
        query_ids,
        lax.all_gather(queries, "bulk", axis=0, tiled=True),
        lax.all_gather(query_ids, "bulk", axis=0, tiled=True),
        own_start,
    )
    masses = row_sums
    masses = jnp.zeros((rows,), jnp.float32).at[arranged].set(masses)
    scores = jnp.log1p(masses)
    back = lax.all_to_all(
        scores.reshape(n_grp, share), "grp", split_axis=0, concat_axis=0, tiled=True
    ).reshape(rows)
    return jnp.zeros((rows,), jnp.float32).at[order].set(back)


def solution(mesh):
    placed = (P(("grp", "bulk"), None), P(("grp", "bulk")))
    return jax.shard_map(
        shards, mesh=mesh, in_specs=placed, out_specs=P(("grp", "bulk")), check_vma=False
    )
```

profile of v0, /device:TPU:0, one launch (start us, length us, event | category | flops | bytes accessed | tf_op | source)
XLA Modules:
  0.0 146.2 jit_solution(1863413525804550793)
XLA Ops:
  6.5 0.7 add_select_fusion
  7.2 3.8 %sort.17 = (s32[384]{0:T(512)}, s32[384]{0:T(512)S(1)}) sort(s32[384]{0:T(512)S(1)} %add_select_fusion, s32[384]{0:T(512)S(1)} %iota.17), dimensions={0}, to_apply=%region_0.0 | sort | flops 3456 | bytes 6144 | tf_op jit(solution)/shard_map/jit(argsort)/sort | solution.py:41
  11.0 1.3 fusion.1
  12.3 1.2 fusion.2
  13.5 2.2 %gather_fusion.1 = bf16[384,768]{1,0:T(8,128)(2,1)S(1)} fusion(bf16[384,768]{1,0:T(8,128)(2,1)S(1)} %fusion.2, s32[1024]{0:T(1024)S(1)} %pad_clamp_fusion), kind=kCustom, calls=%fused_computation.1 | custom fusion | bytes 1181184 | tf_op jit(solution)/shard_map/gather | solution.py:42
  15.7 14.5 %all_to_all.23 = bf16[4,96,768]{2,1,0:T(8,128)(2,1)} all-to-all(bf16[4,96,768]{2,1,0:T(8,128)(2,1)S(1)} %bitcast.6), channel_id=1, replica_groups=mesh['grp'=4,'bulk'=32] {'grp'}, dimensions={0} | all-to-all | bytes 1179648 | tf_op jit(solution)/shard_map/all_to_all | solution.py:44
  30.2 3.6 %gather_fusion = s32[384]{0:T(512)S(1)} fusion(s32[384]{0:T(512)} %param.3, s32[1024]{0:T(1024)S(1)} %pad_clamp_fusion), kind=kCustom, calls=%fused_computation | custom fusion | bytes 4608 | tf_op jit(solution)/shard_map/gather | solution.py:42
  33.8 0.7 all_to_all.15
  34.5 3.2 %all-to-all-start = ((s32[4,1,96]{2,1,0:T(1,128)}), s32[4,1,96]{2,1,0:T(1,128)S(1)}, u32[]{:S(2)}, u32[]{:S(2)}) async-start(s32[4,1,96]{2,1,0:T(1,128)} %all_to_all.15), calls=%async_computation | async-start | bytes 4096 | tf_op jit(solution)/shard_map/all_to_all | solution.py:45
  37.7 5.1 %all-to-all-done = s32[4,1,96]{2,1,0:T(1,128)S(1)} async-done(((s32[4,1,96]{2,1,0:T(1,128)}), s32[4,1,96]{2,1,0:T(1,128)S(1)}, u32[]{:S(2)}, u32[]{:S(2)}) %all-to-all-start) | async-done | bytes 1568 | tf_op jit(solution)/shard_map/all_to_all | solution.py:45
  42.8 0.1 reshape.71
  42.9 0.5 broadcast.55
  43.4 0.7 reduce.8
  44.1 0.1 eq.15
  44.2 25.6 %all-gather = s32[32,1,384]{2,1,0:T(1,128)S(1)} all-gather(s32[1,1,384]{2,1,0:T(1,128)S(1)} %reshape.71), channel_id=1, replica_groups=mesh['grp'=4,'bulk'=32] {'bulk'}, dimensions={0}, use_global_device_ids=true | all-gather | bytes 50688 | tf_op jit(solution)/shard_map/all_gather | solution.py:55
  69.8 38.6 %all-gather.3.cloned.1.call-done = bf16[12288,768]{1,0:T(8,128)(2,1)} async-done(((bf16[384,768]{1,0:T(8,128)(2,1)}), bf16[12288,768]{1,0:T(8,128)(2,1)}) %all-gather.3.cloned.1.call-update) | async-done | bytes 18874384 | tf_op jit(solution)/shard_map/all_gather | solution.py:54
  108.4 13.9 %select_reduce_fusion = f32[384]{0:T(512)S(1)} fusion(bf16[384,768]{1,0:T(8,128)(2,1)} %bitcast.8, bf16[12288,768]{1,0:T(8,128)(2,1)} %all-gather.3.cloned.1.call-done, s32[384]{0:T(512)S(1)} %iota_add_fusion, s32[12288]{0:T(1024)S(1)} %bitcast.9, s32[384]{0:T(512)S(1)} %eq.15), kind=kOutput, calls=%fused_computation.4 | convolution fusion | flops 7280786944 | bytes 19517952 | tf_op jit(solution)/shard_map/dot_general | solution.py:19
  122.3 2.9 %scatter_custom_fusion = f32[384]{0:T(512)S(1)} fusion(s32[384]{0:T(512)S(1)} %iota.20, f32[384]{0:T(512)S(1)} %select_reduce_fusion, f32[]{:T(128)} %constant.12.clone.1), kind=kCustom, calls=%fused_computation.24 | custom fusion | bytes 1540 | tf_op jit(solution)/shard_map/scatter | solution.py:59
  125.3 0.1 all_to_all.18
  125.4 9.3 %all_to_all.24 = f32[4,1,96]{2,1,0:T(1,128)S(1)} all-to-all(f32[4,1,96]{2,1,0:T(1,128)S(1)} %all_to_all.18), channel_id=1, replica_groups=mesh['grp'=4,'bulk'=32] {'grp'}, dimensions={0} | all-to-all | bytes 3072 | tf_op jit(solution)/shard_map/all_to_all | solution.py:61
  134.6 0.5 broadcast.56
  135.1 0.7 reduce.9
  135.8 0.1 reshape.64
  135.9 3.5 %scatter_custom_fusion.1 = f32[384]{0:T(512)} fusion(s32[384]{0:T(512)S(1)} %compare_select_fusion, f32[384]{0:T(512)S(1)} %reshape.64, f32[]{:T(128)} %constant.12.clone.1), kind=kCustom, calls=%fused_computation.22 | custom fusion | bytes 1540 | tf_op jit(solution)/shard_map/scatter | solution.py:64
  (9 shorter events, 0.1 us)
Async XLA Ops:
  6.5 101.9 %all-gather.3.cloned.1.call-start = ((), (), s32[]{:S(2)}) async-start(), calls=%async_computation.3 | async-start | bytes 19464192 | tf_op jit(solution)/shard_map/all_gather | solution.py:54
  34.5 8.4 %all-to-all-start = ((s32[4,1,96]{2,1,0:T(1,128)}), s32[4,1,96]{2,1,0:T(1,128)S(1)}, u32[]{:S(2)}, u32[]{:S(2)}) async-start(s32[4,1,96]{2,1,0:T(1,128)} %all_to_all.15), calls=%async_computation | async-start | bytes 4096 | tf_op jit(solution)/shard_map/all_to_all | solution.py:45
Sparse Core Ops, SparseCore 0:
  30.3 78.0 all-gather.2
where the time goes:
time: 147 us; the launch traced here: 146 us
  blocking collectives  49.4 us (34%)
  waiting for transfers between devices  43.7 us (30%)
  local copies, waits for them, and re-layouts  14.2 us (10%)
  matrix products  13.9 us (9%)
  between operations  13.5 us (9%)
  other arithmetic  8.3 us (6%)
  starting transfers between devices  3.22 us (2%)
    all_gather x1, waiting for transfers between devices, shards(): lax.all_gather(queries, 'bulk', axis=0, tiled=True)  38.6 us
    all_gather x1, blocking collectives, shards(): lax.all_gather(query_ids, 'bulk', axis=0, tiled=True)  25.6 us
    all_to_all x1, blocking collectives, shards(): lax.all_to_all(outgoing[0], 'grp', split_axis=0, concat_axis=0, tiled=True)  14.5 us
    dot_general x1, matrix products, tile_terms(): lax.dot_general(queries, keys, (((1,), (1,)), ((), ())), preferred_elemen...  13.9 us
    all_to_all x1, blocking collectives, shards(): lax.all_to_all(scores.reshape(n_grp, share), 'grp', split_axis=0, concat_...  9.27 us
    all_to_all x1, waiting for transfers between devices, shards(): lax.all_to_all(outgoing[1], 'grp', split_axis=0, concat_axis=0, tiled=True)  5.13 us
    sort x1, other arithmetic, shards(): order = jnp.argsort(cluster_ids // cl_grp, stable=True)  3.77 us
    gather x1, local copies, waits for them, and re-layouts, shards(): cluster_ids[order].reshape(n_grp, share)  3.62 us
  transfers between devices with their start and end apart: 2, of which 2 were waited for; matrix products, arithmetic and copies ran while one was open for 3% of the time, Pallas kernels for 0%

commit v1 on v0

v1 whole, which is shorter than its diff:
```python
import functools

import jax
import jax.numpy as jnp
import numpy as np
from jax import lax
from jax.experimental import pallas as pl
from jax.experimental.pallas import tpu as pltpu
from jax.sharding import Mesh
from jax.sharding import PartitionSpec as P

CL_GRP = 64
GROUPS = 4
TEMP = 0.05
RATE = 1.4426950408889634 / TEMP
AXES = ("x", "y", "z", "c")
SIZES = (4, 4, 4, 2)
TAIL = 16
VMEM_LIMIT = 48 * 1024 * 1024


def iotas(rows, cols):
    return (
        lax.broadcasted_iota(jnp.int32, (rows, cols), 0),
        lax.broadcasted_iota(jnp.int32, (rows, cols), 1),
    )


def as_column(row):
    n = row.shape[1]
    down, across = iotas(n, n)
    return jnp.sum(jnp.where(down == across, row, 0.0), axis=1, keepdims=True)


def prepare_kernel(x_ref, emb_ref, ids_ref, c0_ref, c1_ref, c2_ref, c3_ref, pos_ref):
    rows = emb_ref.shape[0]
    share = rows // GROUPS
    values = emb_ref[...].astype(jnp.float32)
    scale = lax.rsqrt(jnp.sum(values * values, axis=1, keepdims=True) + 1e-06)
    units = (values * scale).astype(jnp.bfloat16)
    ids = ids_ref[...]
    down, across = iotas(rows, rows)
    steps = (lax.shift_right_logical(ids, 6) - x_ref[0]) & (GROUPS - 1)
    key = (steps * rows + across[:1]).astype(jnp.float32)
    pos = jnp.sum(jnp.where(as_column(key) < key, 1.0, 0.0), axis=0, keepdims=True)
    pos_ref[...] = pos
    place = jnp.where(down.astype(jnp.float32) == pos, 1.0, 0.0).astype(jnp.bfloat16)
    placed = jnp.dot(place, units, preferred_element_type=jnp.float32).astype(jnp.bfloat16)
    wide = jnp.broadcast_to(ids.astype(jnp.float32), (TAIL, rows)).astype(jnp.bfloat16)
    placed_ids = lax.dot_general(
        wide, place, (((1,), (1,)), ((), ())), preferred_element_type=jnp.float32
    )
    chunk_of = lax.broadcasted_iota(jnp.int32, (TAIL, rows), 1)
    for k, out in enumerate((c0_ref, c1_ref, c2_ref, c3_ref)):
        out[:share, :] = placed[k * share : (k + 1) * share]
        here = (chunk_of >= k * share) & (chunk_of < (k + 1) * share)
        out[share:, :rows] = jnp.where(here, placed_ids, 0.0).astype(jnp.bfloat16)
        out[share:, rows:] = jnp.zeros((TAIL, out.shape[1] - rows), jnp.bfloat16)


def prepare(x_index, embeddings, ids):
    rows, width = embeddings.shape
    share = rows // GROUPS
    chunk = jax.ShapeDtypeStruct((share + TAIL, width), jnp.bfloat16)
    return pl.pallas_call(
        prepare_kernel,
        out_shape=[chunk] * GROUPS + [jax.ShapeDtypeStruct((1, rows), jnp.float32)],
        in_specs=[
            pl.BlockSpec(memory_space=pltpu.SMEM),
            pl.BlockSpec(memory_space=pltpu.VMEM),
            pl.BlockSpec(memory_space=pltpu.VMEM),
        ],
        compiler_params=pltpu.CompilerParams(vmem_limit_bytes=VMEM_LIMIT),
        name="prepare",
    )(x_index, embeddings, ids)


def join_kernel(c0_ref, c1_ref, c2_ref, c3_ref, out_ref):
    chunks = (c0_ref, c1_ref, c2_ref, c3_ref)
    share = c0_ref.shape[0] - TAIL
    tail = 0.0
    for k, chunk in enumerate(chunks):
        out_ref[k * share : (k + 1) * share, :] = chunk[:share, :]
        tail += chunk[share:, :].astype(jnp.float32)
    out_ref[GROUPS * share :, :] = tail.astype(jnp.bfloat16)


def join(chunks):
    share = chunks[0].shape[0] - TAIL
    return pl.pallas_call(
        join_kernel,
        out_shape=jax.ShapeDtypeStruct((GROUPS * share + TAIL, chunks[0].shape[1]), jnp.bfloat16),
        compiler_params=pltpu.CompilerParams(vmem_limit_bytes=VMEM_LIMIT),
        name="join",
    )(*chunks)


def pairs_kernel(nq, nk, plan, same, *refs):
    queries, keys = refs[:nq], refs[nq : nq + nk]
    out_ref, q_buf, k_buf, q_ids, k_ids, acc, sems = refs[nq + nk :]
    rows = q_ids.shape[2]
    copies = {}

    def fetch(kind, index):
        if (kind, index) in copies:
            return
        source, rows_buf, ids_buf = (
            (queries[index], q_buf, q_ids) if kind == "q" else (keys[index], k_buf, k_ids)
        )
        slot = 2 * (index if kind == "q" else nq + index)
        pair = [
            pltpu.make_async_copy(
                source.at[pl.ds(0, rows), :], rows_buf.at[pl.ds(index * rows, rows), :], sems.at[slot]
            ),
            pltpu.make_async_copy(
                source.at[pl.ds(rows, TAIL), pl.ds(0, rows)], ids_buf.at[index], sems.at[slot + 1]
            ),
        ]
        for copy in pair:
            copy.start()
        copies[kind, index] = pair

    for k, first, count in plan:
        for q in range(first, first + count):
            fetch("q", q)
        fetch("k", k)
    acc[...] = jnp.zeros_like(acc)
    done = set()

    def arrived(kind, index):
        if (kind, index) not in done:
            done.add((kind, index))
            for copy in copies[kind, index]:
                copy.wait()

    for step, (k, first, count) in enumerate(plan):
        for q in range(first, first + count):
            arrived("q", q)
        arrived("k", k)
        id_row = k_ids[k][:1].astype(jnp.float32)
        key_ids = jnp.transpose(jnp.broadcast_to(id_row, (128, rows)))
        key_rows = k_buf[k * rows : (k + 1) * rows, :]
        at = first
        while at < first + count:
            n = min(2, first + count - at)
            similarity = lax.dot_general(
                key_rows,
                q_buf[at * rows : (at + n) * rows, :],
                (((1,), (1,)), ((), ())),
                preferred_element_type=jnp.float32,
            )
            for q in range(at, at + n):
                query_ids = q_ids[q][:1].astype(jnp.float32)
                for lane in range(0, rows, 128):
                    col = (q - at) * rows + lane
                    tile = similarity[:, col : col + 128]
                    keep = key_ids == query_ids[:, lane : lane + 128]
                    if step == same:
                        down, across = iotas(rows, 128)
                        keep = keep & (down != across + lane)
                    terms = jnp.where(keep, jnp.exp2((tile - 1.0) * RATE), 0.0)
                    acc[:, q * rows + lane : q * rows + lane + 128] += jnp.sum(
                        terms.reshape(rows // 8, 8, 128), axis=0
                    )
            at += n
    for q in range(nq):
        out_ref[q] = jnp.sum(acc[:, q * rows : (q + 1) * rows], axis=0, keepdims=True)


def pair_sums(queries, keys, plan, same=None, name="pairs"):
    rows, width = queries[0].shape[0] - TAIL, queries[0].shape[1]
    nq, nk = len(queries), len(keys)
    products = sum(count for _, _, count in plan) * rows * rows
    return pl.pallas_call(
        functools.partial(pairs_kernel, nq, nk, plan, same),
        out_shape=jax.ShapeDtypeStruct((nq, 1, rows), jnp.float32),
        in_specs=[pl.BlockSpec(memory_space=pl.ANY)] * (nq + nk),
        out_specs=pl.BlockSpec(memory_space=pltpu.VMEM),
        scratch_shapes=[
            pltpu.VMEM((nq * rows, width), jnp.bfloat16),
            pltpu.VMEM((nk * rows, width), jnp.bfloat16),
            pltpu.VMEM((nq, TAIL, rows), jnp.bfloat16),
            pltpu.VMEM((nk, TAIL, rows), jnp.bfloat16),
            pltpu.VMEM((8, nq * rows), jnp.float32),
            pltpu.SemaphoreType.DMA((2 * (nq + nk),)),
        ],
        compiler_params=pltpu.CompilerParams(vmem_limit_bytes=VMEM_LIMIT),
        cost_estimate=pl.CostEstimate(
            flops=2 * products * width,
            bytes_accessed=(nq + nk) * rows * width * 2,
            transcendentals=products,
        ),
        name=name,
    )(*queries, *keys)


def finish_kernel(pos_ref, m0_ref, m1_ref, m2_ref, m3_ref, out_ref):
    rows = pos_ref.shape[1]
    share = rows // GROUPS
    lane = lax.broadcasted_iota(jnp.int32, (1, rows), 1)
    masses = m0_ref[...]
    for k, ref in enumerate((m1_ref, m2_ref, m3_ref), 1):
        masses = jnp.where(lane >= k * share, ref[...], masses)
    down, _ = iotas(rows, rows)
    picked = jnp.where(down.astype(jnp.float32) == pos_ref[...], as_column(masses), 0.0)
    out_ref[...] = jnp.log1p(jnp.sum(picked, axis=0, keepdims=True))


def finish(pos, masses):
    return pl.pallas_call(
        finish_kernel,
        out_shape=jax.ShapeDtypeStruct(pos.shape, jnp.float32),
        compiler_params=pltpu.CompilerParams(vmem_limit_bytes=VMEM_LIMIT),
        name="finish",
    )(pos, *masses)


def pairs_of(source_of):
    moves = []
    for here in np.ndindex(*SIZES):
        there = tuple(int(v) % n for v, n in zip(source_of(*here), SIZES))
        moves.append((int(np.ravel_multi_index(there, SIZES)), int(np.ravel_multi_index(here, SIZES))))
    return moves


def receive(array, source_of):
    return lax.ppermute(array, AXES, pairs_of(source_of))


def side(c):
    return -1 if c == 0 else 1


def swap(a):
    return receive(a, lambda x, y, z, c: (x, y, z, 1 - c))


def near_y(a):
    return receive(a, lambda x, y, z, c: (x, y + side(c), z, c))


def near_z(a):
    return receive(a, lambda x, y, z, c: (x, y, z + side(c), c))


def shards(embeddings, cluster_ids):
    rows = embeddings.shape[0]
    x_index = lax.axis_index("x").astype(jnp.int32).reshape(1)
    *chunks, pos = prepare(x_index, embeddings, cluster_ids.reshape(1, rows))
    for k in range(1, GROUPS):
        chunks[k] = receive(chunks[k], lambda x, y, z, c, k=k: (x - k, y, z, c))
    own = join(chunks)

    az, ay = near_z(own), near_y(own)
    other = swap(own)
    bz, by = near_z(other), near_y(other)
    fz, fy = near_z(az), near_y(ay)
    ay2, by2, fy2 = swap(ay), swap(by), swap(fy)

    s0 = pair_sums([own], [own, other], ((0, 0, 1), (1, 0, 1)), same=0, name="pairs_own")
    s1 = pair_sums(
        [own, az], [ay, ay2, own, other], ((0, 0, 2), (1, 0, 2), (2, 1, 1), (3, 1, 1)), name="pairs_a"
    )
    s2 = pair_sums(
        [own, az, bz],
        [by, by2, own, other, ay, ay2],
        ((0, 0, 3), (1, 0, 3), (2, 2, 1), (3, 2, 1), (4, 2, 1), (5, 2, 1)),
        name="pairs_b",
    )
    s3 = pair_sums(
        [own, az, bz, fz],
        [fy, fy2, own, other, ay, ay2, by, by2],
        ((2, 3, 1), (3, 3, 1), (4, 3, 1), (5, 3, 1), (6, 3, 1), (7, 3, 1), (0, 0, 4), (1, 0, 4)),
        name="pairs_f",
    )
    mass = s0[0] + s1[0] + s2[0] + s3[0]
    mass_a = s1[1] + s2[1] + s3[1]
    mass_b = s2[2] + s3[2]
    mass_f = s3[3]
    mass = (
        mass
        + receive(mass_a, lambda x, y, z, c: (x, y, z - side(c), c))
        + receive(mass_b, lambda x, y, z, c: (x, y, z + side(c), 1 - c))
        + receive(mass_f, lambda x, y, z, c: (x, y, z + 2, c))
    )
    masses = [mass] + [
        receive(mass, lambda x, y, z, c, k=k: (x + k, y, z, c)) for k in range(1, GROUPS)
    ]
    return finish(pos, masses).reshape(rows)


def solution(mesh):
    devices = Mesh(np.asarray(mesh.devices).reshape(SIZES), AXES)
    return jax.shard_map(
        shards, mesh=devices, in_specs=(P(AXES, None), P(AXES)), out_specs=P(AXES), check_vma=False
    )
```

time: 147 us -> 73 us (0.50)
  blocking collectives: 49.4 us -> 0 us
  starting transfers between devices: 3.22 us -> 25.8 us
  Pallas kernels: 0 us -> 18.5 us
  waiting for transfers between devices: 43.7 us -> 26 us
  matrix products: 13.9 us -> 0 us
  between operations: 13.5 us -> 0.14 us
  local copies, waits for them, and re-layouts: 14.2 us -> 1.75 us
  other arithmetic: 8.3 us -> 0.62 us
    all_gather x1 -> x0, waiting for transfers between devices: 38.6 us -> none  [shards(): lax.all_gather(queries, 'bulk', axis=0, tiled=True)]
    ppermute x0 -> x19, waiting for transfers between devices: none -> 26 us  [receive(): return lax.ppermute(array, AXES, pairs_of(source_of))]
    ppermute x0 -> x19, starting transfers between devices: none -> 25.8 us  [receive(): return lax.ppermute(array, AXES, pairs_of(source_of))]
    all_gather x1 -> x0, blocking collectives: 25.6 us -> none  [shards(): lax.all_gather(query_ids, 'bulk', axis=0, tiled=True)]
    all_to_all x2 -> x0, blocking collectives: 23.7 us -> none  [the longest x1 14.5 us: shards(): lax.all_to_all(outgoing[0], 'grp', split_axis=0, concat_axis=0, tiled=True)]
    pallas_call x0 -> x7, Pallas kernels: none -> 18.5 us  [the longest x4 17.6 us: pair_sums(): pl.pallas_call(functools.partial(pairs_kernel, nq, nk, plan, same), out_s...]
    dot_general x1 -> x0, matrix products: 13.9 us -> none  [tile_terms(): lax.dot_general(queries, keys, (((1,), (1,)), ((), ())), preferred_elemen...]
    scatter x2 -> x0, local copies, waits for them, and re-layouts: 6.38 us -> none  [the longest x1 3.47 us: shards(): return jnp.zeros((rows,), jnp.float32).at[order].set(back)]
  transfers between devices with their start and end apart: 2 -> 19, of which waited for: 2 -> 9; matrix products, arithmetic and copies ran while one was open for 3% -> 0% of each run, Pallas kernels for 0% -> 14%
where the time goes in v1:
time: 73 us; the launch traced here: 72.8 us
  waiting for transfers between devices  26 us (36%)
  starting transfers between devices  25.8 us (35%)
  Pallas kernels  18.5 us (25%)
  local copies, waits for them, and re-layouts  1.75 us (2%)
    ppermute x19, waiting for transfers between devices, receive(): return lax.ppermute(array, AXES, pairs_of(source_of))  26 us
    ppermute x19, starting transfers between devices, receive(): return lax.ppermute(array, AXES, pairs_of(source_of))  25.8 us
    pallas_call x4, Pallas kernels, pair_sums(): pl.pallas_call(functools.partial(pairs_kernel, nq, nk, plan, same), out_s...  17.6 us
    unnamed x6, local copies, waits for them, and re-layouts  1.75 us
  transfers between devices with their start and end apart: 19, of which 9 were waited for; matrix products, arithmetic and copies ran while one was open for 0% of the time, Pallas kernels for 14%

profile of v1, /device:TPU:0, one launch (start us, length us, event | category | flops | bytes accessed | tf_op | source)
XLA Modules:
  0.0 72.8 jit_solution(1637914384455664588)
XLA Ops:
  0.7 1.1 %copy-done = bf16[384,768]{1,0:T(8,128)(2,1)S(1)} copy-done((bf16[384,768]{1,0:T(8,128)(2,1)S(1)}, bf16[384,768]{1,0:T(8,128)(2,1)}, u32[]{:S(2)}) %copy-start) | copy-done | bytes 589848
  2.5 1.6 %collective-permute-start = (bf16[112,768]{1,0:T(8,128)(2,1)S(1)}, bf16[112,768]{1,0:T(8,128)(2,1)S(1)}, u32[]{:S(2)}, u32[]{:S(2)}) collective-permute-start(bf16[112,768]{1,0:T(8,128)(2,1)S(1)} %get-tuple-element.12), channel_id=1, source_target_pairs={{96,0},{97,1},{98,2},{99,3},{100,4},{101,5},{102,6},{103,7},{104,8... | collective-permute-start | bytes 516104 | tf_op jit(solution)/shard_map/ppermute | solution.py:227
  4.1 2.7 %collective-permute-start.1 = (bf16[112,768]{1,0:T(8,128)(2,1)S(1)}, bf16[112,768]{1,0:T(8,128)(2,1)S(1)}, u32[]{:S(2)}, u32[]{:S(2)}) collective-permute-start(bf16[112,768]{1,0:T(8,128)(2,1)S(1)} %get-tuple-element.13), channel_id=1, source_target_pairs={{64,0},{65,1},{66,2},{67,3},{68,4},{69,5},{70,6},{71,7},{72,8},{73... | collective-permute-start | bytes 516104 | tf_op jit(solution)/shard_map/ppermute | solution.py:227
  6.9 1.4 %collective-permute-start.2 = (bf16[112,768]{1,0:T(8,128)(2,1)S(1)}, bf16[112,768]{1,0:T(8,128)(2,1)S(1)}, u32[]{:S(2)}, u32[]{:S(2)}) collective-permute-start(bf16[112,768]{1,0:T(8,128)(2,1)S(1)} %get-tuple-element.14), channel_id=1, source_target_pairs={{32,0},{33,1},{34,2},{35,3},{36,4},{37,5},{38,6},{39,7},{40,8},{41... | collective-permute-start | bytes 516104 | tf_op jit(solution)/shard_map/ppermute | solution.py:227
  8.3 1.5 %collective-permute-done.c1_ref = bf16[112,768]{1,0:T(8,128)(2,1)S(1)} collective-permute-done((bf16[112,768]{1,0:T(8,128)(2,1)S(1)}, bf16[112,768]{1,0:T(8,128)(2,1)S(1)}, u32[]{:S(2)}, u32[]{:S(2)}) %collective-permute-start) | collective-permute-done | bytes 172064 | tf_op jit(solution)/shard_map/ppermute | solution.py:227
  9.8 4.9 %collective-permute-done.1.c2_ref = bf16[112,768]{1,0:T(8,128)(2,1)S(1)} collective-permute-done((bf16[112,768]{1,0:T(8,128)(2,1)S(1)}, bf16[112,768]{1,0:T(8,128)(2,1)S(1)}, u32[]{:S(2)}, u32[]{:S(2)}) %collective-permute-start.1) | collective-permute-done | bytes 172064 | tf_op jit(solution)/shard_map/ppermute | solution.py:227
  14.8 1.6 %collective-permute-start.5 = (bf16[400,768]{1,0:T(8,128)(2,1)S(1)}, bf16[400,768]{1,0:T(8,128)(2,1)S(1)}, u32[]{:S(2)}, u32[]{:S(2)}) collective-permute-start(bf16[400,768]{1,0:T(8,128)(2,1)S(1)} %join.1.refs_0_.refs_1_.refs_4_.refs_5_.refs_6_), channel_id=1, source_target_pairs={{24,0},{9,1},{26,2},{11,3},{28,4},{13,5},{30,6},{15,7},{0,8},{17,9... | collective-permute-start | bytes 1843208 | tf_op jit(solution)/shard_map/ppermute | solution.py:227
  16.8 1.6 %collective-permute-start.8 = (bf16[400,768]{1,0:T(8,128)(2,1)S(1)}, bf16[400,768]{1,0:T(8,128)(2,1)S(1)}, u32[]{:S(2)}, u32[]{:S(2)}) collective-permute-start(bf16[400,768]{1,0:T(8,128)(2,1)S(1)} %collective-permute-done.3.refs_2_.refs_5_.refs_6_.refs_7_), channel_id=1, source_target_pairs={{24,0},{9,1},{26,2},{11,3},{28,4},{13,5},{30,6},{15,7},{0,8},{17,9... | collective-permute-start | bytes 1843208 | tf_op jit(solution)/shard_map/ppermute | solution.py:227
  18.4 1.9 %collective-permute-start.4 = (bf16[400,768]{1,0:T(8,128)(2,1)S(1)}, bf16[400,768]{1,0:T(8,128)(2,1)S(1)}, u32[]{:S(2)}, u32[]{:S(2)}) collective-permute-start(bf16[400,768]{1,0:T(8,128)(2,1)S(1)} %join.1.refs_0_.refs_1_.refs_4_.refs_5_.refs_6_), channel_id=1, source_target_pairs={{6,0},{3,1},{0,2},{5,3},{2,4},{7,5},{4,6},{1,7},{14,8},{11,9},{8,1... | collective-permute-start | bytes 1843208 | tf_op jit(solution)/shard_map/ppermute | solution.py:227
  20.3 5.9 %collective-permute-done.5.refs_2_.refs_7_.refs_8_ = bf16[400,768]{1,0:T(8,128)(2,1)S(1)} collective-permute-done((bf16[400,768]{1,0:T(8,128)(2,1)S(1)}, bf16[400,768]{1,0:T(8,128)(2,1)S(1)}, u32[]{:S(2)}, u32[]{:S(2)}) %collective-permute-start.5) | collective-permute-done | bytes 614432 | tf_op jit(solution)/shard_map/ppermute | solution.py:227
  26.6 1.9 %collective-permute-start.6 = (bf16[400,768]{1,0:T(8,128)(2,1)S(1)}, bf16[400,768]{1,0:T(8,128)(2,1)S(1)}, u32[]{:S(2)}, u32[]{:S(2)}) collective-permute-start(bf16[400,768]{1,0:T(8,128)(2,1)S(1)} %collective-permute-done.5.refs_2_.refs_7_.refs_8_), channel_id=1, source_target_pairs={{1,0},{0,1},{3,2},{2,3},{5,4},{4,5},{7,6},{6,7},{9,8},{8,9},{11,10... | collective-permute-start | bytes 1843208 | tf_op jit(solution)/shard_map/ppermute | solution.py:227
  28.5 1.6 %collective-permute-start.7 = (bf16[400,768]{1,0:T(8,128)(2,1)S(1)}, bf16[400,768]{1,0:T(8,128)(2,1)S(1)}, u32[]{:S(2)}, u32[]{:S(2)}) collective-permute-start(bf16[400,768]{1,0:T(8,128)(2,1)S(1)} %collective-permute-done.3.refs_2_.refs_5_.refs_6_.refs_7_), channel_id=1, source_target_pairs={{6,0},{3,1},{0,2},{5,3},{2,4},{7,5},{4,6},{1,7},{14,8},{11,9},{8,1... | collective-permute-start | bytes 1843208 | tf_op jit(solution)/shard_map/ppermute | solution.py:227
  30.2 2.7 %collective-permute-done.8.refs_3_.refs_10_ = bf16[400,768]{1,0:T(8,128)(2,1)S(1)} collective-permute-done((bf16[400,768]{1,0:T(8,128)(2,1)S(1)}, bf16[400,768]{1,0:T(8,128)(2,1)S(1)}, u32[]{:S(2)}, u32[]{:S(2)}) %collective-permute-start.8) | collective-permute-done | bytes 614432 | tf_op jit(solution)/shard_map/ppermute | solution.py:227
  32.8 1.9 %collective-permute-start.10 = (bf16[400,768]{1,0:T(8,128)(2,1)S(1)}, bf16[400,768]{1,0:T(8,128)(2,1)S(1)}, u32[]{:S(2)}, u32[]{:S(2)}) collective-permute-start(bf16[400,768]{1,0:T(8,128)(2,1)S(1)} %collective-permute-done.4.refs_1_), channel_id=1, source_target_pairs={{6,0},{3,1},{0,2},{5,3},{2,4},{7,5},{4,6},{1,7},{14,8},{11,9},{8,1... | collective-permute-start | bytes 1843208 | tf_op jit(solution)/shard_map/ppermute | solution.py:227
  34.7 4.7 %collective-permute-done.11.refs_4_ = bf16[400,768]{1,0:T(8,128)(2,1)S(1)} collective-permute-done((bf16[400,768]{1,0:T(8,128)(2,1)S(1)}, bf16[400,768]{1,0:T(8,128)(2,1)S(1)}, u32[]{:S(2)}, u32[]{:S(2)}) %collective-permute-start.11) | collective-permute-done | bytes 614432 | tf_op jit(solution)/shard_map/ppermute | solution.py:227
  39.4 3.6 %pairs_a.1 = f32[2,1,384]{2,1,0:T(1,128)S(1)} custom-call(bf16[400,768]{1,0:T(8,128)(2,1)S(1)} %join.1.refs_0_.refs_1_.refs_4_.refs_5_.refs_6_, bf16[400,768]{1,0:T(8,128)(2,1)S(1)} %collective-permute-done.4.refs_1_, bf16[400,768]{1,0:T(8,128)(2,1)S(1)} %collective-permute-done.5.refs_2_.refs_7_.refs_8_, ...), custom_call_target="tpu_custom_call" | custom-call | flops 1358954496 | bytes 3538944 | tf_op jit(solution)/shard_map/pairs_a/pallas_call | solution.py:174
  43.0 5.4 %pairs_b.1 = f32[3,1,384]{2,1,0:T(1,128)S(1)} custom-call(bf16[400,768]{1,0:T(8,128)(2,1)S(1)} %join.1.refs_0_.refs_1_.refs_4_.refs_5_.refs_6_, bf16[400,768]{1,0:T(8,128)(2,1)S(1)} %collective-permute-done.4.refs_1_, bf16[400,768]{1,0:T(8,128)(2,1)S(1)} %collective-permute-done.7.refs_2_, bf16[400,768]{1,0:T(8,128)(2,1)S(1)} %collective-permute-done.8.refs_3_.refs_10_, ...), custom_call_target="tpu_custom_call" | custom-call | flops 2264924160 | bytes 5308416 | tf_op jit(solution)/shard_map/pairs_b/pallas_call | solution.py:174
  48.5 7.1 %pairs_f.1 = f32[4,1,384]{2,1,0:T(1,128)S(1)} custom-call(bf16[400,768]{1,0:T(8,128)(2,1)S(1)} %join.1.refs_0_.refs_1_.refs_4_.refs_5_.refs_6_, bf16[400,768]{1,0:T(8,128)(2,1)S(1)} %collective-permute-done.4.refs_1_, bf16[400,768]{1,0:T(8,128)(2,1)S(1)} %collective-permute-done.7.refs_2_, bf16[400,768]{1,0:T(8,128)(2,1)S(1)} %collective-permute-done.10.refs_3_, ...), custom_call_target="tpu_custom_call" | custom-call | flops 3170893824 | bytes 7077888 | tf_op jit(solution)/shard_map/pairs_f/pallas_call | solution.py:174
  55.6 4.0 %collective-permute-start.15 = (f32[1,384]{1,0:T(1,128)S(1)}, f32[1,384]{1,0:T(1,128)S(1)}, u32[]{:S(2)}, u32[]{:S(2)}) collective-permute-start(f32[1,384]{1,0:T(1,128)S(1)} %get-tuple-element.17), channel_id=1, source_target_pairs={{4,0},{5,1},{6,2},{7,3},{0,4},{1,5},{2,6},{3,7},{12,8},{13,9},{14,... | collective-permute-start | bytes 4616 | tf_op jit(solution)/shard_map/ppermute | solution.py:227
  60.3 1.5 %pairs_own.1 = f32[1,1,384]{2,1,0:T(1,128)S(1)} custom-call(bf16[400,768]{1,0:T(8,128)(2,1)S(1)} %join.1.refs_0_.refs_1_.refs_4_.refs_5_.refs_6_, bf16[400,768]{1,0:T(8,128)(2,1)S(1)} %join.1.refs_0_.refs_1_.refs_4_.refs_5_.refs_6_, bf16[400,768]{1,0:T(8,128)(2,1)S(1)} %collective-permute-done.3.refs_2_.refs_5_.refs_6_.refs_7_), custom_call_target="tpu_custom_call" | custom-call | flops 452984832 | bytes 1769472 | tf_op jit(solution)/shard_map/pairs_own/pallas_call | solution.py:174
  61.8 1.9 %collective-permute-done.14 = f32[1,384]{1,0:T(1,128)S(1)} collective-permute-done((f32[1,384]{1,0:T(1,128)S(1)}, f32[1,384]{1,0:T(1,128)S(1)}, u32[]{:S(2)}, u32[]{:S(2)}) %collective-permute-start.14) | collective-permute-done | bytes 1568 | tf_op jit(solution)/shard_map/ppermute | solution.py:227
  63.8 2.3 %collective-permute-start.16 = (f32[1,384]{1,0:T(1,128)S(1)}, f32[1,384]{1,0:T(1,128)S(1)}, u32[]{:S(2)}, u32[]{:S(2)}) collective-permute-start(f32[1,384]{1,0:T(1,128)S(1)} %fusion.5.m0_ref), channel_id=1, source_target_pairs={{32,0},{33,1},{34,2},{35,3},{36,4},{37,5},{38,6},{39,7},{40,8},{41... | collective-permute-start | bytes 4616 | tf_op jit(solution)/shard_map/ppermute | solution.py:227
  66.1 1.1 %collective-permute-start.17 = (f32[1,384]{1,0:T(1,128)S(1)}, f32[1,384]{1,0:T(1,128)S(1)}, u32[]{:S(2)}, u32[]{:S(2)}) collective-permute-start(f32[1,384]{1,0:T(1,128)S(1)} %fusion.5.m0_ref), channel_id=1, source_target_pairs={{64,0},{65,1},{66,2},{67,3},{68,4},{69,5},{70,6},{71,7},{72,8},{73... | collective-permute-start | bytes 4616 | tf_op jit(solution)/shard_map/ppermute | solution.py:227
  67.9 3.3 %collective-permute-done.17.m2_ref = f32[1,384]{1,0:T(1,128)S(1)} collective-permute-done((f32[1,384]{1,0:T(1,128)S(1)}, f32[1,384]{1,0:T(1,128)S(1)}, u32[]{:S(2)}, u32[]{:S(2)}) %collective-permute-start.17) | collective-permute-done | bytes 1568 | tf_op jit(solution)/shard_map/ppermute | solution.py:227
  (31 shorter events, 5.4 us)
Async XLA Ops:
  0.0 0.7 copy-start.2
  0.7 1.1 %copy-start = (bf16[384,768]{1,0:T(8,128)(2,1)S(1)}, bf16[384,768]{1,0:T(8,128)(2,1)}, u32[]{:S(2)}) copy-start(bf16[384,768]{1,0:T(8,128)(2,1)} %emb_ref.1) | copy-start | bytes 1769476
  2.5 7.3 %collective-permute-start = (bf16[112,768]{1,0:T(8,128)(2,1)S(1)}, bf16[112,768]{1,0:T(8,128)(2,1)S(1)}, u32[]{:S(2)}, u32[]{:S(2)}) collective-permute-start(bf16[112,768]{1,0:T(8,128)(2,1)S(1)} %get-tuple-element.12), channel_id=1, source_target_pairs={{96,0},{97,1},{98,2},{99,3},{100,4},{101,5},{102,6},{103,7},{104,8... | collective-permute-start | bytes 516104 | tf_op jit(solution)/shard_map/ppermute | solution.py:227
  4.1 10.5 %collective-permute-start.1 = (bf16[112,768]{1,0:T(8,128)(2,1)S(1)}, bf16[112,768]{1,0:T(8,128)(2,1)S(1)}, u32[]{:S(2)}, u32[]{:S(2)}) collective-permute-start(bf16[112,768]{1,0:T(8,128)(2,1)S(1)} %get-tuple-element.13), channel_id=1, source_target_pairs={{64,0},{65,1},{66,2},{67,3},{68,4},{69,5},{70,6},{71,7},{72,8},{73... | collective-permute-start | bytes 516104 | tf_op jit(solution)/shard_map/ppermute | solution.py:227
  6.9 7.8 %collective-permute-start.2 = (bf16[112,768]{1,0:T(8,128)(2,1)S(1)}, bf16[112,768]{1,0:T(8,128)(2,1)S(1)}, u32[]{:S(2)}, u32[]{:S(2)}) collective-permute-start(bf16[112,768]{1,0:T(8,128)(2,1)S(1)} %get-tuple-element.14), channel_id=1, source_target_pairs={{32,0},{33,1},{34,2},{35,3},{36,4},{37,5},{38,6},{39,7},{40,8},{41... | collective-permute-start | bytes 516104 | tf_op jit(solution)/shard_map/ppermute | solution.py:227
  14.7 2.1 %collective-permute-start.3 = (bf16[400,768]{1,0:T(8,128)(2,1)S(1)}, bf16[400,768]{1,0:T(8,128)(2,1)S(1)}, u32[]{:S(2)}, u32[]{:S(2)}) collective-permute-start(bf16[400,768]{1,0:T(8,128)(2,1)S(1)} %join.1.refs_0_.refs_1_.refs_4_.refs_5_.refs_6_), channel_id=1, source_target_pairs={{1,0},{0,1},{3,2},{2,3},{5,4},{4,5},{7,6},{6,7},{9,8},{8,9},{11,10... | collective-permute-start | bytes 1843208 | tf_op jit(solution)/shard_map/ppermute | solution.py:227
  14.8 11.4 %collective-permute-start.5 = (bf16[400,768]{1,0:T(8,128)(2,1)S(1)}, bf16[400,768]{1,0:T(8,128)(2,1)S(1)}, u32[]{:S(2)}, u32[]{:S(2)}) collective-permute-start(bf16[400,768]{1,0:T(8,128)(2,1)S(1)} %join.1.refs_0_.refs_1_.refs_4_.refs_5_.refs_6_), channel_id=1, source_target_pairs={{24,0},{9,1},{26,2},{11,3},{28,4},{13,5},{30,6},{15,7},{0,8},{17,9... | collective-permute-start | bytes 1843208 | tf_op jit(solution)/shard_map/ppermute | solution.py:227
  16.8 16.0 %collective-permute-start.8 = (bf16[400,768]{1,0:T(8,128)(2,1)S(1)}, bf16[400,768]{1,0:T(8,128)(2,1)S(1)}, u32[]{:S(2)}, u32[]{:S(2)}) collective-permute-start(bf16[400,768]{1,0:T(8,128)(2,1)S(1)} %collective-permute-done.3.refs_2_.refs_5_.refs_6_.refs_7_), channel_id=1, source_target_pairs={{24,0},{9,1},{26,2},{11,3},{28,4},{13,5},{30,6},{15,7},{0,8},{17,9... | collective-permute-start | bytes 1843208 | tf_op jit(solution)/shard_map/ppermute | solution.py:227
  18.4 14.4 %collective-permute-start.4 = (bf16[400,768]{1,0:T(8,128)(2,1)S(1)}, bf16[400,768]{1,0:T(8,128)(2,1)S(1)}, u32[]{:S(2)}, u32[]{:S(2)}) collective-permute-start(bf16[400,768]{1,0:T(8,128)(2,1)S(1)} %join.1.refs_0_.refs_1_.refs_4_.refs_5_.refs_6_), channel_id=1, source_target_pairs={{6,0},{3,1},{0,2},{5,3},{2,4},{7,5},{4,6},{1,7},{14,8},{11,9},{8,1... | collective-permute-start | bytes 1843208 | tf_op jit(solution)/shard_map/ppermute | solution.py:227
  26.2 13.2 %collective-permute-start.11 = (bf16[400,768]{1,0:T(8,128)(2,1)S(1)}, bf16[400,768]{1,0:T(8,128)(2,1)S(1)}, u32[]{:S(2)}, u32[]{:S(2)}) collective-permute-start(bf16[400,768]{1,0:T(8,128)(2,1)S(1)} %collective-permute-done.5.refs_2_.refs_7_.refs_8_), channel_id=1, source_target_pairs={{24,0},{9,1},{26,2},{11,3},{28,4},{13,5},{30,6},{15,7},{0,8},{17,9... | collective-permute-start | bytes 1843208 | tf_op jit(solution)/shard_map/ppermute | solution.py:227
  26.6 12.8 %collective-permute-start.6 = (bf16[400,768]{1,0:T(8,128)(2,1)S(1)}, bf16[400,768]{1,0:T(8,128)(2,1)S(1)}, u32[]{:S(2)}, u32[]{:S(2)}) collective-permute-start(bf16[400,768]{1,0:T(8,128)(2,1)S(1)} %collective-permute-done.5.refs_2_.refs_7_.refs_8_), channel_id=1, source_target_pairs={{1,0},{0,1},{3,2},{2,3},{5,4},{4,5},{7,6},{6,7},{9,8},{8,9},{11,10... | collective-permute-start | bytes 1843208 | tf_op jit(solution)/shard_map/ppermute | solution.py:227
  28.5 14.4 %collective-permute-start.7 = (bf16[400,768]{1,0:T(8,128)(2,1)S(1)}, bf16[400,768]{1,0:T(8,128)(2,1)S(1)}, u32[]{:S(2)}, u32[]{:S(2)}) collective-permute-start(bf16[400,768]{1,0:T(8,128)(2,1)S(1)} %collective-permute-done.3.refs_2_.refs_5_.refs_6_.refs_7_), channel_id=1, source_target_pairs={{6,0},{3,1},{0,2},{5,3},{2,4},{7,5},{4,6},{1,7},{14,8},{11,9},{8,1... | collective-permute-start | bytes 1843208 | tf_op jit(solution)/shard_map/ppermute | solution.py:227
  32.8 10.2 %collective-permute-start.9 = (bf16[400,768]{1,0:T(8,128)(2,1)S(1)}, bf16[400,768]{1,0:T(8,128)(2,1)S(1)}, u32[]{:S(2)}, u32[]{:S(2)}) collective-permute-start(bf16[400,768]{1,0:T(8,128)(2,1)S(1)} %collective-permute-done.8.refs_3_.refs_10_), channel_id=1, source_target_pairs={{1,0},{0,1},{3,2},{2,3},{5,4},{4,5},{7,6},{6,7},{9,8},{8,9},{11,10... | collective-permute-start | bytes 1843208 | tf_op jit(solution)/shard_map/ppermute | solution.py:227
  32.8 15.6 %collective-permute-start.10 = (bf16[400,768]{1,0:T(8,128)(2,1)S(1)}, bf16[400,768]{1,0:T(8,128)(2,1)S(1)}, u32[]{:S(2)}, u32[]{:S(2)}) collective-permute-start(bf16[400,768]{1,0:T(8,128)(2,1)S(1)} %collective-permute-done.4.refs_1_), channel_id=1, source_target_pairs={{6,0},{3,1},{0,2},{5,3},{2,4},{7,5},{4,6},{1,7},{14,8},{11,9},{8,1... | collective-permute-start | bytes 1843208 | tf_op jit(solution)/shard_map/ppermute | solution.py:227
  39.4 9.1 %collective-permute-start.12 = (bf16[400,768]{1,0:T(8,128)(2,1)S(1)}, bf16[400,768]{1,0:T(8,128)(2,1)S(1)}, u32[]{:S(2)}, u32[]{:S(2)}) collective-permute-start(bf16[400,768]{1,0:T(8,128)(2,1)S(1)} %collective-permute-done.11.refs_4_), channel_id=1, source_target_pairs={{1,0},{0,1},{3,2},{2,3},{5,4},{4,5},{7,6},{6,7},{9,8},{8,9},{11,10... | collective-permute-start | bytes 1843208 | tf_op jit(solution)/shard_map/ppermute | solution.py:227
  43.0 5.5 %copy-start.1 = (bf16[400,768]{1,0:T(8,128)(2,1)}, bf16[400,768]{1,0:T(8,128)(2,1)S(1)}, u32[]{:S(2)}) copy-start(bf16[400,768]{1,0:T(8,128)(2,1)S(1)} %collective-permute-done.9.refs_4_.refs_11_) | copy-start | bytes 1843204
  55.6 6.2 %collective-permute-start.15 = (f32[1,384]{1,0:T(1,128)S(1)}, f32[1,384]{1,0:T(1,128)S(1)}, u32[]{:S(2)}, u32[]{:S(2)}) collective-permute-start(f32[1,384]{1,0:T(1,128)S(1)} %get-tuple-element.17), channel_id=1, source_target_pairs={{4,0},{5,1},{6,2},{7,3},{0,4},{1,5},{2,6},{3,7},{12,8},{13,9},{14,... | collective-permute-start | bytes 4616 | tf_op jit(solution)/shard_map/ppermute | solution.py:227
  59.5 4.2 %collective-permute-start.14 = (f32[1,384]{1,0:T(1,128)S(1)}, f32[1,384]{1,0:T(1,128)S(1)}, u32[]{:S(2)}, u32[]{:S(2)}) collective-permute-start(f32[1,384]{1,0:T(1,128)S(1)} %get-tuple-element.16), channel_id=1, source_target_pairs={{7,0},{2,1},{1,2},{4,3},{3,4},{6,5},{5,6},{0,7},{15,8},{10,9},{9,1... | collective-permute-start | bytes 4616 | tf_op jit(solution)/shard_map/ppermute | solution.py:227
  60.1 3.7 %collective-permute-start.13 = (f32[1,384]{1,0:T(1,128)S(1)}, f32[1,384]{1,0:T(1,128)S(1)}, u32[]{:S(2)}, u32[]{:S(2)}) collective-permute-start(f32[1,384]{1,0:T(1,128)S(1)} %get-tuple-element.15), channel_id=1, source_target_pairs={{2,0},{7,1},{4,2},{1,3},{6,4},{3,5},{0,6},{5,7},{10,8},{15,9},{12,... | collective-permute-start | bytes 4616 | tf_op jit(solution)/shard_map/ppermute | solution.py:227
  63.8 4.2 %collective-permute-start.16 = (f32[1,384]{1,0:T(1,128)S(1)}, f32[1,384]{1,0:T(1,128)S(1)}, u32[]{:S(2)}, u32[]{:S(2)}) collective-permute-start(f32[1,384]{1,0:T(1,128)S(1)} %fusion.5.m0_ref), channel_id=1, source_target_pairs={{32,0},{33,1},{34,2},{35,3},{36,4},{37,5},{38,6},{39,7},{40,8},{41... | collective-permute-start | bytes 4616 | tf_op jit(solution)/shard_map/ppermute | solution.py:227
  66.1 5.1 %collective-permute-start.17 = (f32[1,384]{1,0:T(1,128)S(1)}, f32[1,384]{1,0:T(1,128)S(1)}, u32[]{:S(2)}, u32[]{:S(2)}) collective-permute-start(f32[1,384]{1,0:T(1,128)S(1)} %fusion.5.m0_ref), channel_id=1, source_target_pairs={{64,0},{65,1},{66,2},{67,3},{68,4},{69,5},{70,6},{71,7},{72,8},{73... | collective-permute-start | bytes 4616 | tf_op jit(solution)/shard_map/ppermute | solution.py:227
  67.2 4.8 %collective-permute-start.18 = (f32[1,384]{1,0:T(1,128)S(1)}, f32[1,384]{1,0:T(1,128)S(1)}, u32[]{:S(2)}, u32[]{:S(2)}) collective-permute-start(f32[1,384]{1,0:T(1,128)S(1)} %fusion.5.m0_ref), channel_id=1, source_target_pairs={{96,0},{97,1},{98,2},{99,3},{100,4},{101,5},{102,6},{103,7},{104,8... | collective-permute-start | bytes 4616 | tf_op jit(solution)/shard_map/ppermute | solution.py:227

commit v2 on v1

v2 whole, which is shorter than its diff:
```python
import functools

import jax
import jax.numpy as jnp
import numpy as np
from jax import lax
from jax.experimental import pallas as pl
from jax.experimental.pallas import tpu as pltpu
from jax.sharding import Mesh
from jax.sharding import PartitionSpec as P

CL_GRP = 64
GROUPS = 4
TEMP = 0.05
RATE = 1.4426950408889634 / TEMP
STEPS = (0, 1, 3, 2)
AXES = ("x", "y", "z", "c")
SIZES = (4, 4, 4, 2)
TAIL = 16
VMEM_LIMIT = 32 * 1024 * 1024


def iotas(rows, cols):
    return (
        lax.broadcasted_iota(jnp.int32, (rows, cols), 0),
        lax.broadcasted_iota(jnp.int32, (rows, cols), 1),
    )


def as_column(row):
    n = row.shape[1]
    down, across = iotas(n, n)
    return jnp.sum(jnp.where(down == across, row, 0.0), axis=1, keepdims=True)


def prepare_kernel(x_ref, emb_ref, ids_ref, c0_ref, c1_ref, c3_ref, c2_ref, pos_ref):
    rows = emb_ref.shape[0]
    share = rows // GROUPS
    values = emb_ref[...].astype(jnp.float32)
    scale = lax.rsqrt(jnp.sum(values * values, axis=1, keepdims=True) + 1e-06)
    units = (values * scale).astype(jnp.bfloat16)
    ids = ids_ref[...]
    down, across = iotas(rows, rows)
    steps = (lax.shift_right_logical(ids, 6) - x_ref[0]) & (GROUPS - 1)
    slot = steps ^ lax.shift_right_logical(steps, 1)
    key = (slot * rows + across[:1]).astype(jnp.float32)
    pos = jnp.sum(jnp.where(as_column(key) < key, 1.0, 0.0), axis=0, keepdims=True)
    pos_ref[...] = pos
    place = jnp.where(down.astype(jnp.float32) == pos, 1.0, 0.0).astype(jnp.bfloat16)
    placed = jnp.dot(place, units, preferred_element_type=jnp.float32).astype(jnp.bfloat16)
    wide = jnp.broadcast_to(ids.astype(jnp.float32), (TAIL, rows)).astype(jnp.bfloat16)
    placed_ids = lax.dot_general(
        wide, place, (((1,), (1,)), ((), ())), preferred_element_type=jnp.float32
    )
    chunk_of = lax.broadcasted_iota(jnp.int32, (TAIL, rows), 1)
    for k, out in enumerate((c0_ref, c1_ref, c3_ref, c2_ref)):
        out[:share, :] = placed[k * share : (k + 1) * share]
        here = (chunk_of >= k * share) & (chunk_of < (k + 1) * share)
        out[share:, :rows] = jnp.where(here, placed_ids, 0.0).astype(jnp.bfloat16)
        out[share:, rows:] = jnp.zeros((TAIL, out.shape[1] - rows), jnp.bfloat16)


def prepare(x_index, embeddings, ids):
    rows, width = embeddings.shape
    share = rows // GROUPS
    chunk = jax.ShapeDtypeStruct((share + TAIL, width), jnp.bfloat16)
    return pl.pallas_call(
        prepare_kernel,
        out_shape=[chunk] * GROUPS + [jax.ShapeDtypeStruct((1, rows), jnp.float32)],
        in_specs=[
            pl.BlockSpec(memory_space=pltpu.SMEM),
            pl.BlockSpec(memory_space=pltpu.VMEM),
            pl.BlockSpec(memory_space=pltpu.VMEM),
        ],
        compiler_params=pltpu.CompilerParams(vmem_limit_bytes=VMEM_LIMIT),
        name="prepare",
    )(x_index, embeddings, ids)


def join_kernel(c0_ref, c1_ref, c2_ref, c3_ref, out_ref):
    chunks = (c0_ref, c1_ref, c2_ref, c3_ref)
    share = c0_ref.shape[0] - TAIL
    tail = 0.0
    for k, chunk in enumerate(chunks):
        out_ref[k * share : (k + 1) * share, :] = chunk[:share, :]
        tail += chunk[share:, :].astype(jnp.float32)
    out_ref[GROUPS * share :, :] = tail.astype(jnp.bfloat16)


def join(chunks):
    share = chunks[0].shape[0] - TAIL
    return pl.pallas_call(
        join_kernel,
        out_shape=jax.ShapeDtypeStruct((GROUPS * share + TAIL, chunks[0].shape[1]), jnp.bfloat16),
        compiler_params=pltpu.CompilerParams(vmem_limit_bytes=VMEM_LIMIT),
        name="join",
    )(*chunks)


def pairs_kernel(nq, nk, plan, *refs):
    queries, keys = refs[:nq], refs[nq : nq + nk]
    out_ref, down_acc, across_acc = refs[nq + nk :]
    rows = out_ref.shape[2]
    down_acc[...] = jnp.zeros_like(down_acc)
    across_acc[...] = jnp.zeros_like(across_acc)

    def id_rows(blocks):
        return [block[rows:, :rows][:1].astype(jnp.float32) for block in blocks]

    def id_column(block):
        return jnp.transpose(jnp.broadcast_to(id_rows([block])[0], (128, rows)))

    def similar(tall, wide):
        parts = [block[:rows, :] for block in wide]
        return lax.dot_general(
            tall[:rows, :],
            jnp.concatenate(parts, axis=0) if len(parts) > 1 else parts[0],
            (((1,), (1,)), ((), ())),
            preferred_element_type=jnp.float32,
        )

    def term(similarity, keep):
        return jnp.where(keep, jnp.exp2((similarity - 1.0) * RATE), 0.0)

    for qs, ks, *same in plan:
        if len(ks) == 1:
            similarity = similar(keys[ks[0]], [queries[q] for q in qs])
            key_ids = id_column(keys[ks[0]])
            for i, (q, query_ids) in enumerate(zip(qs, id_rows([queries[q] for q in qs]))):
                for lane in range(0, rows, 128):
                    tile = similarity[:, i * rows + lane : i * rows + lane + 128]
                    terms = term(tile, key_ids == query_ids[:, lane : lane + 128])
                    down_acc[:, q * rows + lane : q * rows + lane + 128] += jnp.sum(
                        terms.reshape(rows // 8, 8, 128), axis=0
                    )
        else:
            (q,) = qs
            similarity = similar(queries[q], [keys[k] for k in ks])
            query_ids = id_column(queries[q])
            total = across_acc[q]
            for i, key_ids in enumerate(id_rows([keys[k] for k in ks])):
                for lane in range(0, rows, 128):
                    tile = similarity[:, i * rows + lane : i * rows + lane + 128]
                    keep = query_ids == key_ids[:, lane : lane + 128]
                    if same and i == 0:
                        down, across = iotas(rows, 128)
                        keep = keep & (down != across + lane)
                    total += term(tile, keep)
            across_acc[q] = total
    across_used = {qs[0] for qs, ks, *_ in plan if len(ks) > 1}
    for q in range(nq):
        total = jnp.sum(down_acc[:, q * rows : (q + 1) * rows], axis=0, keepdims=True)
        if q in across_used:
            total += jnp.sum(jnp.transpose(across_acc[q]), axis=0, keepdims=True)
        out_ref[q] = total


def pair_sums(queries, keys, plan, name):
    rows, width = queries[0].shape[0] - TAIL, queries[0].shape[1]
    nq, nk = len(queries), len(keys)
    products = sum(len(qs) * len(ks) for qs, ks, *_ in plan) * rows * rows
    return pl.pallas_call(
        functools.partial(pairs_kernel, nq, nk, plan),
        out_shape=jax.ShapeDtypeStruct((nq, 1, rows), jnp.float32),
        in_specs=[pl.BlockSpec(memory_space=pltpu.VMEM)] * (nq + nk),
        out_specs=pl.BlockSpec(memory_space=pltpu.VMEM),
        scratch_shapes=[
            pltpu.VMEM((8, nq * rows), jnp.float32),
            pltpu.VMEM((nq, rows, 128), jnp.float32),
        ],
        compiler_params=pltpu.CompilerParams(vmem_limit_bytes=VMEM_LIMIT),
        cost_estimate=pl.CostEstimate(
            flops=2 * products * width,
            bytes_accessed=(nq + nk) * rows * width * 2,
            transcendentals=products,
        ),
        name=name,
    )(*queries, *keys)


def finish_kernel(pos_ref, m0_ref, m1_ref, m2_ref, m3_ref, out_ref):
    rows = pos_ref.shape[1]
    share = rows // GROUPS
    lane = lax.broadcasted_iota(jnp.int32, (1, rows), 1)
    masses = m0_ref[...]
    for k, ref in enumerate((m1_ref, m2_ref, m3_ref), 1):
        masses = jnp.where(lane >= k * share, ref[...], masses)
    down, _ = iotas(rows, rows)
    picked = jnp.where(down.astype(jnp.float32) == pos_ref[...], as_column(masses), 0.0)
    out_ref[...] = jnp.log1p(jnp.sum(picked, axis=0))


def finish(pos, masses):
    return pl.pallas_call(
        finish_kernel,
        out_shape=jax.ShapeDtypeStruct((pos.shape[1],), jnp.float32),
        compiler_params=pltpu.CompilerParams(vmem_limit_bytes=VMEM_LIMIT),
        name="finish",
    )(pos, *masses)


def pairs_of(source_of):
    moves = []
    for here in np.ndindex(*SIZES):
        there = tuple(int(v) % n for v, n in zip(source_of(*here), SIZES))
        moves.append((int(np.ravel_multi_index(there, SIZES)), int(np.ravel_multi_index(here, SIZES))))
    return moves


def receive(array, source_of):
    return lax.ppermute(array, AXES, pairs_of(source_of))


def side(c):
    return -1 if c == 0 else 1


def swap(a):
    return receive(a, lambda x, y, z, c: (x, y, z, 1 - c))


def near_y(a):
    return receive(a, lambda x, y, z, c: (x, y + side(c), z, c))


def near_z(a):
    return receive(a, lambda x, y, z, c: (x, y, z + side(c), c))


def shards(embeddings, cluster_ids):
    rows = embeddings.shape[0]
    x_index = lax.axis_index("x").astype(jnp.int32).reshape(1)
    *chunks, pos = prepare(x_index, embeddings, cluster_ids.reshape(1, rows))
    for k, step in enumerate(STEPS):
        if step:
            chunks[k] = receive(chunks[k], lambda x, y, z, c, step=step: (x - step, y, z, c))
    own = join(chunks)

    ay, az = lax.optimization_barrier((near_y(own), near_z(own)))
    other = swap(own)
    fz, fy = near_z(az), near_y(ay)
    bz, by = near_z(other), near_y(other)
    by, bz = lax.optimization_barrier((by, bz))
    ay2, by2 = swap(ay), swap(by)
    s1 = pair_sums(
        [az, bz, own],
        [own, other, ay, ay2, by],
        (
            ((0, 1), (0,)),
            ((0, 1), (1,)),
            ((0, 1), (2,)),
            ((0, 1), (3,)),
            ((0, 1), (4,)),
            ((2,), (0, 1), True),
            ((2,), (2, 3)),
        ),
        name="pairs_a",
    )
    fy, fz, s1 = lax.optimization_barrier((fy, fz, s1))
    fy2 = swap(fy)
    s2 = pair_sums(
        [az, bz, fz],
        [by2, own, other, ay, ay2, by],
        (((0, 1), (0,)), ((2,), (1, 2)), ((2,), (3, 4)), ((2,), (5, 0))),
        name="pairs_b",
    )
    s3 = pair_sums(
        [az, bz, fz], [fy, fy2], (((0, 1), (0,)), ((0, 1), (1,)), ((2,), (0, 1))), name="pairs_f"
    )
    s0 = pair_sums([own], [by, by2, fy, fy2], (((0,), (0, 1)), ((0,), (2, 3))), name="pairs_own")
    mass_a = s1[0] + s2[0] + s3[0]
    mass_b = s1[1] + s2[1] + s3[1]
    mass_f = s2[2] + s3[2]
    mass = (
        s0[0]
        + s1[2]
        + receive(mass_f, lambda x, y, z, c: (x, y, z + 2, c))
        + receive(mass_a, lambda x, y, z, c: (x, y, z - side(c), c))
        + receive(mass_b, lambda x, y, z, c: (x, y, z + side(c), 1 - c))
    )
    masses = [
        receive(mass, lambda x, y, z, c, step=step: (x + step, y, z, c)) if step else mass for step in STEPS
    ]
    return finish(pos, masses)


def solution(mesh):
    devices = Mesh(np.asarray(mesh.devices).reshape(SIZES), AXES)
    return jax.shard_map(
        shards, mesh=devices, in_specs=(P(AXES, None), P(AXES)), out_specs=P(AXES), check_vma=False
    )
```

time: 73 us -> 62.5 us (0.86)
  Pallas kernels: 18.5 us -> 10.4 us
  starting transfers between devices: 25.8 us -> 24.4 us
    pallas_call x5, Pallas kernels: 17.7 us -> 9.59 us  [the longest x4 8.88 us: pair_sums(): pl.pallas_call(functools.partial(pairs_kernel, nq, nk, plan), out_shape=j...]
    ppermute x19, starting transfers between devices: 25.8 us -> 24.4 us  [receive(): return lax.ppermute(array, AXES, pairs_of(source_of))]
    unnamed x6 -> x4, local copies, waits for them, and re-layouts: 1.75 us -> 1.74 us
  transfers between devices with their start and end apart: 19 -> 19, of which waited for: 9 -> 12; matrix products, arithmetic and copies ran while one was open for 0% -> 0% of each run, Pallas kernels for 14% -> 12%
where the time goes in v2:
time: 62.5 us; the launch traced here: 62 us
  waiting for transfers between devices  25.3 us (40%)
  starting transfers between devices  24.4 us (39%)
  Pallas kernels  10.4 us (17%)
  local copies, waits for them, and re-layouts  1.75 us (3%)
    ppermute x19, waiting for transfers between devices, receive(): return lax.ppermute(array, AXES, pairs_of(source_of))  25.3 us
    ppermute x19, starting transfers between devices, receive(): return lax.ppermute(array, AXES, pairs_of(source_of))  24.4 us
    pallas_call x4, Pallas kernels, pair_sums(): pl.pallas_call(functools.partial(pairs_kernel, nq, nk, plan), out_shape=j...  8.88 us
    unnamed x4, local copies, waits for them, and re-layouts  1.74 us
  transfers between devices with their start and end apart: 19, of which 12 were waited for; matrix products, arithmetic and copies ran while one was open for 0% of the time, Pallas kernels for 12%

profile of v2, /device:TPU:0, one launch (start us, length us, event | category | flops | bytes accessed | tf_op | source)
XLA Modules:
  0.0 62.0 jit_solution(309478165820697927)
XLA Ops:
  2.5 1.6 %collective-permute-start = (bf16[112,768]{1,0:T(8,128)(2,1)S(1)}, bf16[112,768]{1,0:T(8,128)(2,1)S(1)}, u32[]{:S(2)}, u32[]{:S(2)}) collective-permute-start(bf16[112,768]{1,0:T(8,128)(2,1)S(1)} %get-tuple-element.19), channel_id=1, source_target_pairs={{96,0},{97,1},{98,2},{99,3},{100,4},{101,5},{102,6},{103,7},{104,8... | collective-permute-start | bytes 516104 | tf_op jit(solution)/shard_map/ppermute | solution.py:211
  4.1 1.7 %collective-permute-start.1 = (bf16[112,768]{1,0:T(8,128)(2,1)S(1)}, bf16[112,768]{1,0:T(8,128)(2,1)S(1)}, u32[]{:S(2)}, u32[]{:S(2)}) collective-permute-start(bf16[112,768]{1,0:T(8,128)(2,1)S(1)} %get-tuple-element.20), channel_id=1, source_target_pairs={{32,0},{33,1},{34,2},{35,3},{36,4},{37,5},{38,6},{39,7},{40,8},{41... | collective-permute-start | bytes 516104 | tf_op jit(solution)/shard_map/ppermute | solution.py:211
  5.8 1.9 %collective-permute-start.2 = (bf16[112,768]{1,0:T(8,128)(2,1)S(1)}, bf16[112,768]{1,0:T(8,128)(2,1)S(1)}, u32[]{:S(2)}, u32[]{:S(2)}) collective-permute-start(bf16[112,768]{1,0:T(8,128)(2,1)S(1)} %get-tuple-element.21), channel_id=1, source_target_pairs={{64,0},{65,1},{66,2},{67,3},{68,4},{69,5},{70,6},{71,7},{72,8},{73... | collective-permute-start | bytes 516104 | tf_op jit(solution)/shard_map/ppermute | solution.py:211
  7.7 2.1 %collective-permute-done.c1_ref = bf16[112,768]{1,0:T(8,128)(2,1)S(1)} collective-permute-done((bf16[112,768]{1,0:T(8,128)(2,1)S(1)}, bf16[112,768]{1,0:T(8,128)(2,1)S(1)}, u32[]{:S(2)}, u32[]{:S(2)}) %collective-permute-start) | collective-permute-done | bytes 172064 | tf_op jit(solution)/shard_map/ppermute | solution.py:211
  9.8 1.7 %collective-permute-done.1.c2_ref = bf16[112,768]{1,0:T(8,128)(2,1)S(1)} collective-permute-done((bf16[112,768]{1,0:T(8,128)(2,1)S(1)}, bf16[112,768]{1,0:T(8,128)(2,1)S(1)}, u32[]{:S(2)}, u32[]{:S(2)}) %collective-permute-start.1) | collective-permute-done | bytes 172064 | tf_op jit(solution)/shard_map/ppermute | solution.py:211
  11.4 3.2 %collective-permute-done.2.c3_ref = bf16[112,768]{1,0:T(8,128)(2,1)S(1)} collective-permute-done((bf16[112,768]{1,0:T(8,128)(2,1)S(1)}, bf16[112,768]{1,0:T(8,128)(2,1)S(1)}, u32[]{:S(2)}, u32[]{:S(2)}) %collective-permute-start.2) | collective-permute-done | bytes 172064 | tf_op jit(solution)/shard_map/ppermute | solution.py:211
  14.8 1.6 %collective-permute-start.7 = (bf16[400,768]{1,0:T(8,128)(2,1)S(1)}, bf16[400,768]{1,0:T(8,128)(2,1)S(1)}, u32[]{:S(2)}, u32[]{:S(2)}) collective-permute-start(bf16[400,768]{1,0:T(8,128)(2,1)S(1)} %join.1.refs_2_.refs_3_.refs_0_.refs_4_), channel_id=1, source_target_pairs={{24,0},{9,1},{26,2},{11,3},{28,4},{13,5},{30,6},{15,7},{0,8},{17,9... | collective-permute-start | bytes 1843208 | tf_op jit(solution)/shard_map/ppermute | solution.py:211
  16.4 1.9 %collective-permute-start.8 = (bf16[400,768]{1,0:T(8,128)(2,1)S(1)}, bf16[400,768]{1,0:T(8,128)(2,1)S(1)}, u32[]{:S(2)}, u32[]{:S(2)}) collective-permute-start(bf16[400,768]{1,0:T(8,128)(2,1)S(1)} %join.1.refs_2_.refs_3_.refs_0_.refs_4_), channel_id=1, source_target_pairs={{6,0},{3,1},{0,2},{5,3},{2,4},{7,5},{4,6},{1,7},{14,8},{11,9},{8,1... | collective-permute-start | bytes 1843208 | tf_op jit(solution)/shard_map/ppermute | solution.py:211
  18.4 1.6 %collective-permute-start.4 = (bf16[400,768]{1,0:T(8,128)(2,1)S(1)}, bf16[400,768]{1,0:T(8,128)(2,1)S(1)}, u32[]{:S(2)}, u32[]{:S(2)}) collective-permute-start(bf16[400,768]{1,0:T(8,128)(2,1)S(1)} %collective-permute-done.3.refs_4_.refs_5_), channel_id=1, source_target_pairs={{24,0},{9,1},{26,2},{11,3},{28,4},{13,5},{30,6},{15,7},{0,8},{17,9... | collective-permute-start | bytes 1843208 | tf_op jit(solution)/shard_map/ppermute | solution.py:211
  19.9 1.9 %collective-permute-start.5 = (bf16[400,768]{1,0:T(8,128)(2,1)S(1)}, bf16[400,768]{1,0:T(8,128)(2,1)S(1)}, u32[]{:S(2)}, u32[]{:S(2)}) collective-permute-start(bf16[400,768]{1,0:T(8,128)(2,1)S(1)} %collective-permute-done.3.refs_4_.refs_5_), channel_id=1, source_target_pairs={{6,0},{3,1},{0,2},{5,3},{2,4},{7,5},{4,6},{1,7},{14,8},{11,9},{8,1... | collective-permute-start | bytes 1843208 | tf_op jit(solution)/shard_map/ppermute | solution.py:211
  21.9 4.4 %collective-permute-done.7.refs_5_.refs_6_ = bf16[400,768]{1,0:T(8,128)(2,1)S(1)} collective-permute-done((bf16[400,768]{1,0:T(8,128)(2,1)S(1)}, bf16[400,768]{1,0:T(8,128)(2,1)S(1)}, u32[]{:S(2)}, u32[]{:S(2)}) %collective-permute-start.7) | collective-permute-done | bytes 614432 | tf_op jit(solution)/shard_map/ppermute | solution.py:211
  26.2 2.4 %collective-permute-done.8.refs_0_ = bf16[400,768]{1,0:T(8,128)(2,1)S(1)} collective-permute-done((bf16[400,768]{1,0:T(8,128)(2,1)S(1)}, bf16[400,768]{1,0:T(8,128)(2,1)S(1)}, u32[]{:S(2)}, u32[]{:S(2)}) %collective-permute-start.8) | collective-permute-done | bytes 614432 | tf_op jit(solution)/shard_map/ppermute | solution.py:211
  30.2 2.6 %collective-permute-done.4.refs_7_.refs_1_.refs_8_ = bf16[400,768]{1,0:T(8,128)(2,1)S(1)} collective-permute-done((bf16[400,768]{1,0:T(8,128)(2,1)S(1)}, bf16[400,768]{1,0:T(8,128)(2,1)S(1)}, u32[]{:S(2)}, u32[]{:S(2)}) %collective-permute-start.4) | collective-permute-done | bytes 614432 | tf_op jit(solution)/shard_map/ppermute | solution.py:211
  32.8 2.4 %collective-permute-done.5.refs_1_ = bf16[400,768]{1,0:T(8,128)(2,1)S(1)} collective-permute-done((bf16[400,768]{1,0:T(8,128)(2,1)S(1)}, bf16[400,768]{1,0:T(8,128)(2,1)S(1)}, u32[]{:S(2)}, u32[]{:S(2)}) %collective-permute-start.5) | collective-permute-done | bytes 614432 | tf_op jit(solution)/shard_map/ppermute | solution.py:211
  35.5 3.6 %pairs_a.1 = f32[3,1,384]{2,1,0:T(1,128)S(1)} custom-call(bf16[400,768]{1,0:T(8,128)(2,1)S(1)} %collective-permute-done.8.refs_0_, bf16[400,768]{1,0:T(8,128)(2,1)S(1)} %collective-permute-done.5.refs_1_, bf16[400,768]{1,0:T(8,128)(2,1)S(1)} %join.1.refs_2_.refs_3_.refs_0_.refs_4_, bf16[400,768]{1,0:T(8,128)(2,1)S(1)} %join.1.refs_2_.refs_3_.refs_0_.refs_4_, ...), custom_call_target="tpu_custom_call" | custom-call | flops 3170893824 | bytes 4718592 | tf_op jit(solution)/shard_map/pairs_a/pallas_call | solution.py:162
  39.0 2.7 %collective-permute-done.10.refs_2_ = bf16[400,768]{1,0:T(8,128)(2,1)S(1)} collective-permute-done((bf16[400,768]{1,0:T(8,128)(2,1)S(1)}, bf16[400,768]{1,0:T(8,128)(2,1)S(1)}, u32[]{:S(2)}, u32[]{:S(2)}) %collective-permute-start.10) | collective-permute-done | bytes 614432 | tf_op jit(solution)/shard_map/ppermute | solution.py:211
  42.0 2.3 %pairs_b.1 = f32[3,1,384]{2,1,0:T(1,128)S(1)} custom-call(bf16[400,768]{1,0:T(8,128)(2,1)S(1)} %collective-permute-done.8.refs_0_, bf16[400,768]{1,0:T(8,128)(2,1)S(1)} %collective-permute-done.5.refs_1_, bf16[400,768]{1,0:T(8,128)(2,1)S(1)} %collective-permute-done.10.refs_2_, bf16[400,768]{1,0:T(8,128)(2,1)S(1)} %collective-permute-done.6.refs_2_.refs_3_, ...), custom_call_target="tpu_custom_call" | custom-call | flops 1811939328 | bytes 5308416 | tf_op jit(solution)/shard_map/pairs_b/pallas_call | solution.py:162
  44.4 1.7 %pairs_f.1 = f32[3,1,384]{2,1,0:T(1,128)S(1)} custom-call(bf16[400,768]{1,0:T(8,128)(2,1)S(1)} %collective-permute-done.8.refs_0_, bf16[400,768]{1,0:T(8,128)(2,1)S(1)} %collective-permute-done.5.refs_1_, bf16[400,768]{1,0:T(8,128)(2,1)S(1)} %collective-permute-done.10.refs_2_, bf16[400,768]{1,0:T(8,128)(2,1)S(1)} %collective-permute-done.9.refs_3_, ...), custom_call_target="tpu_custom_call" | custom-call | flops 1358954496 | bytes 2949120 | tf_op jit(solution)/shard_map/pairs_f/pallas_call | solution.py:162
  46.1 3.6 %collective-permute-start.13 = (f32[1,384]{1,0:T(1,128)S(1)}, f32[1,384]{1,0:T(1,128)S(1)}, u32[]{:S(2)}, u32[]{:S(2)}) collective-permute-start(f32[1,384]{1,0:T(1,128)S(1)} %get-tuple-element.31), channel_id=1, source_target_pairs={{4,0},{5,1},{6,2},{7,3},{0,4},{1,5},{2,6},{3,7},{12,8},{13,9},{14,... | collective-permute-start | bytes 4616 | tf_op jit(solution)/shard_map/ppermute | solution.py:211
  49.8 2.7 %collective-permute-start.15 = (f32[1,384]{1,0:T(1,128)S(1)}, f32[1,384]{1,0:T(1,128)S(1)}, u32[]{:S(2)}, u32[]{:S(2)}) collective-permute-start(f32[1,384]{1,0:T(1,128)S(1)} %get-tuple-element.30), channel_id=1, source_target_pairs={{7,0},{2,1},{1,2},{4,3},{3,4},{6,5},{5,6},{0,7},{15,8},{10,9},{9,1... | collective-permute-start | bytes 4616 | tf_op jit(solution)/shard_map/ppermute | solution.py:211
  52.5 1.3 %pairs_own.1 = f32[1,1,384]{2,1,0:T(1,128)S(1)} custom-call(bf16[400,768]{1,0:T(8,128)(2,1)S(1)} %join.1.refs_2_.refs_3_.refs_0_.refs_4_, bf16[400,768]{1,0:T(8,128)(2,1)S(1)} %collective-permute-done.4.refs_7_.refs_1_.refs_8_, bf16[400,768]{1,0:T(8,128)(2,1)S(1)} %collective-permute-done.6.refs_2_.refs_3_, ...), custom_call_target="tpu_custom_call" | custom-call | flops 905969664 | bytes 2949120 | tf_op jit(solution)/shard_map/pairs_own/pallas_call | solution.py:162
  54.1 2.0 %collective-permute-start.16 = (f32[1,384]{1,0:T(1,128)S(1)}, f32[1,384]{1,0:T(1,128)S(1)}, u32[]{:S(2)}, u32[]{:S(2)}) collective-permute-start(f32[1,384]{1,0:T(1,128)S(1)} %fusion.4.m0_ref), channel_id=1, source_target_pairs={{32,0},{33,1},{34,2},{35,3},{36,4},{37,5},{38,6},{39,7},{40,8},{41... | collective-permute-start | bytes 4616 | tf_op jit(solution)/shard_map/ppermute | solution.py:211
  56.2 1.5 %collective-permute-start.18 = (f32[1,384]{1,0:T(1,128)S(1)}, f32[1,384]{1,0:T(1,128)S(1)}, u32[]{:S(2)}, u32[]{:S(2)}) collective-permute-start(f32[1,384]{1,0:T(1,128)S(1)} %fusion.4.m0_ref), channel_id=1, source_target_pairs={{64,0},{65,1},{66,2},{67,3},{68,4},{69,5},{70,6},{71,7},{72,8},{73... | collective-permute-start | bytes 4616 | tf_op jit(solution)/shard_map/ppermute | solution.py:211
  57.7 3.2 %collective-permute-done.17.m2_ref = f32[1,384]{1,0:T(1,128)S(1)} collective-permute-done((f32[1,384]{1,0:T(1,128)S(1)}, f32[1,384]{1,0:T(1,128)S(1)}, u32[]{:S(2)}, u32[]{:S(2)}) %collective-permute-start.17) | collective-permute-done | bytes 1568 | tf_op jit(solution)/shard_map/ppermute | solution.py:211
  (28 shorter events, 6.3 us)
Async XLA Ops:
  0.0 0.7 %copy-start.1 = (s32[384]{0:T(512)S(1)}, s32[384]{0:T(512)}, u32[]{:S(2)}) copy-start(s32[384]{0:T(512)} %param.3) | copy-start | bytes 4612
  0.7 1.1 %copy-start = (bf16[384,768]{1,0:T(8,128)(2,1)S(1)}, bf16[384,768]{1,0:T(8,128)(2,1)}, u32[]{:S(2)}) copy-start(bf16[384,768]{1,0:T(8,128)(2,1)} %emb_ref.1) | copy-start | bytes 1769476
  2.5 7.3 %collective-permute-start = (bf16[112,768]{1,0:T(8,128)(2,1)S(1)}, bf16[112,768]{1,0:T(8,128)(2,1)S(1)}, u32[]{:S(2)}, u32[]{:S(2)}) collective-permute-start(bf16[112,768]{1,0:T(8,128)(2,1)S(1)} %get-tuple-element.19), channel_id=1, source_target_pairs={{96,0},{97,1},{98,2},{99,3},{100,4},{101,5},{102,6},{103,7},{104,8... | collective-permute-start | bytes 516104 | tf_op jit(solution)/shard_map/ppermute | solution.py:211
  4.1 7.3 %collective-permute-start.1 = (bf16[112,768]{1,0:T(8,128)(2,1)S(1)}, bf16[112,768]{1,0:T(8,128)(2,1)S(1)}, u32[]{:S(2)}, u32[]{:S(2)}) collective-permute-start(bf16[112,768]{1,0:T(8,128)(2,1)S(1)} %get-tuple-element.20), channel_id=1, source_target_pairs={{32,0},{33,1},{34,2},{35,3},{36,4},{37,5},{38,6},{39,7},{40,8},{41... | collective-permute-start | bytes 516104 | tf_op jit(solution)/shard_map/ppermute | solution.py:211
  5.8 8.8 %collective-permute-start.2 = (bf16[112,768]{1,0:T(8,128)(2,1)S(1)}, bf16[112,768]{1,0:T(8,128)(2,1)S(1)}, u32[]{:S(2)}, u32[]{:S(2)}) collective-permute-start(bf16[112,768]{1,0:T(8,128)(2,1)S(1)} %get-tuple-element.21), channel_id=1, source_target_pairs={{64,0},{65,1},{66,2},{67,3},{68,4},{69,5},{70,6},{71,7},{72,8},{73... | collective-permute-start | bytes 516104 | tf_op jit(solution)/shard_map/ppermute | solution.py:211
  14.7 3.7 %collective-permute-start.3 = (bf16[400,768]{1,0:T(8,128)(2,1)S(1)}, bf16[400,768]{1,0:T(8,128)(2,1)S(1)}, u32[]{:S(2)}, u32[]{:S(2)}) collective-permute-start(bf16[400,768]{1,0:T(8,128)(2,1)S(1)} %join.1.refs_2_.refs_3_.refs_0_.refs_4_), channel_id=1, source_target_pairs={{1,0},{0,1},{3,2},{2,3},{5,4},{4,5},{7,6},{6,7},{9,8},{8,9},{11,10... | collective-permute-start | bytes 1843208 | tf_op jit(solution)/shard_map/ppermute | solution.py:211
  14.8 11.4 %collective-permute-start.7 = (bf16[400,768]{1,0:T(8,128)(2,1)S(1)}, bf16[400,768]{1,0:T(8,128)(2,1)S(1)}, u32[]{:S(2)}, u32[]{:S(2)}) collective-permute-start(bf16[400,768]{1,0:T(8,128)(2,1)S(1)} %join.1.refs_2_.refs_3_.refs_0_.refs_4_), channel_id=1, source_target_pairs={{24,0},{9,1},{26,2},{11,3},{28,4},{13,5},{30,6},{15,7},{0,8},{17,9... | collective-permute-start | bytes 1843208 | tf_op jit(solution)/shard_map/ppermute | solution.py:211
  16.4 12.2 %collective-permute-start.8 = (bf16[400,768]{1,0:T(8,128)(2,1)S(1)}, bf16[400,768]{1,0:T(8,128)(2,1)S(1)}, u32[]{:S(2)}, u32[]{:S(2)}) collective-permute-start(bf16[400,768]{1,0:T(8,128)(2,1)S(1)} %join.1.refs_2_.refs_3_.refs_0_.refs_4_), channel_id=1, source_target_pairs={{6,0},{3,1},{0,2},{5,3},{2,4},{7,5},{4,6},{1,7},{14,8},{11,9},{8,1... | collective-permute-start | bytes 1843208 | tf_op jit(solution)/shard_map/ppermute | solution.py:211
  18.4 14.4 %collective-permute-start.4 = (bf16[400,768]{1,0:T(8,128)(2,1)S(1)}, bf16[400,768]{1,0:T(8,128)(2,1)S(1)}, u32[]{:S(2)}, u32[]{:S(2)}) collective-permute-start(bf16[400,768]{1,0:T(8,128)(2,1)S(1)} %collective-permute-done.3.refs_4_.refs_5_), channel_id=1, source_target_pairs={{24,0},{9,1},{26,2},{11,3},{28,4},{13,5},{30,6},{15,7},{0,8},{17,9... | collective-permute-start | bytes 1843208 | tf_op jit(solution)/shard_map/ppermute | solution.py:211
  19.9 15.2 %collective-permute-start.5 = (bf16[400,768]{1,0:T(8,128)(2,1)S(1)}, bf16[400,768]{1,0:T(8,128)(2,1)S(1)}, u32[]{:S(2)}, u32[]{:S(2)}) collective-permute-start(bf16[400,768]{1,0:T(8,128)(2,1)S(1)} %collective-permute-done.3.refs_4_.refs_5_), channel_id=1, source_target_pairs={{6,0},{3,1},{0,2},{5,3},{2,4},{7,5},{4,6},{1,7},{14,8},{11,9},{8,1... | collective-permute-start | bytes 1843208 | tf_op jit(solution)/shard_map/ppermute | solution.py:211
  28.6 6.9 %collective-permute-start.11 = (bf16[400,768]{1,0:T(8,128)(2,1)S(1)}, bf16[400,768]{1,0:T(8,128)(2,1)S(1)}, u32[]{:S(2)}, u32[]{:S(2)}) collective-permute-start(bf16[400,768]{1,0:T(8,128)(2,1)S(1)} %collective-permute-done.7.refs_5_.refs_6_), channel_id=1, source_target_pairs={{1,0},{0,1},{3,2},{2,3},{5,4},{4,5},{7,6},{6,7},{9,8},{8,9},{11,10... | collective-permute-start | bytes 1843208 | tf_op jit(solution)/shard_map/ppermute | solution.py:211
  28.9 12.9 %collective-permute-start.10 = (bf16[400,768]{1,0:T(8,128)(2,1)S(1)}, bf16[400,768]{1,0:T(8,128)(2,1)S(1)}, u32[]{:S(2)}, u32[]{:S(2)}) collective-permute-start(bf16[400,768]{1,0:T(8,128)(2,1)S(1)} %collective-permute-done.8.refs_0_), channel_id=1, source_target_pairs={{6,0},{3,1},{0,2},{5,3},{2,4},{7,5},{4,6},{1,7},{14,8},{11,9},{8,1... | collective-permute-start | bytes 1843208 | tf_op jit(solution)/shard_map/ppermute | solution.py:211
  29.4 12.4 %collective-permute-start.9 = (bf16[400,768]{1,0:T(8,128)(2,1)S(1)}, bf16[400,768]{1,0:T(8,128)(2,1)S(1)}, u32[]{:S(2)}, u32[]{:S(2)}) collective-permute-start(bf16[400,768]{1,0:T(8,128)(2,1)S(1)} %collective-permute-done.7.refs_5_.refs_6_), channel_id=1, source_target_pairs={{24,0},{9,1},{26,2},{11,3},{28,4},{13,5},{30,6},{15,7},{0,8},{17,9... | collective-permute-start | bytes 1843208 | tf_op jit(solution)/shard_map/ppermute | solution.py:211
  35.2 6.9 %collective-permute-start.6 = (bf16[400,768]{1,0:T(8,128)(2,1)S(1)}, bf16[400,768]{1,0:T(8,128)(2,1)S(1)}, u32[]{:S(2)}, u32[]{:S(2)}) collective-permute-start(bf16[400,768]{1,0:T(8,128)(2,1)S(1)} %collective-permute-done.4.refs_7_.refs_1_.refs_8_), channel_id=1, source_target_pairs={{1,0},{0,1},{3,2},{2,3},{5,4},{4,5},{7,6},{6,7},{9,8},{8,9},{11,10... | collective-permute-start | bytes 1843208 | tf_op jit(solution)/shard_map/ppermute | solution.py:211
  41.8 2.6 %collective-permute-start.12 = (bf16[400,768]{1,0:T(8,128)(2,1)S(1)}, bf16[400,768]{1,0:T(8,128)(2,1)S(1)}, u32[]{:S(2)}, u32[]{:S(2)}) collective-permute-start(bf16[400,768]{1,0:T(8,128)(2,1)S(1)} %collective-permute-done.9.refs_3_), channel_id=1, source_target_pairs={{1,0},{0,1},{3,2},{2,3},{5,4},{4,5},{7,6},{6,7},{9,8},{8,9},{11,10... | collective-permute-start | bytes 1843208 | tf_op jit(solution)/shard_map/ppermute | solution.py:211
  46.1 7.7 %collective-permute-start.13 = (f32[1,384]{1,0:T(1,128)S(1)}, f32[1,384]{1,0:T(1,128)S(1)}, u32[]{:S(2)}, u32[]{:S(2)}) collective-permute-start(f32[1,384]{1,0:T(1,128)S(1)} %get-tuple-element.31), channel_id=1, source_target_pairs={{4,0},{5,1},{6,2},{7,3},{0,4},{1,5},{2,6},{3,7},{12,8},{13,9},{14,... | collective-permute-start | bytes 4616 | tf_op jit(solution)/shard_map/ppermute | solution.py:211
  49.7 4.1 %collective-permute-start.14 = (f32[1,384]{1,0:T(1,128)S(1)}, f32[1,384]{1,0:T(1,128)S(1)}, u32[]{:S(2)}, u32[]{:S(2)}) collective-permute-start(f32[1,384]{1,0:T(1,128)S(1)} %get-tuple-element.29), channel_id=1, source_target_pairs={{2,0},{7,1},{4,2},{1,3},{6,4},{3,5},{0,6},{5,7},{10,8},{15,9},{12,... | collective-permute-start | bytes 4616 | tf_op jit(solution)/shard_map/ppermute | solution.py:211
  49.8 4.2 %collective-permute-start.15 = (f32[1,384]{1,0:T(1,128)S(1)}, f32[1,384]{1,0:T(1,128)S(1)}, u32[]{:S(2)}, u32[]{:S(2)}) collective-permute-start(f32[1,384]{1,0:T(1,128)S(1)} %get-tuple-element.30), channel_id=1, source_target_pairs={{7,0},{2,1},{1,2},{4,3},{3,4},{6,5},{5,6},{0,7},{15,8},{10,9},{9,1... | collective-permute-start | bytes 4616 | tf_op jit(solution)/shard_map/ppermute | solution.py:211
  54.1 3.6 %collective-permute-start.16 = (f32[1,384]{1,0:T(1,128)S(1)}, f32[1,384]{1,0:T(1,128)S(1)}, u32[]{:S(2)}, u32[]{:S(2)}) collective-permute-start(f32[1,384]{1,0:T(1,128)S(1)} %fusion.4.m0_ref), channel_id=1, source_target_pairs={{32,0},{33,1},{34,2},{35,3},{36,4},{37,5},{38,6},{39,7},{40,8},{41... | collective-permute-start | bytes 4616 | tf_op jit(solution)/shard_map/ppermute | solution.py:211
  56.1 4.8 %collective-permute-start.17 = (f32[1,384]{1,0:T(1,128)S(1)}, f32[1,384]{1,0:T(1,128)S(1)}, u32[]{:S(2)}, u32[]{:S(2)}) collective-permute-start(f32[1,384]{1,0:T(1,128)S(1)} %fusion.4.m0_ref), channel_id=1, source_target_pairs={{96,0},{97,1},{98,2},{99,3},{100,4},{101,5},{102,6},{103,7},{104,8... | collective-permute-start | bytes 4616 | tf_op jit(solution)/shard_map/ppermute | solution.py:211
  56.2 5.1 %collective-permute-start.18 = (f32[1,384]{1,0:T(1,128)S(1)}, f32[1,384]{1,0:T(1,128)S(1)}, u32[]{:S(2)}, u32[]{:S(2)}) collective-permute-start(f32[1,384]{1,0:T(1,128)S(1)} %fusion.4.m0_ref), channel_id=1, source_target_pairs={{64,0},{65,1},{66,2},{67,3},{68,4},{69,5},{70,6},{71,7},{72,8},{73... | collective-permute-start | bytes 4616 | tf_op jit(solution)/shard_map/ppermute | solution.py:211

commit v3 on v2

--- a/solution.py
+++ b/solution.py
@@ -16,7 +16,7 @@
 STEPS = (0, 1, 3, 2)
 AXES = ("x", "y", "z", "c")
 SIZES = (4, 4, 4, 2)
-TAIL = 16
+TAIL = 8
 VMEM_LIMIT = 32 * 1024 * 1024
 
 
@@ -33,25 +33,31 @@
     return jnp.sum(jnp.where(down == across, row, 0.0), axis=1, keepdims=True)
 
 
-def prepare_kernel(x_ref, emb_ref, ids_ref, c0_ref, c1_ref, c3_ref, c2_ref, pos_ref):
+def prepare_kernel(x_ref, emb_hbm, ids_hbm, c0_ref, c1_ref, c3_ref, c2_ref, pos_ref, emb_ref, ids_ref, sems):
+    emb_copy = pltpu.make_async_copy(emb_hbm, emb_ref, sems.at[0])
+    ids_copy = pltpu.make_async_copy(ids_hbm, ids_ref, sems.at[1])
+    emb_copy.start()
+    ids_copy.start()
     rows = emb_ref.shape[0]
     share = rows // GROUPS
-    values = emb_ref[...].astype(jnp.float32)
-    scale = lax.rsqrt(jnp.sum(values * values, axis=1, keepdims=True) + 1e-06)
-    units = (values * scale).astype(jnp.bfloat16)
-    ids = ids_ref[...]
     down, across = iotas(rows, rows)
+    ids_copy.wait()
+    ids = ids_ref[...].reshape(1, rows)
     steps = (lax.shift_right_logical(ids, 6) - x_ref[0]) & (GROUPS - 1)
     slot = steps ^ lax.shift_right_logical(steps, 1)
     key = (slot * rows + across[:1]).astype(jnp.float32)
     pos = jnp.sum(jnp.where(as_column(key) < key, 1.0, 0.0), axis=0, keepdims=True)
     pos_ref[...] = pos
     place = jnp.where(down.astype(jnp.float32) == pos, 1.0, 0.0).astype(jnp.bfloat16)
-    placed = jnp.dot(place, units, preferred_element_type=jnp.float32).astype(jnp.bfloat16)
     wide = jnp.broadcast_to(ids.astype(jnp.float32), (TAIL, rows)).astype(jnp.bfloat16)
     placed_ids = lax.dot_general(
         wide, place, (((1,), (1,)), ((), ())), preferred_element_type=jnp.float32
     )
+    emb_copy.wait()
+    values = emb_ref[...].astype(jnp.float32)
+    scale = lax.rsqrt(jnp.sum(values * values, axis=1, keepdims=True) + 1e-06)
+    units = (values * scale).astype(jnp.bfloat16)
+    placed = jnp.dot(place, units, preferred_element_type=jnp.float32).astype(jnp.bfloat16)
     chunk_of = lax.broadcasted_iota(jnp.int32, (TAIL, rows), 1)
     for k, out in enumerate((c0_ref, c1_ref, c3_ref, c2_ref)):
         out[:share, :] = placed[k * share : (k + 1) * share]
@@ -69,12 +75,17 @@
         out_shape=[chunk] * GROUPS + [jax.ShapeDtypeStruct((1, rows), jnp.float32)],
         in_specs=[
             pl.BlockSpec(memory_space=pltpu.SMEM),
-            pl.BlockSpec(memory_space=pltpu.VMEM),
-            pl.BlockSpec(memory_space=pltpu.VMEM),
+            pl.BlockSpec(memory_space=pltpu.HBM),
+            pl.BlockSpec(memory_space=pltpu.HBM),
         ],
+        scratch_shapes=[
+            pltpu.VMEM((rows, width), jnp.bfloat16),
+            pltpu.VMEM((rows,), jnp.int32),
+            pltpu.SemaphoreType.DMA((2,)),
+        ],
         compiler_params=pltpu.CompilerParams(vmem_limit_bytes=VMEM_LIMIT),
         name="prepare",
-    )(x_index, embeddings, ids)
+    )(x_index, *(pltpu.with_memory_space_constraint(a, pltpu.HBM) for a in (embeddings, ids)))
 
 
 def join_kernel(c0_ref, c1_ref, c2_ref, c3_ref, out_ref):
@@ -230,17 +241,16 @@
 def shards(embeddings, cluster_ids):
     rows = embeddings.shape[0]
     x_index = lax.axis_index("x").astype(jnp.int32).reshape(1)
-    *chunks, pos = prepare(x_index, embeddings, cluster_ids.reshape(1, rows))
+    *chunks, pos = prepare(x_index, embeddings, cluster_ids)
     for k, step in enumerate(STEPS):
         if step:
             chunks[k] = receive(chunks[k], lambda x, y, z, c, step=step: (x - step, y, z, c))
     own = join(chunks)
 
-    ay, az = lax.optimization_barrier((near_y(own), near_z(own)))
+    az, ay = lax.optimization_barrier((near_z(own), near_y(own)))
     other = swap(own)
     fz, fy = near_z(az), near_y(ay)
-    bz, by = near_z(other), near_y(other)
-    by, bz = lax.optimization_barrier((by, bz))
+    bz, by = lax.optimization_barrier((near_z(other), near_y(other)))
     ay2, by2 = swap(ay), swap(by)
     s1 = pair_sums(
         [az, bz, own],
@@ -256,21 +266,19 @@
         ),
         name="pairs_a",
     )
-    fy, fz, s1 = lax.optimization_barrier((fy, fz, s1))
+    fy, s1 = lax.optimization_barrier((fy, s1))
     fy2 = swap(fy)
-    s2 = pair_sums(
+    s2 = pair_sums([az, bz], [by2, fy], (((0, 1), (0,)), ((0, 1), (1,))), name="pairs_b")
+    s3 = pair_sums(
         [az, bz, fz],
-        [by2, own, other, ay, ay2, by],
-        (((0, 1), (0,)), ((2,), (1, 2)), ((2,), (3, 4)), ((2,), (5, 0))),
-        name="pairs_b",
-    )
-    s3 = pair_sums(
-        [az, bz, fz], [fy, fy2], (((0, 1), (0,)), ((0, 1), (1,)), ((2,), (0, 1))), name="pairs_f"
+        [own, other, ay, ay2, by, by2, fy, fy2],
+        (((2,), (0, 1)), ((2,), (2, 3)), ((2,), (4, 5)), ((2,), (6, 7)), ((0, 1), (7,))),
+        name="pairs_f",
     )
     s0 = pair_sums([own], [by, by2, fy, fy2], (((0,), (0, 1)), ((0,), (2, 3))), name="pairs_own")
     mass_a = s1[0] + s2[0] + s3[0]
     mass_b = s1[1] + s2[1] + s3[1]
-    mass_f = s2[2] + s3[2]
+    mass_f = s3[2]
     mass = (
         s0[0]
         + s1[2]

time: 62.5 us -> 59.9 us (0.958)
  local copies, waits for them, and re-layouts: 1.75 us -> 0 us
  starting transfers between devices: 24.4 us -> 23 us
  Pallas kernels: 10.4 us -> 11.4 us
    unnamed x4 -> x0, local copies, waits for them, and re-layouts: 1.74 us -> none
    ppermute x19, starting transfers between devices: 24.4 us -> 23 us  [receive(): return lax.ppermute(array, AXES, pairs_of(source_of))]
    pallas_call x1, Pallas kernels: 0.73 us -> 1.88 us  [prepare(): pl.pallas_call(prepare_kernel, out_shape=[chunk] * GROUPS + [jax.ShapeDty...]
  transfers between devices with their start and end apart: 19 -> 19, of which waited for: 12 -> 15; matrix products, arithmetic and copies ran while one was open for 0% -> 0% of each run, Pallas kernels for 12% -> 10%
where the time goes in v3:
time: 59.9 us; the launch traced here: 59.8 us
  waiting for transfers between devices  25.3 us (42%)
  starting transfers between devices  23 us (38%)
  Pallas kernels  11.4 us (19%)
    ppermute x19, waiting for transfers between devices, receive(): return lax.ppermute(array, AXES, pairs_of(source_of))  25.3 us
    ppermute x19, starting transfers between devices, receive(): return lax.ppermute(array, AXES, pairs_of(source_of))  23 us
    pallas_call x4, Pallas kernels, pair_sums(): pl.pallas_call(functools.partial(pairs_kernel, nq, nk, plan), out_shape=j...  8.75 us
    pallas_call x1, Pallas kernels, prepare(): pl.pallas_call(prepare_kernel, out_shape=[chunk] * GROUPS + [jax.ShapeDty...  1.88 us
  transfers between devices with their start and end apart: 19, of which 15 were waited for; matrix products, arithmetic and copies ran while one was open for 0% of the time, Pallas kernels for 10%

profile of v3, /device:TPU:0, one launch (start us, length us, event | category | flops | bytes accessed | tf_op | source)
XLA Modules:
  0.0 59.8 jit_solution(490629754728187754)
XLA Ops:
  0.0 1.9 %prepare.1 = (bf16[104,768]{1,0:T(8,128)(2,1)S(1)}, bf16[104,768]{1,0:T(8,128)(2,1)S(1)}, bf16[104,768]{1,0:T(8,128)(2,1)S(1)}, bf16[104,768]{1,0:T(8,128)(2,1)S(1)}, f32[1,384]{1,0:T(1,128)S(1)}) custom-call(s32[1]{0:T(128)} %bitcast.x_ref, bf16[384,768]{1,0:T(8,128)(2,1)} %emb_hbm.1, s32[384]{0:T(512)} %ids_hbm.1), custom_call_target="tpu_custom_call" | custom-call | tf_op jit(solution)/shard_map/prepare/pallas_call | solution.py:73
  1.9 1.6 %collective-permute-start = (bf16[104,768]{1,0:T(8,128)(2,1)S(1)}, bf16[104,768]{1,0:T(8,128)(2,1)S(1)}, u32[]{:S(2)}, u32[]{:S(2)}) collective-permute-start(bf16[104,768]{1,0:T(8,128)(2,1)S(1)} %get-tuple-element.18), channel_id=1, source_target_pairs={{96,0},{97,1},{98,2},{99,3},{100,4},{101,5},{102,6},{103,7},{104,8... | collective-permute-start | bytes 479240 | tf_op jit(solution)/shard_map/ppermute | solution.py:222
  3.5 1.7 %collective-permute-start.1 = (bf16[104,768]{1,0:T(8,128)(2,1)S(1)}, bf16[104,768]{1,0:T(8,128)(2,1)S(1)}, u32[]{:S(2)}, u32[]{:S(2)}) collective-permute-start(bf16[104,768]{1,0:T(8,128)(2,1)S(1)} %get-tuple-element.19), channel_id=1, source_target_pairs={{32,0},{33,1},{34,2},{35,3},{36,4},{37,5},{38,6},{39,7},{40,8},{41... | collective-permute-start | bytes 479240 | tf_op jit(solution)/shard_map/ppermute | solution.py:222
  5.2 1.9 %collective-permute-start.2 = (bf16[104,768]{1,0:T(8,128)(2,1)S(1)}, bf16[104,768]{1,0:T(8,128)(2,1)S(1)}, u32[]{:S(2)}, u32[]{:S(2)}) collective-permute-start(bf16[104,768]{1,0:T(8,128)(2,1)S(1)} %get-tuple-element.20), channel_id=1, source_target_pairs={{64,0},{65,1},{66,2},{67,3},{68,4},{69,5},{70,6},{71,7},{72,8},{73... | collective-permute-start | bytes 479240 | tf_op jit(solution)/shard_map/ppermute | solution.py:222
  7.1 1.8 %collective-permute-done.c1_ref = bf16[104,768]{1,0:T(8,128)(2,1)S(1)} collective-permute-done((bf16[104,768]{1,0:T(8,128)(2,1)S(1)}, bf16[104,768]{1,0:T(8,128)(2,1)S(1)}, u32[]{:S(2)}, u32[]{:S(2)}) %collective-permute-start) | collective-permute-done | bytes 159776 | tf_op jit(solution)/shard_map/ppermute | solution.py:222
  8.9 1.7 %collective-permute-done.1.c2_ref = bf16[104,768]{1,0:T(8,128)(2,1)S(1)} collective-permute-done((bf16[104,768]{1,0:T(8,128)(2,1)S(1)}, bf16[104,768]{1,0:T(8,128)(2,1)S(1)}, u32[]{:S(2)}, u32[]{:S(2)}) %collective-permute-start.1) | collective-permute-done | bytes 159776 | tf_op jit(solution)/shard_map/ppermute | solution.py:222
  10.6 2.9 %collective-permute-done.2.c3_ref = bf16[104,768]{1,0:T(8,128)(2,1)S(1)} collective-permute-done((bf16[104,768]{1,0:T(8,128)(2,1)S(1)}, bf16[104,768]{1,0:T(8,128)(2,1)S(1)}, u32[]{:S(2)}, u32[]{:S(2)}) %collective-permute-start.2) | collective-permute-done | bytes 159776 | tf_op jit(solution)/shard_map/ppermute | solution.py:222
  13.7 1.6 %collective-permute-start.8 = (bf16[392,768]{1,0:T(8,128)(2,1)S(1)}, bf16[392,768]{1,0:T(8,128)(2,1)S(1)}, u32[]{:S(2)}, u32[]{:S(2)}) collective-permute-start(bf16[392,768]{1,0:T(8,128)(2,1)S(1)} %join.1.refs_2_.refs_3_.refs_0_), channel_id=1, source_target_pairs={{24,0},{9,1},{26,2},{11,3},{28,4},{13,5},{30,6},{15,7},{0,8},{17,9... | collective-permute-start | bytes 1806344 | tf_op jit(solution)/shard_map/ppermute | solution.py:222
  15.3 1.9 %collective-permute-start.7 = (bf16[392,768]{1,0:T(8,128)(2,1)S(1)}, bf16[392,768]{1,0:T(8,128)(2,1)S(1)}, u32[]{:S(2)}, u32[]{:S(2)}) collective-permute-start(bf16[392,768]{1,0:T(8,128)(2,1)S(1)} %join.1.refs_2_.refs_3_.refs_0_), channel_id=1, source_target_pairs={{6,0},{3,1},{0,2},{5,3},{2,4},{7,5},{4,6},{1,7},{14,8},{11,9},{8,1... | collective-permute-start | bytes 1806344 | tf_op jit(solution)/shard_map/ppermute | solution.py:222
  17.2 1.6 %collective-permute-start.5 = (bf16[392,768]{1,0:T(8,128)(2,1)S(1)}, bf16[392,768]{1,0:T(8,128)(2,1)S(1)}, u32[]{:S(2)}, u32[]{:S(2)}) collective-permute-start(bf16[392,768]{1,0:T(8,128)(2,1)S(1)} %collective-permute-done.3.refs_4_), channel_id=1, source_target_pairs={{24,0},{9,1},{26,2},{11,3},{28,4},{13,5},{30,6},{15,7},{0,8},{17,9... | collective-permute-start | bytes 1806344 | tf_op jit(solution)/shard_map/ppermute | solution.py:222
  18.8 1.9 %collective-permute-start.4 = (bf16[392,768]{1,0:T(8,128)(2,1)S(1)}, bf16[392,768]{1,0:T(8,128)(2,1)S(1)}, u32[]{:S(2)}, u32[]{:S(2)}) collective-permute-start(bf16[392,768]{1,0:T(8,128)(2,1)S(1)} %collective-permute-done.3.refs_4_), channel_id=1, source_target_pairs={{6,0},{3,1},{0,2},{5,3},{2,4},{7,5},{4,6},{1,7},{14,8},{11,9},{8,1... | collective-permute-start | bytes 1806344 | tf_op jit(solution)/shard_map/ppermute | solution.py:222
  20.7 4.2 %collective-permute-done.8.refs_5_ = bf16[392,768]{1,0:T(8,128)(2,1)S(1)} collective-permute-done((bf16[392,768]{1,0:T(8,128)(2,1)S(1)}, bf16[392,768]{1,0:T(8,128)(2,1)S(1)}, u32[]{:S(2)}, u32[]{:S(2)}) %collective-permute-start.8) | collective-permute-done | bytes 602144 | tf_op jit(solution)/shard_map/ppermute | solution.py:222
  25.0 2.4 %collective-permute-done.7.refs_0_ = bf16[392,768]{1,0:T(8,128)(2,1)S(1)} collective-permute-done((bf16[392,768]{1,0:T(8,128)(2,1)S(1)}, bf16[392,768]{1,0:T(8,128)(2,1)S(1)}, u32[]{:S(2)}, u32[]{:S(2)}) %collective-permute-start.7) | collective-permute-done | bytes 602144 | tf_op jit(solution)/shard_map/ppermute | solution.py:222
  27.6 1.3 %collective-permute-start.9 = (bf16[392,768]{1,0:T(8,128)(2,1)S(1)}, bf16[392,768]{1,0:T(8,128)(2,1)S(1)}, u32[]{:S(2)}, u32[]{:S(2)}) collective-permute-start(bf16[392,768]{1,0:T(8,128)(2,1)S(1)} %collective-permute-done.8.refs_5_), channel_id=1, source_target_pairs={{24,0},{9,1},{26,2},{11,3},{28,4},{13,5},{30,6},{15,7},{0,8},{17,9... | collective-permute-start | bytes 1806344 | tf_op jit(solution)/shard_map/ppermute | solution.py:222
  28.9 2.5 %collective-permute-done.5.refs_7_.refs_1_ = bf16[392,768]{1,0:T(8,128)(2,1)S(1)} collective-permute-done((bf16[392,768]{1,0:T(8,128)(2,1)S(1)}, bf16[392,768]{1,0:T(8,128)(2,1)S(1)}, u32[]{:S(2)}, u32[]{:S(2)}) %collective-permute-start.5) | collective-permute-done | bytes 602144 | tf_op jit(solution)/shard_map/ppermute | solution.py:222
  31.4 2.4 %collective-permute-done.4.refs_1_ = bf16[392,768]{1,0:T(8,128)(2,1)S(1)} collective-permute-done((bf16[392,768]{1,0:T(8,128)(2,1)S(1)}, bf16[392,768]{1,0:T(8,128)(2,1)S(1)}, u32[]{:S(2)}, u32[]{:S(2)}) %collective-permute-start.4) | collective-permute-done | bytes 602144 | tf_op jit(solution)/shard_map/ppermute | solution.py:222
  34.1 3.6 %pairs_a.1 = f32[3,1,384]{2,1,0:T(1,128)S(1)} custom-call(bf16[392,768]{1,0:T(8,128)(2,1)S(1)} %collective-permute-done.7.refs_0_, bf16[392,768]{1,0:T(8,128)(2,1)S(1)} %collective-permute-done.4.refs_1_, bf16[392,768]{1,0:T(8,128)(2,1)S(1)} %join.1.refs_2_.refs_3_.refs_0_, bf16[392,768]{1,0:T(8,128)(2,1)S(1)} %join.1.refs_2_.refs_3_.refs_0_, ...), custom_call_target="tpu_custom_call" | custom-call | flops 3170893824 | bytes 4718592 | tf_op jit(solution)/shard_map/pairs_a/pallas_call | solution.py:173
  38.8 1.2 %pairs_b.1 = f32[2,1,384]{2,1,0:T(1,128)S(1)} custom-call(bf16[392,768]{1,0:T(8,128)(2,1)S(1)} %collective-permute-done.7.refs_0_, bf16[392,768]{1,0:T(8,128)(2,1)S(1)} %collective-permute-done.4.refs_1_, bf16[392,768]{1,0:T(8,128)(2,1)S(1)} %collective-permute-done.6.refs_2_.refs_8_, bf16[392,768]{1,0:T(8,128)(2,1)S(1)} %collective-permute-done.9.refs_3_.refs_9_), custom_call_target="tpu_custom_call" | custom-call | flops 905969664 | bytes 2359296 | tf_op jit(solution)/shard_map/pairs_b/pallas_call | solution.py:173
  40.9 2.6 %pairs_f.1 = f32[3,1,384]{2,1,0:T(1,128)S(1)} custom-call(bf16[392,768]{1,0:T(8,128)(2,1)S(1)} %collective-permute-done.7.refs_0_, bf16[392,768]{1,0:T(8,128)(2,1)S(1)} %collective-permute-done.4.refs_1_, bf16[392,768]{1,0:T(8,128)(2,1)S(1)} %collective-permute-done.12.refs_2_, bf16[392,768]{1,0:T(8,128)(2,1)S(1)} %join.1.refs_2_.refs_3_.refs_0_, ...), custom_call_target="tpu_custom_call" | custom-call | flops 2264924160 | bytes 6488064 | tf_op jit(solution)/shard_map/pairs_f/pallas_call | solution.py:173
  43.5 3.9 %collective-permute-start.14 = (f32[1,384]{1,0:T(1,128)S(1)}, f32[1,384]{1,0:T(1,128)S(1)}, u32[]{:S(2)}, u32[]{:S(2)}) collective-permute-start(f32[1,384]{1,0:T(1,128)S(1)} %get-tuple-element.27), channel_id=1, source_target_pairs={{2,0},{7,1},{4,2},{1,3},{6,4},{3,5},{0,6},{5,7},{10,8},{15,9},{12,... | collective-permute-start | bytes 4616 | tf_op jit(solution)/shard_map/ppermute | solution.py:222
  48.2 1.3 %pairs_own.1 = f32[1,1,384]{2,1,0:T(1,128)S(1)} custom-call(bf16[392,768]{1,0:T(8,128)(2,1)S(1)} %join.1.refs_2_.refs_3_.refs_0_, bf16[392,768]{1,0:T(8,128)(2,1)S(1)} %collective-permute-done.5.refs_7_.refs_1_, bf16[392,768]{1,0:T(8,128)(2,1)S(1)} %collective-permute-done.6.refs_2_.refs_8_, bf16[392,768]{1,0:T(8,128)(2,1)S(1)} %collective-permute-done.9.refs_3_.refs_9_, ...), custom_call_target="tpu_custom_call" | custom-call | flops 905969664 | bytes 2949120 | tf_op jit(solution)/shard_map/pairs_own/pallas_call | solution.py:173
  49.5 2.2 %collective-permute-done.15 = f32[1,384]{1,0:T(1,128)S(1)} collective-permute-done((f32[1,384]{1,0:T(1,128)S(1)}, f32[1,384]{1,0:T(1,128)S(1)}, u32[]{:S(2)}, u32[]{:S(2)}) %collective-permute-start.15) | collective-permute-done | bytes 1568 | tf_op jit(solution)/shard_map/ppermute | solution.py:222
  53.5 2.0 %collective-permute-start.17 = (f32[1,384]{1,0:T(1,128)S(1)}, f32[1,384]{1,0:T(1,128)S(1)}, u32[]{:S(2)}, u32[]{:S(2)}) collective-permute-start(f32[1,384]{1,0:T(1,128)S(1)} %fusion.3.m0_ref), channel_id=1, source_target_pairs={{96,0},{97,1},{98,2},{99,3},{100,4},{101,5},{102,6},{103,7},{104,8... | collective-permute-start | bytes 4616 | tf_op jit(solution)/shard_map/ppermute | solution.py:222
  55.5 1.2 %collective-permute-start.16 = (f32[1,384]{1,0:T(1,128)S(1)}, f32[1,384]{1,0:T(1,128)S(1)}, u32[]{:S(2)}, u32[]{:S(2)}) collective-permute-start(f32[1,384]{1,0:T(1,128)S(1)} %fusion.3.m0_ref), channel_id=1, source_target_pairs={{32,0},{33,1},{34,2},{35,3},{36,4},{37,5},{38,6},{39,7},{40,8},{41... | collective-permute-start | bytes 4616 | tf_op jit(solution)/shard_map/ppermute | solution.py:222
  (23 shorter events, 8.2 us)
Async XLA Ops:
  1.9 7.0 %collective-permute-start = (bf16[104,768]{1,0:T(8,128)(2,1)S(1)}, bf16[104,768]{1,0:T(8,128)(2,1)S(1)}, u32[]{:S(2)}, u32[]{:S(2)}) collective-permute-start(bf16[104,768]{1,0:T(8,128)(2,1)S(1)} %get-tuple-element.18), channel_id=1, source_target_pairs={{96,0},{97,1},{98,2},{99,3},{100,4},{101,5},{102,6},{103,7},{104,8... | collective-permute-start | bytes 479240 | tf_op jit(solution)/shard_map/ppermute | solution.py:222
  3.5 7.0 %collective-permute-start.1 = (bf16[104,768]{1,0:T(8,128)(2,1)S(1)}, bf16[104,768]{1,0:T(8,128)(2,1)S(1)}, u32[]{:S(2)}, u32[]{:S(2)}) collective-permute-start(bf16[104,768]{1,0:T(8,128)(2,1)S(1)} %get-tuple-element.19), channel_id=1, source_target_pairs={{32,0},{33,1},{34,2},{35,3},{36,4},{37,5},{38,6},{39,7},{40,8},{41... | collective-permute-start | bytes 479240 | tf_op jit(solution)/shard_map/ppermute | solution.py:222
  5.2 8.3 %collective-permute-start.2 = (bf16[104,768]{1,0:T(8,128)(2,1)S(1)}, bf16[104,768]{1,0:T(8,128)(2,1)S(1)}, u32[]{:S(2)}, u32[]{:S(2)}) collective-permute-start(bf16[104,768]{1,0:T(8,128)(2,1)S(1)} %get-tuple-element.20), channel_id=1, source_target_pairs={{64,0},{65,1},{66,2},{67,3},{68,4},{69,5},{70,6},{71,7},{72,8},{73... | collective-permute-start | bytes 479240 | tf_op jit(solution)/shard_map/ppermute | solution.py:222
  13.6 3.7 %collective-permute-start.3 = (bf16[392,768]{1,0:T(8,128)(2,1)S(1)}, bf16[392,768]{1,0:T(8,128)(2,1)S(1)}, u32[]{:S(2)}, u32[]{:S(2)}) collective-permute-start(bf16[392,768]{1,0:T(8,128)(2,1)S(1)} %join.1.refs_2_.refs_3_.refs_0_), channel_id=1, source_target_pairs={{1,0},{0,1},{3,2},{2,3},{5,4},{4,5},{7,6},{6,7},{9,8},{8,9},{11,10... | collective-permute-start | bytes 1806344 | tf_op jit(solution)/shard_map/ppermute | solution.py:222
  13.7 11.3 %collective-permute-start.8 = (bf16[392,768]{1,0:T(8,128)(2,1)S(1)}, bf16[392,768]{1,0:T(8,128)(2,1)S(1)}, u32[]{:S(2)}, u32[]{:S(2)}) collective-permute-start(bf16[392,768]{1,0:T(8,128)(2,1)S(1)} %join.1.refs_2_.refs_3_.refs_0_), channel_id=1, source_target_pairs={{24,0},{9,1},{26,2},{11,3},{28,4},{13,5},{30,6},{15,7},{0,8},{17,9... | collective-permute-start | bytes 1806344 | tf_op jit(solution)/shard_map/ppermute | solution.py:222
  15.3 12.0 %collective-permute-start.7 = (bf16[392,768]{1,0:T(8,128)(2,1)S(1)}, bf16[392,768]{1,0:T(8,128)(2,1)S(1)}, u32[]{:S(2)}, u32[]{:S(2)}) collective-permute-start(bf16[392,768]{1,0:T(8,128)(2,1)S(1)} %join.1.refs_2_.refs_3_.refs_0_), channel_id=1, source_target_pairs={{6,0},{3,1},{0,2},{5,3},{2,4},{7,5},{4,6},{1,7},{14,8},{11,9},{8,1... | collective-permute-start | bytes 1806344 | tf_op jit(solution)/shard_map/ppermute | solution.py:222
  17.2 14.2 %collective-permute-start.5 = (bf16[392,768]{1,0:T(8,128)(2,1)S(1)}, bf16[392,768]{1,0:T(8,128)(2,1)S(1)}, u32[]{:S(2)}, u32[]{:S(2)}) collective-permute-start(bf16[392,768]{1,0:T(8,128)(2,1)S(1)} %collective-permute-done.3.refs_4_), channel_id=1, source_target_pairs={{24,0},{9,1},{26,2},{11,3},{28,4},{13,5},{30,6},{15,7},{0,8},{17,9... | collective-permute-start | bytes 1806344 | tf_op jit(solution)/shard_map/ppermute | solution.py:222
  18.8 15.0 %collective-permute-start.4 = (bf16[392,768]{1,0:T(8,128)(2,1)S(1)}, bf16[392,768]{1,0:T(8,128)(2,1)S(1)}, u32[]{:S(2)}, u32[]{:S(2)}) collective-permute-start(bf16[392,768]{1,0:T(8,128)(2,1)S(1)} %collective-permute-done.3.refs_4_), channel_id=1, source_target_pairs={{6,0},{3,1},{0,2},{5,3},{2,4},{7,5},{4,6},{1,7},{14,8},{11,9},{8,1... | collective-permute-start | bytes 1806344 | tf_op jit(solution)/shard_map/ppermute | solution.py:222
  27.3 6.7 %collective-permute-start.10 = (bf16[392,768]{1,0:T(8,128)(2,1)S(1)}, bf16[392,768]{1,0:T(8,128)(2,1)S(1)}, u32[]{:S(2)}, u32[]{:S(2)}) collective-permute-start(bf16[392,768]{1,0:T(8,128)(2,1)S(1)} %collective-permute-done.8.refs_5_), channel_id=1, source_target_pairs={{1,0},{0,1},{3,2},{2,3},{5,4},{4,5},{7,6},{6,7},{9,8},{8,9},{11,10... | collective-permute-start | bytes 1806344 | tf_op jit(solution)/shard_map/ppermute | solution.py:222
  27.6 11.2 %collective-permute-start.9 = (bf16[392,768]{1,0:T(8,128)(2,1)S(1)}, bf16[392,768]{1,0:T(8,128)(2,1)S(1)}, u32[]{:S(2)}, u32[]{:S(2)}) collective-permute-start(bf16[392,768]{1,0:T(8,128)(2,1)S(1)} %collective-permute-done.8.refs_5_), channel_id=1, source_target_pairs={{24,0},{9,1},{26,2},{11,3},{28,4},{13,5},{30,6},{15,7},{0,8},{17,9... | collective-permute-start | bytes 1806344 | tf_op jit(solution)/shard_map/ppermute | solution.py:222
  28.9 11.3 %collective-permute-start.12 = (bf16[392,768]{1,0:T(8,128)(2,1)S(1)}, bf16[392,768]{1,0:T(8,128)(2,1)S(1)}, u32[]{:S(2)}, u32[]{:S(2)}) collective-permute-start(bf16[392,768]{1,0:T(8,128)(2,1)S(1)} %collective-permute-done.7.refs_0_), channel_id=1, source_target_pairs={{6,0},{3,1},{0,2},{5,3},{2,4},{7,5},{4,6},{1,7},{14,8},{11,9},{8,1... | collective-permute-start | bytes 1806344 | tf_op jit(solution)/shard_map/ppermute | solution.py:222
  33.8 5.1 %collective-permute-start.6 = (bf16[392,768]{1,0:T(8,128)(2,1)S(1)}, bf16[392,768]{1,0:T(8,128)(2,1)S(1)}, u32[]{:S(2)}, u32[]{:S(2)}) collective-permute-start(bf16[392,768]{1,0:T(8,128)(2,1)S(1)} %collective-permute-done.5.refs_7_.refs_1_), channel_id=1, source_target_pairs={{1,0},{0,1},{3,2},{2,3},{5,4},{4,5},{7,6},{6,7},{9,8},{8,9},{11,10... | collective-permute-start | bytes 1806344 | tf_op jit(solution)/shard_map/ppermute | solution.py:222
  38.8 2.0 %collective-permute-start.11 = (bf16[392,768]{1,0:T(8,128)(2,1)S(1)}, bf16[392,768]{1,0:T(8,128)(2,1)S(1)}, u32[]{:S(2)}, u32[]{:S(2)}) collective-permute-start(bf16[392,768]{1,0:T(8,128)(2,1)S(1)} %collective-permute-done.9.refs_3_.refs_9_), channel_id=1, source_target_pairs={{1,0},{0,1},{3,2},{2,3},{5,4},{4,5},{7,6},{6,7},{9,8},{8,9},{11,10... | collective-permute-start | bytes 1806344 | tf_op jit(solution)/shard_map/ppermute | solution.py:222
  43.5 5.9 %collective-permute-start.14 = (f32[1,384]{1,0:T(1,128)S(1)}, f32[1,384]{1,0:T(1,128)S(1)}, u32[]{:S(2)}, u32[]{:S(2)}) collective-permute-start(f32[1,384]{1,0:T(1,128)S(1)} %get-tuple-element.27), channel_id=1, source_target_pairs={{2,0},{7,1},{4,2},{1,3},{6,4},{3,5},{0,6},{5,7},{10,8},{15,9},{12,... | collective-permute-start | bytes 4616 | tf_op jit(solution)/shard_map/ppermute | solution.py:222
  47.5 4.2 %collective-permute-start.15 = (f32[1,384]{1,0:T(1,128)S(1)}, f32[1,384]{1,0:T(1,128)S(1)}, u32[]{:S(2)}, u32[]{:S(2)}) collective-permute-start(f32[1,384]{1,0:T(1,128)S(1)} %get-tuple-element.28), channel_id=1, source_target_pairs={{7,0},{2,1},{1,2},{4,3},{3,4},{6,5},{5,6},{0,7},{15,8},{10,9},{9,1... | collective-permute-start | bytes 4616 | tf_op jit(solution)/shard_map/ppermute | solution.py:222
  47.5 5.1 %collective-permute-start.13 = (f32[1,384]{1,0:T(1,128)S(1)}, f32[1,384]{1,0:T(1,128)S(1)}, u32[]{:S(2)}, u32[]{:S(2)}) collective-permute-start(f32[1,384]{1,0:T(1,128)S(1)} %get-tuple-element.29), channel_id=1, source_target_pairs={{4,0},{5,1},{6,2},{7,3},{0,4},{1,5},{2,6},{3,7},{12,8},{13,9},{14,... | collective-permute-start | bytes 4616 | tf_op jit(solution)/shard_map/ppermute | solution.py:222
  52.6 5.2 %collective-permute-start.18 = (f32[1,384]{1,0:T(1,128)S(1)}, f32[1,384]{1,0:T(1,128)S(1)}, u32[]{:S(2)}, u32[]{:S(2)}) collective-permute-start(f32[1,384]{1,0:T(1,128)S(1)} %fusion.3.m0_ref), channel_id=1, source_target_pairs={{64,0},{65,1},{66,2},{67,3},{68,4},{69,5},{70,6},{71,7},{72,8},{73... | collective-permute-start | bytes 4616 | tf_op jit(solution)/shard_map/ppermute | solution.py:222
  53.5 4.8 %collective-permute-start.17 = (f32[1,384]{1,0:T(1,128)S(1)}, f32[1,384]{1,0:T(1,128)S(1)}, u32[]{:S(2)}, u32[]{:S(2)}) collective-permute-start(f32[1,384]{1,0:T(1,128)S(1)} %fusion.3.m0_ref), channel_id=1, source_target_pairs={{96,0},{97,1},{98,2},{99,3},{100,4},{101,5},{102,6},{103,7},{104,8... | collective-permute-start | bytes 4616 | tf_op jit(solution)/shard_map/ppermute | solution.py:222
  55.5 3.6 %collective-permute-start.16 = (f32[1,384]{1,0:T(1,128)S(1)}, f32[1,384]{1,0:T(1,128)S(1)}, u32[]{:S(2)}, u32[]{:S(2)}) collective-permute-start(f32[1,384]{1,0:T(1,128)S(1)} %fusion.3.m0_ref), channel_id=1, source_target_pairs={{32,0},{33,1},{34,2},{35,3},{36,4},{37,5},{38,6},{39,7},{40,8},{41... | collective-permute-start | bytes 4616 | tf_op jit(solution)/shard_map/ppermute | solution.py:222

commit v4 on v3

--- a/solution.py
+++ b/solution.py
@@ -247,7 +247,7 @@
             chunks[k] = receive(chunks[k], lambda x, y, z, c, step=step: (x - step, y, z, c))
     own = join(chunks)
 
-    az, ay = lax.optimization_barrier((near_z(own), near_y(own)))
+    az, ay = near_z(own), near_y(own)
     other = swap(own)
     fz, fy = near_z(az), near_y(ay)
     bz, by = lax.optimization_barrier((near_z(other), near_y(other)))

time: 59.9 us -> 59.3 us (0.990)
  transfers between devices with their start and end apart: 19 -> 19, of which waited for: 15 -> 14; matrix products, arithmetic and copies ran while one was open for 0% -> 0% of each run, Pallas kernels for 10% -> 10%
where the time goes in v4:
time: 59.3 us; the launch traced here: 59.1 us
  waiting for transfers between devices  25.1 us (42%)
  starting transfers between devices  22.5 us (38%)
  Pallas kernels  11.4 us (19%)
    ppermute x19, waiting for transfers between devices, receive(): return lax.ppermute(array, AXES, pairs_of(source_of))  25.1 us
    ppermute x19, starting transfers between devices, receive(): return lax.ppermute(array, AXES, pairs_of(source_of))  22.5 us
    pallas_call x4, Pallas kernels, pair_sums(): pl.pallas_call(functools.partial(pairs_kernel, nq, nk, plan), out_shape=j...  8.74 us
    pallas_call x1, Pallas kernels, prepare(): pl.pallas_call(prepare_kernel, out_shape=[chunk] * GROUPS + [jax.ShapeDty...  1.88 us
  transfers between devices with their start and end apart: 19, of which 14 were waited for; matrix products, arithmetic and copies ran while one was open for 0% of the time, Pallas kernels for 10%

profile of v4, /device:TPU:0, one launch (start us, length us, event | category | flops | bytes accessed | tf_op | source)
XLA Modules:
  0.0 59.1 jit_solution(14928517725700629946)
XLA Ops:
  0.0 1.9 %prepare.1 = (bf16[104,768]{1,0:T(8,128)(2,1)S(1)}, bf16[104,768]{1,0:T(8,128)(2,1)S(1)}, bf16[104,768]{1,0:T(8,128)(2,1)S(1)}, bf16[104,768]{1,0:T(8,128)(2,1)S(1)}, f32[1,384]{1,0:T(1,128)S(1)}) custom-call(s32[1]{0:T(128)} %bitcast.x_ref, bf16[384,768]{1,0:T(8,128)(2,1)} %emb_hbm.1, s32[384]{0:T(512)} %ids_hbm.1), custom_call_target="tpu_custom_call" | custom-call | tf_op jit(solution)/shard_map/prepare/pallas_call | solution.py:73
  1.9 1.6 %collective-permute-start = (bf16[104,768]{1,0:T(8,128)(2,1)S(1)}, bf16[104,768]{1,0:T(8,128)(2,1)S(1)}, u32[]{:S(2)}, u32[]{:S(2)}) collective-permute-start(bf16[104,768]{1,0:T(8,128)(2,1)S(1)} %get-tuple-element.16), channel_id=1, source_target_pairs={{96,0},{97,1},{98,2},{99,3},{100,4},{101,5},{102,6},{103,7},{104,8... | collective-permute-start | bytes 479240 | tf_op jit(solution)/shard_map/ppermute | solution.py:222
  3.5 1.7 %collective-permute-start.1 = (bf16[104,768]{1,0:T(8,128)(2,1)S(1)}, bf16[104,768]{1,0:T(8,128)(2,1)S(1)}, u32[]{:S(2)}, u32[]{:S(2)}) collective-permute-start(bf16[104,768]{1,0:T(8,128)(2,1)S(1)} %get-tuple-element.17), channel_id=1, source_target_pairs={{32,0},{33,1},{34,2},{35,3},{36,4},{37,5},{38,6},{39,7},{40,8},{41... | collective-permute-start | bytes 479240 | tf_op jit(solution)/shard_map/ppermute | solution.py:222
  5.2 1.9 %collective-permute-start.2 = (bf16[104,768]{1,0:T(8,128)(2,1)S(1)}, bf16[104,768]{1,0:T(8,128)(2,1)S(1)}, u32[]{:S(2)}, u32[]{:S(2)}) collective-permute-start(bf16[104,768]{1,0:T(8,128)(2,1)S(1)} %get-tuple-element.18), channel_id=1, source_target_pairs={{64,0},{65,1},{66,2},{67,3},{68,4},{69,5},{70,6},{71,7},{72,8},{73... | collective-permute-start | bytes 479240 | tf_op jit(solution)/shard_map/ppermute | solution.py:222
  7.1 1.8 %collective-permute-done.c1_ref = bf16[104,768]{1,0:T(8,128)(2,1)S(1)} collective-permute-done((bf16[104,768]{1,0:T(8,128)(2,1)S(1)}, bf16[104,768]{1,0:T(8,128)(2,1)S(1)}, u32[]{:S(2)}, u32[]{:S(2)}) %collective-permute-start) | collective-permute-done | bytes 159776 | tf_op jit(solution)/shard_map/ppermute | solution.py:222
  8.9 1.7 %collective-permute-done.1.c2_ref = bf16[104,768]{1,0:T(8,128)(2,1)S(1)} collective-permute-done((bf16[104,768]{1,0:T(8,128)(2,1)S(1)}, bf16[104,768]{1,0:T(8,128)(2,1)S(1)}, u32[]{:S(2)}, u32[]{:S(2)}) %collective-permute-start.1) | collective-permute-done | bytes 159776 | tf_op jit(solution)/shard_map/ppermute | solution.py:222
  10.6 2.9 %collective-permute-done.2.c3_ref = bf16[104,768]{1,0:T(8,128)(2,1)S(1)} collective-permute-done((bf16[104,768]{1,0:T(8,128)(2,1)S(1)}, bf16[104,768]{1,0:T(8,128)(2,1)S(1)}, u32[]{:S(2)}, u32[]{:S(2)}) %collective-permute-start.2) | collective-permute-done | bytes 159776 | tf_op jit(solution)/shard_map/ppermute | solution.py:222
  13.7 1.6 %collective-permute-start.7 = (bf16[392,768]{1,0:T(8,128)(2,1)S(1)}, bf16[392,768]{1,0:T(8,128)(2,1)S(1)}, u32[]{:S(2)}, u32[]{:S(2)}) collective-permute-start(bf16[392,768]{1,0:T(8,128)(2,1)S(1)} %join.1.refs_2_.refs_3_.refs_0_), channel_id=1, source_target_pairs={{24,0},{9,1},{26,2},{11,3},{28,4},{13,5},{30,6},{15,7},{0,8},{17,9... | collective-permute-start | bytes 1806344 | tf_op jit(solution)/shard_map/ppermute | solution.py:222
  15.3 1.9 %collective-permute-start.9 = (bf16[392,768]{1,0:T(8,128)(2,1)S(1)}, bf16[392,768]{1,0:T(8,128)(2,1)S(1)}, u32[]{:S(2)}, u32[]{:S(2)}) collective-permute-start(bf16[392,768]{1,0:T(8,128)(2,1)S(1)} %join.1.refs_2_.refs_3_.refs_0_), channel_id=1, source_target_pairs={{6,0},{3,1},{0,2},{5,3},{2,4},{7,5},{4,6},{1,7},{14,8},{11,9},{8,1... | collective-permute-start | bytes 1806344 | tf_op jit(solution)/shard_map/ppermute | solution.py:222
  17.2 1.6 %collective-permute-start.5 = (bf16[392,768]{1,0:T(8,128)(2,1)S(1)}, bf16[392,768]{1,0:T(8,128)(2,1)S(1)}, u32[]{:S(2)}, u32[]{:S(2)}) collective-permute-start(bf16[392,768]{1,0:T(8,128)(2,1)S(1)} %collective-permute-done.3.refs_4_), channel_id=1, source_target_pairs={{24,0},{9,1},{26,2},{11,3},{28,4},{13,5},{30,6},{15,7},{0,8},{17,9... | collective-permute-start | bytes 1806344 | tf_op jit(solution)/shard_map/ppermute | solution.py:222
  18.8 1.9 %collective-permute-start.4 = (bf16[392,768]{1,0:T(8,128)(2,1)S(1)}, bf16[392,768]{1,0:T(8,128)(2,1)S(1)}, u32[]{:S(2)}, u32[]{:S(2)}) collective-permute-start(bf16[392,768]{1,0:T(8,128)(2,1)S(1)} %collective-permute-done.3.refs_4_), channel_id=1, source_target_pairs={{6,0},{3,1},{0,2},{5,3},{2,4},{7,5},{4,6},{1,7},{14,8},{11,9},{8,1... | collective-permute-start | bytes 1806344 | tf_op jit(solution)/shard_map/ppermute | solution.py:222
  20.7 4.2 %collective-permute-done.7.refs_5_ = bf16[392,768]{1,0:T(8,128)(2,1)S(1)} collective-permute-done((bf16[392,768]{1,0:T(8,128)(2,1)S(1)}, bf16[392,768]{1,0:T(8,128)(2,1)S(1)}, u32[]{:S(2)}, u32[]{:S(2)}) %collective-permute-start.7) | collective-permute-done | bytes 602144 | tf_op jit(solution)/shard_map/ppermute | solution.py:222
  25.3 2.0 %collective-permute-done.9.refs_0_ = bf16[392,768]{1,0:T(8,128)(2,1)S(1)} collective-permute-done((bf16[392,768]{1,0:T(8,128)(2,1)S(1)}, bf16[392,768]{1,0:T(8,128)(2,1)S(1)}, u32[]{:S(2)}, u32[]{:S(2)}) %collective-permute-start.9) | collective-permute-done | bytes 602144 | tf_op jit(solution)/shard_map/ppermute | solution.py:222
  27.3 4.1 %collective-permute-done.5.refs_7_.refs_1_ = bf16[392,768]{1,0:T(8,128)(2,1)S(1)} collective-permute-done((bf16[392,768]{1,0:T(8,128)(2,1)S(1)}, bf16[392,768]{1,0:T(8,128)(2,1)S(1)}, u32[]{:S(2)}, u32[]{:S(2)}) %collective-permute-start.5) | collective-permute-done | bytes 602144 | tf_op jit(solution)/shard_map/ppermute | solution.py:222
  31.4 2.4 %collective-permute-done.4.refs_1_ = bf16[392,768]{1,0:T(8,128)(2,1)S(1)} collective-permute-done((bf16[392,768]{1,0:T(8,128)(2,1)S(1)}, bf16[392,768]{1,0:T(8,128)(2,1)S(1)}, u32[]{:S(2)}, u32[]{:S(2)}) %collective-permute-start.4) | collective-permute-done | bytes 602144 | tf_op jit(solution)/shard_map/ppermute | solution.py:222
  34.1 3.6 %pairs_a.1 = f32[3,1,384]{2,1,0:T(1,128)S(1)} custom-call(bf16[392,768]{1,0:T(8,128)(2,1)S(1)} %collective-permute-done.9.refs_0_, bf16[392,768]{1,0:T(8,128)(2,1)S(1)} %collective-permute-done.4.refs_1_, bf16[392,768]{1,0:T(8,128)(2,1)S(1)} %join.1.refs_2_.refs_3_.refs_0_, bf16[392,768]{1,0:T(8,128)(2,1)S(1)} %join.1.refs_2_.refs_3_.refs_0_, ...), custom_call_target="tpu_custom_call" | custom-call | flops 3170893824 | bytes 4718592 | tf_op jit(solution)/shard_map/pairs_a/pallas_call | solution.py:173
  38.0 1.2 %pairs_b.1 = f32[2,1,384]{2,1,0:T(1,128)S(1)} custom-call(bf16[392,768]{1,0:T(8,128)(2,1)S(1)} %collective-permute-done.9.refs_0_, bf16[392,768]{1,0:T(8,128)(2,1)S(1)} %collective-permute-done.4.refs_1_, bf16[392,768]{1,0:T(8,128)(2,1)S(1)} %collective-permute-done.6.refs_2_.refs_8_, bf16[392,768]{1,0:T(8,128)(2,1)S(1)} %collective-permute-done.8.refs_3_.refs_9_), custom_call_target="tpu_custom_call" | custom-call | flops 905969664 | bytes 2359296 | tf_op jit(solution)/shard_map/pairs_b/pallas_call | solution.py:173
  40.2 2.6 %pairs_f.1 = f32[3,1,384]{2,1,0:T(1,128)S(1)} custom-call(bf16[392,768]{1,0:T(8,128)(2,1)S(1)} %collective-permute-done.9.refs_0_, bf16[392,768]{1,0:T(8,128)(2,1)S(1)} %collective-permute-done.4.refs_1_, bf16[392,768]{1,0:T(8,128)(2,1)S(1)} %collective-permute-done.12.refs_2_, bf16[392,768]{1,0:T(8,128)(2,1)S(1)} %join.1.refs_2_.refs_3_.refs_0_, ...), custom_call_target="tpu_custom_call" | custom-call | flops 2264924160 | bytes 6488064 | tf_op jit(solution)/shard_map/pairs_f/pallas_call | solution.py:173
  42.9 3.9 %collective-permute-start.14 = (f32[1,384]{1,0:T(1,128)S(1)}, f32[1,384]{1,0:T(1,128)S(1)}, u32[]{:S(2)}, u32[]{:S(2)}) collective-permute-start(f32[1,384]{1,0:T(1,128)S(1)} %get-tuple-element.23), channel_id=1, source_target_pairs={{2,0},{7,1},{4,2},{1,3},{6,4},{3,5},{0,6},{5,7},{10,8},{15,9},{12,... | collective-permute-start | bytes 4616 | tf_op jit(solution)/shard_map/ppermute | solution.py:222
  46.8 1.3 %collective-permute-start.13 = (f32[1,384]{1,0:T(1,128)S(1)}, f32[1,384]{1,0:T(1,128)S(1)}, u32[]{:S(2)}, u32[]{:S(2)}) collective-permute-start(f32[1,384]{1,0:T(1,128)S(1)} %get-tuple-element.25), channel_id=1, source_target_pairs={{4,0},{5,1},{6,2},{7,3},{0,4},{1,5},{2,6},{3,7},{12,8},{13,9},{14,... | collective-permute-start | bytes 4616 | tf_op jit(solution)/shard_map/ppermute | solution.py:222
  48.2 1.3 %pairs_own.1 = f32[1,1,384]{2,1,0:T(1,128)S(1)} custom-call(bf16[392,768]{1,0:T(8,128)(2,1)S(1)} %join.1.refs_2_.refs_3_.refs_0_, bf16[392,768]{1,0:T(8,128)(2,1)S(1)} %collective-permute-done.5.refs_7_.refs_1_, bf16[392,768]{1,0:T(8,128)(2,1)S(1)} %collective-permute-done.6.refs_2_.refs_8_, bf16[392,768]{1,0:T(8,128)(2,1)S(1)} %collective-permute-done.8.refs_3_.refs_9_, ...), custom_call_target="tpu_custom_call" | custom-call | flops 905969664 | bytes 2949120 | tf_op jit(solution)/shard_map/pairs_own/pallas_call | solution.py:173
  49.5 1.6 %collective-permute-done.15 = f32[1,384]{1,0:T(1,128)S(1)} collective-permute-done((f32[1,384]{1,0:T(1,128)S(1)}, f32[1,384]{1,0:T(1,128)S(1)}, u32[]{:S(2)}, u32[]{:S(2)}) %collective-permute-start.15) | collective-permute-done | bytes 1568 | tf_op jit(solution)/shard_map/ppermute | solution.py:222
  52.8 2.0 %collective-permute-start.17 = (f32[1,384]{1,0:T(1,128)S(1)}, f32[1,384]{1,0:T(1,128)S(1)}, u32[]{:S(2)}, u32[]{:S(2)}) collective-permute-start(f32[1,384]{1,0:T(1,128)S(1)} %fusion.3.m0_ref), channel_id=1, source_target_pairs={{96,0},{97,1},{98,2},{99,3},{100,4},{101,5},{102,6},{103,7},{104,8... | collective-permute-start | bytes 4616 | tf_op jit(solution)/shard_map/ppermute | solution.py:222
  54.8 1.2 %collective-permute-start.16 = (f32[1,384]{1,0:T(1,128)S(1)}, f32[1,384]{1,0:T(1,128)S(1)}, u32[]{:S(2)}, u32[]{:S(2)}) collective-permute-start(f32[1,384]{1,0:T(1,128)S(1)} %fusion.3.m0_ref), channel_id=1, source_target_pairs={{32,0},{33,1},{34,2},{35,3},{36,4},{37,5},{38,6},{39,7},{40,8},{41... | collective-permute-start | bytes 4616 | tf_op jit(solution)/shard_map/ppermute | solution.py:222
  (23 shorter events, 7.0 us)
Async XLA Ops:
  1.9 7.0 %collective-permute-start = (bf16[104,768]{1,0:T(8,128)(2,1)S(1)}, bf16[104,768]{1,0:T(8,128)(2,1)S(1)}, u32[]{:S(2)}, u32[]{:S(2)}) collective-permute-start(bf16[104,768]{1,0:T(8,128)(2,1)S(1)} %get-tuple-element.16), channel_id=1, source_target_pairs={{96,0},{97,1},{98,2},{99,3},{100,4},{101,5},{102,6},{103,7},{104,8... | collective-permute-start | bytes 479240 | tf_op jit(solution)/shard_map/ppermute | solution.py:222
  3.5 7.0 %collective-permute-start.1 = (bf16[104,768]{1,0:T(8,128)(2,1)S(1)}, bf16[104,768]{1,0:T(8,128)(2,1)S(1)}, u32[]{:S(2)}, u32[]{:S(2)}) collective-permute-start(bf16[104,768]{1,0:T(8,128)(2,1)S(1)} %get-tuple-element.17), channel_id=1, source_target_pairs={{32,0},{33,1},{34,2},{35,3},{36,4},{37,5},{38,6},{39,7},{40,8},{41... | collective-permute-start | bytes 479240 | tf_op jit(solution)/shard_map/ppermute | solution.py:222
  5.2 8.3 %collective-permute-start.2 = (bf16[104,768]{1,0:T(8,128)(2,1)S(1)}, bf16[104,768]{1,0:T(8,128)(2,1)S(1)}, u32[]{:S(2)}, u32[]{:S(2)}) collective-permute-start(bf16[104,768]{1,0:T(8,128)(2,1)S(1)} %get-tuple-element.18), channel_id=1, source_target_pairs={{64,0},{65,1},{66,2},{67,3},{68,4},{69,5},{70,6},{71,7},{72,8},{73... | collective-permute-start | bytes 479240 | tf_op jit(solution)/shard_map/ppermute | solution.py:222
  13.6 3.7 %collective-permute-start.3 = (bf16[392,768]{1,0:T(8,128)(2,1)S(1)}, bf16[392,768]{1,0:T(8,128)(2,1)S(1)}, u32[]{:S(2)}, u32[]{:S(2)}) collective-permute-start(bf16[392,768]{1,0:T(8,128)(2,1)S(1)} %join.1.refs_2_.refs_3_.refs_0_), channel_id=1, source_target_pairs={{1,0},{0,1},{3,2},{2,3},{5,4},{4,5},{7,6},{6,7},{9,8},{8,9},{11,10... | collective-permute-start | bytes 1806344 | tf_op jit(solution)/shard_map/ppermute | solution.py:222
  13.7 11.3 %collective-permute-start.7 = (bf16[392,768]{1,0:T(8,128)(2,1)S(1)}, bf16[392,768]{1,0:T(8,128)(2,1)S(1)}, u32[]{:S(2)}, u32[]{:S(2)}) collective-permute-start(bf16[392,768]{1,0:T(8,128)(2,1)S(1)} %join.1.refs_2_.refs_3_.refs_0_), channel_id=1, source_target_pairs={{24,0},{9,1},{26,2},{11,3},{28,4},{13,5},{30,6},{15,7},{0,8},{17,9... | collective-permute-start | bytes 1806344 | tf_op jit(solution)/shard_map/ppermute | solution.py:222
  15.3 12.0 %collective-permute-start.9 = (bf16[392,768]{1,0:T(8,128)(2,1)S(1)}, bf16[392,768]{1,0:T(8,128)(2,1)S(1)}, u32[]{:S(2)}, u32[]{:S(2)}) collective-permute-start(bf16[392,768]{1,0:T(8,128)(2,1)S(1)} %join.1.refs_2_.refs_3_.refs_0_), channel_id=1, source_target_pairs={{6,0},{3,1},{0,2},{5,3},{2,4},{7,5},{4,6},{1,7},{14,8},{11,9},{8,1... | collective-permute-start | bytes 1806344 | tf_op jit(solution)/shard_map/ppermute | solution.py:222
  17.2 14.2 %collective-permute-start.5 = (bf16[392,768]{1,0:T(8,128)(2,1)S(1)}, bf16[392,768]{1,0:T(8,128)(2,1)S(1)}, u32[]{:S(2)}, u32[]{:S(2)}) collective-permute-start(bf16[392,768]{1,0:T(8,128)(2,1)S(1)} %collective-permute-done.3.refs_4_), channel_id=1, source_target_pairs={{24,0},{9,1},{26,2},{11,3},{28,4},{13,5},{30,6},{15,7},{0,8},{17,9... | collective-permute-start | bytes 1806344 | tf_op jit(solution)/shard_map/ppermute | solution.py:222
  18.8 15.0 %collective-permute-start.4 = (bf16[392,768]{1,0:T(8,128)(2,1)S(1)}, bf16[392,768]{1,0:T(8,128)(2,1)S(1)}, u32[]{:S(2)}, u32[]{:S(2)}) collective-permute-start(bf16[392,768]{1,0:T(8,128)(2,1)S(1)} %collective-permute-done.3.refs_4_), channel_id=1, source_target_pairs={{6,0},{3,1},{0,2},{5,3},{2,4},{7,5},{4,6},{1,7},{14,8},{11,9},{8,1... | collective-permute-start | bytes 1806344 | tf_op jit(solution)/shard_map/ppermute | solution.py:222
  25.0 9.1 %collective-permute-start.10 = (bf16[392,768]{1,0:T(8,128)(2,1)S(1)}, bf16[392,768]{1,0:T(8,128)(2,1)S(1)}, u32[]{:S(2)}, u32[]{:S(2)}) collective-permute-start(bf16[392,768]{1,0:T(8,128)(2,1)S(1)} %collective-permute-done.7.refs_5_), channel_id=1, source_target_pairs={{1,0},{0,1},{3,2},{2,3},{5,4},{4,5},{7,6},{6,7},{9,8},{8,9},{11,10... | collective-permute-start | bytes 1806344 | tf_op jit(solution)/shard_map/ppermute | solution.py:222
  25.0 12.9 %collective-permute-start.8 = (bf16[392,768]{1,0:T(8,128)(2,1)S(1)}, bf16[392,768]{1,0:T(8,128)(2,1)S(1)}, u32[]{:S(2)}, u32[]{:S(2)}) collective-permute-start(bf16[392,768]{1,0:T(8,128)(2,1)S(1)} %collective-permute-done.7.refs_5_), channel_id=1, source_target_pairs={{24,0},{9,1},{26,2},{11,3},{28,4},{13,5},{30,6},{15,7},{0,8},{17,9... | collective-permute-start | bytes 1806344 | tf_op jit(solution)/shard_map/ppermute | solution.py:222
  27.3 12.9 %collective-permute-start.12 = (bf16[392,768]{1,0:T(8,128)(2,1)S(1)}, bf16[392,768]{1,0:T(8,128)(2,1)S(1)}, u32[]{:S(2)}, u32[]{:S(2)}) collective-permute-start(bf16[392,768]{1,0:T(8,128)(2,1)S(1)} %collective-permute-done.9.refs_0_), channel_id=1, source_target_pairs={{6,0},{3,1},{0,2},{5,3},{2,4},{7,5},{4,6},{1,7},{14,8},{11,9},{8,1... | collective-permute-start | bytes 1806344 | tf_op jit(solution)/shard_map/ppermute | solution.py:222
  33.8 4.2 %collective-permute-start.6 = (bf16[392,768]{1,0:T(8,128)(2,1)S(1)}, bf16[392,768]{1,0:T(8,128)(2,1)S(1)}, u32[]{:S(2)}, u32[]{:S(2)}) collective-permute-start(bf16[392,768]{1,0:T(8,128)(2,1)S(1)} %collective-permute-done.5.refs_7_.refs_1_), channel_id=1, source_target_pairs={{1,0},{0,1},{3,2},{2,3},{5,4},{4,5},{7,6},{6,7},{9,8},{8,9},{11,10... | collective-permute-start | bytes 1806344 | tf_op jit(solution)/shard_map/ppermute | solution.py:222
  37.9 2.4 %collective-permute-start.11 = (bf16[392,768]{1,0:T(8,128)(2,1)S(1)}, bf16[392,768]{1,0:T(8,128)(2,1)S(1)}, u32[]{:S(2)}, u32[]{:S(2)}) collective-permute-start(bf16[392,768]{1,0:T(8,128)(2,1)S(1)} %collective-permute-done.8.refs_3_.refs_9_), channel_id=1, source_target_pairs={{1,0},{0,1},{3,2},{2,3},{5,4},{4,5},{7,6},{6,7},{9,8},{8,9},{11,10... | collective-permute-start | bytes 1806344 | tf_op jit(solution)/shard_map/ppermute | solution.py:222
  42.9 6.6 %collective-permute-start.14 = (f32[1,384]{1,0:T(1,128)S(1)}, f32[1,384]{1,0:T(1,128)S(1)}, u32[]{:S(2)}, u32[]{:S(2)}) collective-permute-start(f32[1,384]{1,0:T(1,128)S(1)} %get-tuple-element.23), channel_id=1, source_target_pairs={{2,0},{7,1},{4,2},{1,3},{6,4},{3,5},{0,6},{5,7},{10,8},{15,9},{12,... | collective-permute-start | bytes 4616 | tf_op jit(solution)/shard_map/ppermute | solution.py:222
  46.8 4.2 %collective-permute-start.15 = (f32[1,384]{1,0:T(1,128)S(1)}, f32[1,384]{1,0:T(1,128)S(1)}, u32[]{:S(2)}, u32[]{:S(2)}) collective-permute-start(f32[1,384]{1,0:T(1,128)S(1)} %get-tuple-element.24), channel_id=1, source_target_pairs={{7,0},{2,1},{1,2},{4,3},{3,4},{6,5},{5,6},{0,7},{15,8},{10,9},{9,1... | collective-permute-start | bytes 4616 | tf_op jit(solution)/shard_map/ppermute | solution.py:222
  46.8 5.1 %collective-permute-start.13 = (f32[1,384]{1,0:T(1,128)S(1)}, f32[1,384]{1,0:T(1,128)S(1)}, u32[]{:S(2)}, u32[]{:S(2)}) collective-permute-start(f32[1,384]{1,0:T(1,128)S(1)} %get-tuple-element.25), channel_id=1, source_target_pairs={{4,0},{5,1},{6,2},{7,3},{0,4},{1,5},{2,6},{3,7},{12,8},{13,9},{14,... | collective-permute-start | bytes 4616 | tf_op jit(solution)/shard_map/ppermute | solution.py:222
  51.9 5.2 %collective-permute-start.18 = (f32[1,384]{1,0:T(1,128)S(1)}, f32[1,384]{1,0:T(1,128)S(1)}, u32[]{:S(2)}, u32[]{:S(2)}) collective-permute-start(f32[1,384]{1,0:T(1,128)S(1)} %fusion.3.m0_ref), channel_id=1, source_target_pairs={{64,0},{65,1},{66,2},{67,3},{68,4},{69,5},{70,6},{71,7},{72,8},{73... | collective-permute-start | bytes 4616 | tf_op jit(solution)/shard_map/ppermute | solution.py:222
  52.8 4.8 %collective-permute-start.17 = (f32[1,384]{1,0:T(1,128)S(1)}, f32[1,384]{1,0:T(1,128)S(1)}, u32[]{:S(2)}, u32[]{:S(2)}) collective-permute-start(f32[1,384]{1,0:T(1,128)S(1)} %fusion.3.m0_ref), channel_id=1, source_target_pairs={{96,0},{97,1},{98,2},{99,3},{100,4},{101,5},{102,6},{103,7},{104,8... | collective-permute-start | bytes 4616 | tf_op jit(solution)/shard_map/ppermute | solution.py:222
  54.8 3.6 %collective-permute-start.16 = (f32[1,384]{1,0:T(1,128)S(1)}, f32[1,384]{1,0:T(1,128)S(1)}, u32[]{:S(2)}, u32[]{:S(2)}) collective-permute-start(f32[1,384]{1,0:T(1,128)S(1)} %fusion.3.m0_ref), channel_id=1, source_target_pairs={{32,0},{33,1},{34,2},{35,3},{36,4},{37,5},{38,6},{39,7},{40,8},{41... | collective-permute-start | bytes 4616 | tf_op jit(solution)/shard_map/ppermute | solution.py:222

commit v5 on v4

--- a/solution.py
+++ b/solution.py
@@ -253,17 +253,9 @@
     bz, by = lax.optimization_barrier((near_z(other), near_y(other)))
     ay2, by2 = swap(ay), swap(by)
     s1 = pair_sums(
-        [az, bz, own],
+        [az, bz],
         [own, other, ay, ay2, by],
-        (
-            ((0, 1), (0,)),
-            ((0, 1), (1,)),
-            ((0, 1), (2,)),
-            ((0, 1), (3,)),
-            ((0, 1), (4,)),
-            ((2,), (0, 1), True),
-            ((2,), (2, 3)),
-        ),
+        (((0, 1), (0,)), ((0, 1), (1,)), ((0, 1), (2,)), ((0, 1), (3,)), ((0, 1), (4,))),
         name="pairs_a",
     )
     fy, s1 = lax.optimization_barrier((fy, s1))
@@ -275,13 +267,17 @@
         (((2,), (0, 1)), ((2,), (2, 3)), ((2,), (4, 5)), ((2,), (6, 7)), ((0, 1), (7,))),
         name="pairs_f",
     )
-    s0 = pair_sums([own], [by, by2, fy, fy2], (((0,), (0, 1)), ((0,), (2, 3))), name="pairs_own")
+    s0 = pair_sums(
+        [own],
+        [own, other, ay, ay2, by, by2, fy, fy2],
+        (((0,), (0, 1), True), ((0,), (2, 3)), ((0,), (4, 5)), ((0,), (6, 7))),
+        name="pairs_own",
+    )
     mass_a = s1[0] + s2[0] + s3[0]
     mass_b = s1[1] + s2[1] + s3[1]
     mass_f = s3[2]
     mass = (
         s0[0]
-        + s1[2]
         + receive(mass_f, lambda x, y, z, c: (x, y, z + 2, c))
         + receive(mass_a, lambda x, y, z, c: (x, y, z - side(c), c))
         + receive(mass_b, lambda x, y, z, c: (x, y, z + side(c), 1 - c))

time: 59.3 us -> 59 us (level)
  no operation moved by 1% of the time
where the time goes in v5:
time: 59 us; the launch traced here: 58.9 us
  waiting for transfers between devices  25.3 us (43%)
  starting transfers between devices  22.1 us (37%)
  Pallas kernels  11.4 us (19%)
    ppermute x19, waiting for transfers between devices, receive(): return lax.ppermute(array, AXES, pairs_of(source_of))  25.3 us
    ppermute x19, starting transfers between devices, receive(): return lax.ppermute(array, AXES, pairs_of(source_of))  22.1 us
    pallas_call x4, Pallas kernels, pair_sums(): pl.pallas_call(functools.partial(pairs_kernel, nq, nk, plan), out_shape=j...  8.77 us
    pallas_call x1, Pallas kernels, prepare(): pl.pallas_call(prepare_kernel, out_shape=[chunk] * GROUPS + [jax.ShapeDty...  1.88 us
  transfers between devices with their start and end apart: 19, of which 14 were waited for; matrix products, arithmetic and copies ran while one was open for 0% of the time, Pallas kernels for 10%

profile of v5, /device:TPU:0, one launch (start us, length us, event | category | flops | bytes accessed | tf_op | source)
XLA Modules:
  0.0 58.9 jit_solution(8943443286094764599)
XLA Ops:
  0.0 1.9 %prepare.1 = (bf16[104,768]{1,0:T(8,128)(2,1)S(1)}, bf16[104,768]{1,0:T(8,128)(2,1)S(1)}, bf16[104,768]{1,0:T(8,128)(2,1)S(1)}, bf16[104,768]{1,0:T(8,128)(2,1)S(1)}, f32[1,384]{1,0:T(1,128)S(1)}) custom-call(s32[1]{0:T(128)} %bitcast.x_ref, bf16[384,768]{1,0:T(8,128)(2,1)} %emb_hbm.1, s32[384]{0:T(512)} %ids_hbm.1), custom_call_target="tpu_custom_call" | custom-call | tf_op jit(solution)/shard_map/prepare/pallas_call | solution.py:73
  1.9 1.6 %collective-permute-start = (bf16[104,768]{1,0:T(8,128)(2,1)S(1)}, bf16[104,768]{1,0:T(8,128)(2,1)S(1)}, u32[]{:S(2)}, u32[]{:S(2)}) collective-permute-start(bf16[104,768]{1,0:T(8,128)(2,1)S(1)} %get-tuple-element.16), channel_id=1, source_target_pairs={{96,0},{97,1},{98,2},{99,3},{100,4},{101,5},{102,6},{103,7},{104,8... | collective-permute-start | bytes 479240 | tf_op jit(solution)/shard_map/ppermute | solution.py:222
  3.5 1.7 %collective-permute-start.1 = (bf16[104,768]{1,0:T(8,128)(2,1)S(1)}, bf16[104,768]{1,0:T(8,128)(2,1)S(1)}, u32[]{:S(2)}, u32[]{:S(2)}) collective-permute-start(bf16[104,768]{1,0:T(8,128)(2,1)S(1)} %get-tuple-element.17), channel_id=1, source_target_pairs={{32,0},{33,1},{34,2},{35,3},{36,4},{37,5},{38,6},{39,7},{40,8},{41... | collective-permute-start | bytes 479240 | tf_op jit(solution)/shard_map/ppermute | solution.py:222
  5.2 1.9 %collective-permute-start.2 = (bf16[104,768]{1,0:T(8,128)(2,1)S(1)}, bf16[104,768]{1,0:T(8,128)(2,1)S(1)}, u32[]{:S(2)}, u32[]{:S(2)}) collective-permute-start(bf16[104,768]{1,0:T(8,128)(2,1)S(1)} %get-tuple-element.18), channel_id=1, source_target_pairs={{64,0},{65,1},{66,2},{67,3},{68,4},{69,5},{70,6},{71,7},{72,8},{73... | collective-permute-start | bytes 479240 | tf_op jit(solution)/shard_map/ppermute | solution.py:222
  7.1 1.8 %collective-permute-done.c1_ref = bf16[104,768]{1,0:T(8,128)(2,1)S(1)} collective-permute-done((bf16[104,768]{1,0:T(8,128)(2,1)S(1)}, bf16[104,768]{1,0:T(8,128)(2,1)S(1)}, u32[]{:S(2)}, u32[]{:S(2)}) %collective-permute-start) | collective-permute-done | bytes 159776 | tf_op jit(solution)/shard_map/ppermute | solution.py:222
  8.9 1.7 %collective-permute-done.1.c2_ref = bf16[104,768]{1,0:T(8,128)(2,1)S(1)} collective-permute-done((bf16[104,768]{1,0:T(8,128)(2,1)S(1)}, bf16[104,768]{1,0:T(8,128)(2,1)S(1)}, u32[]{:S(2)}, u32[]{:S(2)}) %collective-permute-start.1) | collective-permute-done | bytes 159776 | tf_op jit(solution)/shard_map/ppermute | solution.py:222
  10.6 2.9 %collective-permute-done.2.c3_ref = bf16[104,768]{1,0:T(8,128)(2,1)S(1)} collective-permute-done((bf16[104,768]{1,0:T(8,128)(2,1)S(1)}, bf16[104,768]{1,0:T(8,128)(2,1)S(1)}, u32[]{:S(2)}, u32[]{:S(2)}) %collective-permute-start.2) | collective-permute-done | bytes 159776 | tf_op jit(solution)/shard_map/ppermute | solution.py:222
  13.7 1.6 %collective-permute-start.4 = (bf16[392,768]{1,0:T(8,128)(2,1)S(1)}, bf16[392,768]{1,0:T(8,128)(2,1)S(1)}, u32[]{:S(2)}, u32[]{:S(2)}) collective-permute-start(bf16[392,768]{1,0:T(8,128)(2,1)S(1)} %join.1.refs_2_.refs_0_.refs_1_.refs_3_), channel_id=1, source_target_pairs={{24,0},{9,1},{26,2},{11,3},{28,4},{13,5},{30,6},{15,7},{0,8},{17,9... | collective-permute-start | bytes 1806344 | tf_op jit(solution)/shard_map/ppermute | solution.py:222
  15.3 1.9 %collective-permute-start.10 = (bf16[392,768]{1,0:T(8,128)(2,1)S(1)}, bf16[392,768]{1,0:T(8,128)(2,1)S(1)}, u32[]{:S(2)}, u32[]{:S(2)}) collective-permute-start(bf16[392,768]{1,0:T(8,128)(2,1)S(1)} %join.1.refs_2_.refs_0_.refs_1_.refs_3_), channel_id=1, source_target_pairs={{6,0},{3,1},{0,2},{5,3},{2,4},{7,5},{4,6},{1,7},{14,8},{11,9},{8,1... | collective-permute-start | bytes 1806344 | tf_op jit(solution)/shard_map/ppermute | solution.py:222
  17.2 1.6 %collective-permute-start.7 = (bf16[392,768]{1,0:T(8,128)(2,1)S(1)}, bf16[392,768]{1,0:T(8,128)(2,1)S(1)}, u32[]{:S(2)}, u32[]{:S(2)}) collective-permute-start(bf16[392,768]{1,0:T(8,128)(2,1)S(1)} %collective-permute-done.3.refs_3_.refs_2_.refs_4_), channel_id=1, source_target_pairs={{24,0},{9,1},{26,2},{11,3},{28,4},{13,5},{30,6},{15,7},{0,8},{17,9... | collective-permute-start | bytes 1806344 | tf_op jit(solution)/shard_map/ppermute | solution.py:222
  18.8 1.9 %collective-permute-start.6 = (bf16[392,768]{1,0:T(8,128)(2,1)S(1)}, bf16[392,768]{1,0:T(8,128)(2,1)S(1)}, u32[]{:S(2)}, u32[]{:S(2)}) collective-permute-start(bf16[392,768]{1,0:T(8,128)(2,1)S(1)} %collective-permute-done.3.refs_3_.refs_2_.refs_4_), channel_id=1, source_target_pairs={{6,0},{3,1},{0,2},{5,3},{2,4},{7,5},{4,6},{1,7},{14,8},{11,9},{8,1... | collective-permute-start | bytes 1806344 | tf_op jit(solution)/shard_map/ppermute | solution.py:222
  20.7 4.2 %collective-permute-done.4.refs_4_.refs_3_.refs_5_ = bf16[392,768]{1,0:T(8,128)(2,1)S(1)} collective-permute-done((bf16[392,768]{1,0:T(8,128)(2,1)S(1)}, bf16[392,768]{1,0:T(8,128)(2,1)S(1)}, u32[]{:S(2)}, u32[]{:S(2)}) %collective-permute-start.4) | collective-permute-done | bytes 602144 | tf_op jit(solution)/shard_map/ppermute | solution.py:222
  25.3 2.0 %collective-permute-done.10.refs_0_ = bf16[392,768]{1,0:T(8,128)(2,1)S(1)} collective-permute-done((bf16[392,768]{1,0:T(8,128)(2,1)S(1)}, bf16[392,768]{1,0:T(8,128)(2,1)S(1)}, u32[]{:S(2)}, u32[]{:S(2)}) %collective-permute-start.10) | collective-permute-done | bytes 602144 | tf_op jit(solution)/shard_map/ppermute | solution.py:222
  27.3 4.1 %collective-permute-done.7.refs_6_.refs_5_.refs_7_ = bf16[392,768]{1,0:T(8,128)(2,1)S(1)} collective-permute-done((bf16[392,768]{1,0:T(8,128)(2,1)S(1)}, bf16[392,768]{1,0:T(8,128)(2,1)S(1)}, u32[]{:S(2)}, u32[]{:S(2)}) %collective-permute-start.7) | collective-permute-done | bytes 602144 | tf_op jit(solution)/shard_map/ppermute | solution.py:222
  31.4 2.4 %collective-permute-done.6.refs_1_ = bf16[392,768]{1,0:T(8,128)(2,1)S(1)} collective-permute-done((bf16[392,768]{1,0:T(8,128)(2,1)S(1)}, bf16[392,768]{1,0:T(8,128)(2,1)S(1)}, u32[]{:S(2)}, u32[]{:S(2)}) %collective-permute-start.6) | collective-permute-done | bytes 602144 | tf_op jit(solution)/shard_map/ppermute | solution.py:222
  34.1 2.6 %pairs_a.1 = f32[2,1,384]{2,1,0:T(1,128)S(1)} custom-call(bf16[392,768]{1,0:T(8,128)(2,1)S(1)} %collective-permute-done.10.refs_0_, bf16[392,768]{1,0:T(8,128)(2,1)S(1)} %collective-permute-done.6.refs_1_, bf16[392,768]{1,0:T(8,128)(2,1)S(1)} %join.1.refs_2_.refs_0_.refs_1_.refs_3_, bf16[392,768]{1,0:T(8,128)(2,1)S(1)} %collective-permute-done.3.refs_3_.refs_2_.refs_4_, ...), custom_call_target="tpu_custom_call" | custom-call | flops 2264924160 | bytes 4128768 | tf_op jit(solution)/shard_map/pairs_a/pallas_call | solution.py:173
  36.7 1.2 %collective-permute-done.9.refs_7_.refs_9_.refs_3_ = bf16[392,768]{1,0:T(8,128)(2,1)S(1)} collective-permute-done((bf16[392,768]{1,0:T(8,128)(2,1)S(1)}, bf16[392,768]{1,0:T(8,128)(2,1)S(1)}, u32[]{:S(2)}, u32[]{:S(2)}) %collective-permute-start.9) | collective-permute-done | bytes 602144 | tf_op jit(solution)/shard_map/ppermute | solution.py:222
  37.9 1.2 %pairs_b.1 = f32[2,1,384]{2,1,0:T(1,128)S(1)} custom-call(bf16[392,768]{1,0:T(8,128)(2,1)S(1)} %collective-permute-done.10.refs_0_, bf16[392,768]{1,0:T(8,128)(2,1)S(1)} %collective-permute-done.6.refs_1_, bf16[392,768]{1,0:T(8,128)(2,1)S(1)} %collective-permute-done.8.refs_6_.refs_8_.refs_2_, bf16[392,768]{1,0:T(8,128)(2,1)S(1)} %collective-permute-done.9.refs_7_.refs_9_.refs_3_), custom_call_target="tpu_custom_call" | custom-call | flops 905969664 | bytes 2359296 | tf_op jit(solution)/shard_map/pairs_b/pallas_call | solution.py:173
  40.2 2.7 %pairs_f.1 = f32[3,1,384]{2,1,0:T(1,128)S(1)} custom-call(bf16[392,768]{1,0:T(8,128)(2,1)S(1)} %collective-permute-done.10.refs_0_, bf16[392,768]{1,0:T(8,128)(2,1)S(1)} %collective-permute-done.6.refs_1_, bf16[392,768]{1,0:T(8,128)(2,1)S(1)} %collective-permute-done.12.refs_2_, bf16[392,768]{1,0:T(8,128)(2,1)S(1)} %join.1.refs_2_.refs_0_.refs_1_.refs_3_, ...), custom_call_target="tpu_custom_call" | custom-call | flops 2264924160 | bytes 6488064 | tf_op jit(solution)/shard_map/pairs_f/pallas_call | solution.py:173
  42.9 3.7 %collective-permute-start.14 = (f32[1,384]{1,0:T(1,128)S(1)}, f32[1,384]{1,0:T(1,128)S(1)}, u32[]{:S(2)}, u32[]{:S(2)}) collective-permute-start(f32[1,384]{1,0:T(1,128)S(1)} %get-tuple-element.23), channel_id=1, source_target_pairs={{2,0},{7,1},{4,2},{1,3},{6,4},{3,5},{0,6},{5,7},{10,8},{15,9},{12,... | collective-permute-start | bytes 4616 | tf_op jit(solution)/shard_map/ppermute | solution.py:222
  46.7 1.3 %collective-permute-start.13 = (f32[1,384]{1,0:T(1,128)S(1)}, f32[1,384]{1,0:T(1,128)S(1)}, u32[]{:S(2)}, u32[]{:S(2)}) collective-permute-start(f32[1,384]{1,0:T(1,128)S(1)} %get-tuple-element.25), channel_id=1, source_target_pairs={{4,0},{5,1},{6,2},{7,3},{0,4},{1,5},{2,6},{3,7},{12,8},{13,9},{14,... | collective-permute-start | bytes 4616 | tf_op jit(solution)/shard_map/ppermute | solution.py:222
  48.0 2.3 %pairs_own.1 = f32[1,1,384]{2,1,0:T(1,128)S(1)} custom-call(bf16[392,768]{1,0:T(8,128)(2,1)S(1)} %join.1.refs_2_.refs_0_.refs_1_.refs_3_, bf16[392,768]{1,0:T(8,128)(2,1)S(1)} %join.1.refs_2_.refs_0_.refs_1_.refs_3_, bf16[392,768]{1,0:T(8,128)(2,1)S(1)} %collective-permute-done.3.refs_3_.refs_2_.refs_4_, ...), custom_call_target="tpu_custom_call" | custom-call | flops 1811939328 | bytes 5308416 | tf_op jit(solution)/shard_map/pairs_own/pallas_call | solution.py:173
  52.6 2.0 %collective-permute-start.17 = (f32[1,384]{1,0:T(1,128)S(1)}, f32[1,384]{1,0:T(1,128)S(1)}, u32[]{:S(2)}, u32[]{:S(2)}) collective-permute-start(f32[1,384]{1,0:T(1,128)S(1)} %fusion.3.m0_ref), channel_id=1, source_target_pairs={{96,0},{97,1},{98,2},{99,3},{100,4},{101,5},{102,6},{103,7},{104,8... | collective-permute-start | bytes 4616 | tf_op jit(solution)/shard_map/ppermute | solution.py:222
  54.6 1.2 %collective-permute-start.16 = (f32[1,384]{1,0:T(1,128)S(1)}, f32[1,384]{1,0:T(1,128)S(1)}, u32[]{:S(2)}, u32[]{:S(2)}) collective-permute-start(f32[1,384]{1,0:T(1,128)S(1)} %fusion.3.m0_ref), channel_id=1, source_target_pairs={{32,0},{33,1},{34,2},{35,3},{36,4},{37,5},{38,6},{39,7},{40,8},{41... | collective-permute-start | bytes 4616 | tf_op jit(solution)/shard_map/ppermute | solution.py:222
  (23 shorter events, 7.3 us)
Async XLA Ops:
  1.9 7.0 %collective-permute-start = (bf16[104,768]{1,0:T(8,128)(2,1)S(1)}, bf16[104,768]{1,0:T(8,128)(2,1)S(1)}, u32[]{:S(2)}, u32[]{:S(2)}) collective-permute-start(bf16[104,768]{1,0:T(8,128)(2,1)S(1)} %get-tuple-element.16), channel_id=1, source_target_pairs={{96,0},{97,1},{98,2},{99,3},{100,4},{101,5},{102,6},{103,7},{104,8... | collective-permute-start | bytes 479240 | tf_op jit(solution)/shard_map/ppermute | solution.py:222
  3.5 7.0 %collective-permute-start.1 = (bf16[104,768]{1,0:T(8,128)(2,1)S(1)}, bf16[104,768]{1,0:T(8,128)(2,1)S(1)}, u32[]{:S(2)}, u32[]{:S(2)}) collective-permute-start(bf16[104,768]{1,0:T(8,128)(2,1)S(1)} %get-tuple-element.17), channel_id=1, source_target_pairs={{32,0},{33,1},{34,2},{35,3},{36,4},{37,5},{38,6},{39,7},{40,8},{41... | collective-permute-start | bytes 479240 | tf_op jit(solution)/shard_map/ppermute | solution.py:222
  5.2 8.3 %collective-permute-start.2 = (bf16[104,768]{1,0:T(8,128)(2,1)S(1)}, bf16[104,768]{1,0:T(8,128)(2,1)S(1)}, u32[]{:S(2)}, u32[]{:S(2)}) collective-permute-start(bf16[104,768]{1,0:T(8,128)(2,1)S(1)} %get-tuple-element.18), channel_id=1, source_target_pairs={{64,0},{65,1},{66,2},{67,3},{68,4},{69,5},{70,6},{71,7},{72,8},{73... | collective-permute-start | bytes 479240 | tf_op jit(solution)/shard_map/ppermute | solution.py:222
  13.6 3.7 %collective-permute-start.3 = (bf16[392,768]{1,0:T(8,128)(2,1)S(1)}, bf16[392,768]{1,0:T(8,128)(2,1)S(1)}, u32[]{:S(2)}, u32[]{:S(2)}) collective-permute-start(bf16[392,768]{1,0:T(8,128)(2,1)S(1)} %join.1.refs_2_.refs_0_.refs_1_.refs_3_), channel_id=1, source_target_pairs={{1,0},{0,1},{3,2},{2,3},{5,4},{4,5},{7,6},{6,7},{9,8},{8,9},{11,10... | collective-permute-start | bytes 1806344 | tf_op jit(solution)/shard_map/ppermute | solution.py:222
  13.7 11.3 %collective-permute-start.4 = (bf16[392,768]{1,0:T(8,128)(2,1)S(1)}, bf16[392,768]{1,0:T(8,128)(2,1)S(1)}, u32[]{:S(2)}, u32[]{:S(2)}) collective-permute-start(bf16[392,768]{1,0:T(8,128)(2,1)S(1)} %join.1.refs_2_.refs_0_.refs_1_.refs_3_), channel_id=1, source_target_pairs={{24,0},{9,1},{26,2},{11,3},{28,4},{13,5},{30,6},{15,7},{0,8},{17,9... | collective-permute-start | bytes 1806344 | tf_op jit(solution)/shard_map/ppermute | solution.py:222
  15.3 12.0 %collective-permute-start.10 = (bf16[392,768]{1,0:T(8,128)(2,1)S(1)}, bf16[392,768]{1,0:T(8,128)(2,1)S(1)}, u32[]{:S(2)}, u32[]{:S(2)}) collective-permute-start(bf16[392,768]{1,0:T(8,128)(2,1)S(1)} %join.1.refs_2_.refs_0_.refs_1_.refs_3_), channel_id=1, source_target_pairs={{6,0},{3,1},{0,2},{5,3},{2,4},{7,5},{4,6},{1,7},{14,8},{11,9},{8,1... | collective-permute-start | bytes 1806344 | tf_op jit(solution)/shard_map/ppermute | solution.py:222
  17.2 14.2 %collective-permute-start.7 = (bf16[392,768]{1,0:T(8,128)(2,1)S(1)}, bf16[392,768]{1,0:T(8,128)(2,1)S(1)}, u32[]{:S(2)}, u32[]{:S(2)}) collective-permute-start(bf16[392,768]{1,0:T(8,128)(2,1)S(1)} %collective-permute-done.3.refs_3_.refs_2_.refs_4_), channel_id=1, source_target_pairs={{24,0},{9,1},{26,2},{11,3},{28,4},{13,5},{30,6},{15,7},{0,8},{17,9... | collective-permute-start | bytes 1806344 | tf_op jit(solution)/shard_map/ppermute | solution.py:222
  18.8 15.0 %collective-permute-start.6 = (bf16[392,768]{1,0:T(8,128)(2,1)S(1)}, bf16[392,768]{1,0:T(8,128)(2,1)S(1)}, u32[]{:S(2)}, u32[]{:S(2)}) collective-permute-start(bf16[392,768]{1,0:T(8,128)(2,1)S(1)} %collective-permute-done.3.refs_3_.refs_2_.refs_4_), channel_id=1, source_target_pairs={{6,0},{3,1},{0,2},{5,3},{2,4},{7,5},{4,6},{1,7},{14,8},{11,9},{8,1... | collective-permute-start | bytes 1806344 | tf_op jit(solution)/shard_map/ppermute | solution.py:222
  25.0 9.1 %collective-permute-start.5 = (bf16[392,768]{1,0:T(8,128)(2,1)S(1)}, bf16[392,768]{1,0:T(8,128)(2,1)S(1)}, u32[]{:S(2)}, u32[]{:S(2)}) collective-permute-start(bf16[392,768]{1,0:T(8,128)(2,1)S(1)} %collective-permute-done.4.refs_4_.refs_3_.refs_5_), channel_id=1, source_target_pairs={{1,0},{0,1},{3,2},{2,3},{5,4},{4,5},{7,6},{6,7},{9,8},{8,9},{11,10... | collective-permute-start | bytes 1806344 | tf_op jit(solution)/shard_map/ppermute | solution.py:222
  25.0 12.9 %collective-permute-start.9 = (bf16[392,768]{1,0:T(8,128)(2,1)S(1)}, bf16[392,768]{1,0:T(8,128)(2,1)S(1)}, u32[]{:S(2)}, u32[]{:S(2)}) collective-permute-start(bf16[392,768]{1,0:T(8,128)(2,1)S(1)} %collective-permute-done.4.refs_4_.refs_3_.refs_5_), channel_id=1, source_target_pairs={{24,0},{9,1},{26,2},{11,3},{28,4},{13,5},{30,6},{15,7},{0,8},{17,9... | collective-permute-start | bytes 1806344 | tf_op jit(solution)/shard_map/ppermute | solution.py:222
  27.3 12.9 %collective-permute-start.12 = (bf16[392,768]{1,0:T(8,128)(2,1)S(1)}, bf16[392,768]{1,0:T(8,128)(2,1)S(1)}, u32[]{:S(2)}, u32[]{:S(2)}) collective-permute-start(bf16[392,768]{1,0:T(8,128)(2,1)S(1)} %collective-permute-done.10.refs_0_), channel_id=1, source_target_pairs={{6,0},{3,1},{0,2},{5,3},{2,4},{7,5},{4,6},{1,7},{14,8},{11,9},{8,1... | collective-permute-start | bytes 1806344 | tf_op jit(solution)/shard_map/ppermute | solution.py:222
  33.8 4.1 %collective-permute-start.8 = (bf16[392,768]{1,0:T(8,128)(2,1)S(1)}, bf16[392,768]{1,0:T(8,128)(2,1)S(1)}, u32[]{:S(2)}, u32[]{:S(2)}) collective-permute-start(bf16[392,768]{1,0:T(8,128)(2,1)S(1)} %collective-permute-done.7.refs_6_.refs_5_.refs_7_), channel_id=1, source_target_pairs={{1,0},{0,1},{3,2},{2,3},{5,4},{4,5},{7,6},{6,7},{9,8},{8,9},{11,10... | collective-permute-start | bytes 1806344 | tf_op jit(solution)/shard_map/ppermute | solution.py:222
  37.9 2.4 %collective-permute-start.11 = (bf16[392,768]{1,0:T(8,128)(2,1)S(1)}, bf16[392,768]{1,0:T(8,128)(2,1)S(1)}, u32[]{:S(2)}, u32[]{:S(2)}) collective-permute-start(bf16[392,768]{1,0:T(8,128)(2,1)S(1)} %collective-permute-done.9.refs_7_.refs_9_.refs_3_), channel_id=1, source_target_pairs={{1,0},{0,1},{3,2},{2,3},{5,4},{4,5},{7,6},{6,7},{9,8},{8,9},{11,10... | collective-permute-start | bytes 1806344 | tf_op jit(solution)/shard_map/ppermute | solution.py:222
  42.9 7.4 %collective-permute-start.14 = (f32[1,384]{1,0:T(1,128)S(1)}, f32[1,384]{1,0:T(1,128)S(1)}, u32[]{:S(2)}, u32[]{:S(2)}) collective-permute-start(f32[1,384]{1,0:T(1,128)S(1)} %get-tuple-element.23), channel_id=1, source_target_pairs={{2,0},{7,1},{4,2},{1,3},{6,4},{3,5},{0,6},{5,7},{10,8},{15,9},{12,... | collective-permute-start | bytes 4616 | tf_op jit(solution)/shard_map/ppermute | solution.py:222
  46.7 4.2 %collective-permute-start.15 = (f32[1,384]{1,0:T(1,128)S(1)}, f32[1,384]{1,0:T(1,128)S(1)}, u32[]{:S(2)}, u32[]{:S(2)}) collective-permute-start(f32[1,384]{1,0:T(1,128)S(1)} %get-tuple-element.24), channel_id=1, source_target_pairs={{7,0},{2,1},{1,2},{4,3},{3,4},{6,5},{5,6},{0,7},{15,8},{10,9},{9,1... | collective-permute-start | bytes 4616 | tf_op jit(solution)/shard_map/ppermute | solution.py:222
  46.7 5.1 %collective-permute-start.13 = (f32[1,384]{1,0:T(1,128)S(1)}, f32[1,384]{1,0:T(1,128)S(1)}, u32[]{:S(2)}, u32[]{:S(2)}) collective-permute-start(f32[1,384]{1,0:T(1,128)S(1)} %get-tuple-element.25), channel_id=1, source_target_pairs={{4,0},{5,1},{6,2},{7,3},{0,4},{1,5},{2,6},{3,7},{12,8},{13,9},{14,... | collective-permute-start | bytes 4616 | tf_op jit(solution)/shard_map/ppermute | solution.py:222
  51.8 5.1 %collective-permute-start.18 = (f32[1,384]{1,0:T(1,128)S(1)}, f32[1,384]{1,0:T(1,128)S(1)}, u32[]{:S(2)}, u32[]{:S(2)}) collective-permute-start(f32[1,384]{1,0:T(1,128)S(1)} %fusion.3.m0_ref), channel_id=1, source_target_pairs={{64,0},{65,1},{66,2},{67,3},{68,4},{69,5},{70,6},{71,7},{72,8},{73... | collective-permute-start | bytes 4616 | tf_op jit(solution)/shard_map/ppermute | solution.py:222
  52.6 4.8 %collective-permute-start.17 = (f32[1,384]{1,0:T(1,128)S(1)}, f32[1,384]{1,0:T(1,128)S(1)}, u32[]{:S(2)}, u32[]{:S(2)}) collective-permute-start(f32[1,384]{1,0:T(1,128)S(1)} %fusion.3.m0_ref), channel_id=1, source_target_pairs={{96,0},{97,1},{98,2},{99,3},{100,4},{101,5},{102,6},{103,7},{104,8... | collective-permute-start | bytes 4616 | tf_op jit(solution)/shard_map/ppermute | solution.py:222
  54.6 3.6 %collective-permute-start.16 = (f32[1,384]{1,0:T(1,128)S(1)}, f32[1,384]{1,0:T(1,128)S(1)}, u32[]{:S(2)}, u32[]{:S(2)}) collective-permute-start(f32[1,384]{1,0:T(1,128)S(1)} %fusion.3.m0_ref), channel_id=1, source_target_pairs={{32,0},{33,1},{34,2},{35,3},{36,4},{37,5},{38,6},{39,7},{40,8},{41... | collective-permute-start | bytes 4616 | tf_op jit(solution)/shard_map/ppermute | solution.py:222

commit v6 on v5

--- a/solution.py
+++ b/solution.py
@@ -273,15 +273,9 @@
         (((0,), (0, 1), True), ((0,), (2, 3)), ((0,), (4, 5)), ((0,), (6, 7))),
         name="pairs_own",
     )
-    mass_a = s1[0] + s2[0] + s3[0]
-    mass_b = s1[1] + s2[1] + s3[1]
-    mass_f = s3[2]
-    mass = (
-        s0[0]
-        + receive(mass_f, lambda x, y, z, c: (x, y, z + 2, c))
-        + receive(mass_a, lambda x, y, z, c: (x, y, z - side(c), c))
-        + receive(mass_b, lambda x, y, z, c: (x, y, z + side(c), 1 - c))
-    )
+    near = receive(s1 + s2 + s3[:2], lambda x, y, z, c: (x, y, z - side(c), c))
+    far = receive(s3[2], lambda x, y, z, c: (x, y, z + 2, c))
+    mass = s0[0] + near[0] + swap(near[1]) + far
     masses = [
         receive(mass, lambda x, y, z, c, step=step: (x + step, y, z, c)) if step else mass for step in STEPS
     ]

time: 59 us -> 59.1 us (level)
  waiting for transfers between devices: 25.3 us -> 26.6 us
  starting transfers between devices: 22.1 us -> 20.9 us
    ppermute x19, waiting for transfers between devices: 25.3 us -> 26.6 us  [receive(): return lax.ppermute(array, AXES, pairs_of(source_of))]
    ppermute x19, starting transfers between devices: 22.1 us -> 20.9 us  [receive(): return lax.ppermute(array, AXES, pairs_of(source_of))]
where the time goes in v6:
time: 59.1 us; the launch traced here: 59 us
  waiting for transfers between devices  26.6 us (45%)
  starting transfers between devices  20.9 us (35%)
  Pallas kernels  11.4 us (19%)
    ppermute x19, waiting for transfers between devices, receive(): return lax.ppermute(array, AXES, pairs_of(source_of))  26.6 us
    ppermute x19, starting transfers between devices, receive(): return lax.ppermute(array, AXES, pairs_of(source_of))  20.9 us
    pallas_call x4, Pallas kernels, pair_sums(): pl.pallas_call(functools.partial(pairs_kernel, nq, nk, plan), out_shape=j...  8.77 us
    pallas_call x1, Pallas kernels, prepare(): pl.pallas_call(prepare_kernel, out_shape=[chunk] * GROUPS + [jax.ShapeDty...  1.88 us
  transfers between devices with their start and end apart: 19, of which 14 were waited for; matrix products, arithmetic and copies ran while one was open for 0% of the time, Pallas kernels for 10%

profile of v6, /device:TPU:0, one launch (start us, length us, event | category | flops | bytes accessed | tf_op | source)
XLA Modules:
  0.0 59.0 jit_solution(10084841173847796733)
XLA Ops:
  0.0 1.9 %prepare.1 = (bf16[104,768]{1,0:T(8,128)(2,1)S(1)}, bf16[104,768]{1,0:T(8,128)(2,1)S(1)}, bf16[104,768]{1,0:T(8,128)(2,1)S(1)}, bf16[104,768]{1,0:T(8,128)(2,1)S(1)}, f32[1,384]{1,0:T(1,128)S(1)}) custom-call(s32[1]{0:T(128)} %bitcast.x_ref, bf16[384,768]{1,0:T(8,128)(2,1)} %emb_hbm.1, s32[384]{0:T(512)} %ids_hbm.1), custom_call_target="tpu_custom_call" | custom-call | tf_op jit(solution)/shard_map/prepare/pallas_call | solution.py:73
  1.9 1.6 %collective-permute-start = (bf16[104,768]{1,0:T(8,128)(2,1)S(1)}, bf16[104,768]{1,0:T(8,128)(2,1)S(1)}, u32[]{:S(2)}, u32[]{:S(2)}) collective-permute-start(bf16[104,768]{1,0:T(8,128)(2,1)S(1)} %get-tuple-element.16), channel_id=1, source_target_pairs={{96,0},{97,1},{98,2},{99,3},{100,4},{101,5},{102,6},{103,7},{104,8... | collective-permute-start | bytes 479240 | tf_op jit(solution)/shard_map/ppermute | solution.py:222
  3.5 1.7 %collective-permute-start.1 = (bf16[104,768]{1,0:T(8,128)(2,1)S(1)}, bf16[104,768]{1,0:T(8,128)(2,1)S(1)}, u32[]{:S(2)}, u32[]{:S(2)}) collective-permute-start(bf16[104,768]{1,0:T(8,128)(2,1)S(1)} %get-tuple-element.17), channel_id=1, source_target_pairs={{32,0},{33,1},{34,2},{35,3},{36,4},{37,5},{38,6},{39,7},{40,8},{41... | collective-permute-start | bytes 479240 | tf_op jit(solution)/shard_map/ppermute | solution.py:222
  5.2 1.9 %collective-permute-start.2 = (bf16[104,768]{1,0:T(8,128)(2,1)S(1)}, bf16[104,768]{1,0:T(8,128)(2,1)S(1)}, u32[]{:S(2)}, u32[]{:S(2)}) collective-permute-start(bf16[104,768]{1,0:T(8,128)(2,1)S(1)} %get-tuple-element.18), channel_id=1, source_target_pairs={{64,0},{65,1},{66,2},{67,3},{68,4},{69,5},{70,6},{71,7},{72,8},{73... | collective-permute-start | bytes 479240 | tf_op jit(solution)/shard_map/ppermute | solution.py:222
  7.1 1.8 %collective-permute-done.c1_ref = bf16[104,768]{1,0:T(8,128)(2,1)S(1)} collective-permute-done((bf16[104,768]{1,0:T(8,128)(2,1)S(1)}, bf16[104,768]{1,0:T(8,128)(2,1)S(1)}, u32[]{:S(2)}, u32[]{:S(2)}) %collective-permute-start) | collective-permute-done | bytes 159776 | tf_op jit(solution)/shard_map/ppermute | solution.py:222
  8.9 1.7 %collective-permute-done.1.c2_ref = bf16[104,768]{1,0:T(8,128)(2,1)S(1)} collective-permute-done((bf16[104,768]{1,0:T(8,128)(2,1)S(1)}, bf16[104,768]{1,0:T(8,128)(2,1)S(1)}, u32[]{:S(2)}, u32[]{:S(2)}) %collective-permute-start.1) | collective-permute-done | bytes 159776 | tf_op jit(solution)/shard_map/ppermute | solution.py:222
  10.6 2.9 %collective-permute-done.2.c3_ref = bf16[104,768]{1,0:T(8,128)(2,1)S(1)} collective-permute-done((bf16[104,768]{1,0:T(8,128)(2,1)S(1)}, bf16[104,768]{1,0:T(8,128)(2,1)S(1)}, u32[]{:S(2)}, u32[]{:S(2)}) %collective-permute-start.2) | collective-permute-done | bytes 159776 | tf_op jit(solution)/shard_map/ppermute | solution.py:222
  13.7 1.6 %collective-permute-start.4 = (bf16[392,768]{1,0:T(8,128)(2,1)S(1)}, bf16[392,768]{1,0:T(8,128)(2,1)S(1)}, u32[]{:S(2)}, u32[]{:S(2)}) collective-permute-start(bf16[392,768]{1,0:T(8,128)(2,1)S(1)} %join.1.refs_2_.refs_0_.refs_1_.refs_3_), channel_id=1, source_target_pairs={{24,0},{9,1},{26,2},{11,3},{28,4},{13,5},{30,6},{15,7},{0,8},{17,9... | collective-permute-start | bytes 1806344 | tf_op jit(solution)/shard_map/ppermute | solution.py:222
  15.3 1.9 %collective-permute-start.10 = (bf16[392,768]{1,0:T(8,128)(2,1)S(1)}, bf16[392,768]{1,0:T(8,128)(2,1)S(1)}, u32[]{:S(2)}, u32[]{:S(2)}) collective-permute-start(bf16[392,768]{1,0:T(8,128)(2,1)S(1)} %join.1.refs_2_.refs_0_.refs_1_.refs_3_), channel_id=1, source_target_pairs={{6,0},{3,1},{0,2},{5,3},{2,4},{7,5},{4,6},{1,7},{14,8},{11,9},{8,1... | collective-permute-start | bytes 1806344 | tf_op jit(solution)/shard_map/ppermute | solution.py:222
  17.2 1.6 %collective-permute-start.7 = (bf16[392,768]{1,0:T(8,128)(2,1)S(1)}, bf16[392,768]{1,0:T(8,128)(2,1)S(1)}, u32[]{:S(2)}, u32[]{:S(2)}) collective-permute-start(bf16[392,768]{1,0:T(8,128)(2,1)S(1)} %collective-permute-done.3.refs_3_.refs_2_.refs_4_), channel_id=1, source_target_pairs={{24,0},{9,1},{26,2},{11,3},{28,4},{13,5},{30,6},{15,7},{0,8},{17,9... | collective-permute-start | bytes 1806344 | tf_op jit(solution)/shard_map/ppermute | solution.py:222
  18.8 1.9 %collective-permute-start.6 = (bf16[392,768]{1,0:T(8,128)(2,1)S(1)}, bf16[392,768]{1,0:T(8,128)(2,1)S(1)}, u32[]{:S(2)}, u32[]{:S(2)}) collective-permute-start(bf16[392,768]{1,0:T(8,128)(2,1)S(1)} %collective-permute-done.3.refs_3_.refs_2_.refs_4_), channel_id=1, source_target_pairs={{6,0},{3,1},{0,2},{5,3},{2,4},{7,5},{4,6},{1,7},{14,8},{11,9},{8,1... | collective-permute-start | bytes 1806344 | tf_op jit(solution)/shard_map/ppermute | solution.py:222
  20.7 4.2 %collective-permute-done.4.refs_4_.refs_3_.refs_5_ = bf16[392,768]{1,0:T(8,128)(2,1)S(1)} collective-permute-done((bf16[392,768]{1,0:T(8,128)(2,1)S(1)}, bf16[392,768]{1,0:T(8,128)(2,1)S(1)}, u32[]{:S(2)}, u32[]{:S(2)}) %collective-permute-start.4) | collective-permute-done | bytes 602144 | tf_op jit(solution)/shard_map/ppermute | solution.py:222
  25.3 2.0 %collective-permute-done.10.refs_0_ = bf16[392,768]{1,0:T(8,128)(2,1)S(1)} collective-permute-done((bf16[392,768]{1,0:T(8,128)(2,1)S(1)}, bf16[392,768]{1,0:T(8,128)(2,1)S(1)}, u32[]{:S(2)}, u32[]{:S(2)}) %collective-permute-start.10) | collective-permute-done | bytes 602144 | tf_op jit(solution)/shard_map/ppermute | solution.py:222
  27.3 4.1 %collective-permute-done.7.refs_6_.refs_5_.refs_7_ = bf16[392,768]{1,0:T(8,128)(2,1)S(1)} collective-permute-done((bf16[392,768]{1,0:T(8,128)(2,1)S(1)}, bf16[392,768]{1,0:T(8,128)(2,1)S(1)}, u32[]{:S(2)}, u32[]{:S(2)}) %collective-permute-start.7) | collective-permute-done | bytes 602144 | tf_op jit(solution)/shard_map/ppermute | solution.py:222
  31.4 2.4 %collective-permute-done.6.refs_1_ = bf16[392,768]{1,0:T(8,128)(2,1)S(1)} collective-permute-done((bf16[392,768]{1,0:T(8,128)(2,1)S(1)}, bf16[392,768]{1,0:T(8,128)(2,1)S(1)}, u32[]{:S(2)}, u32[]{:S(2)}) %collective-permute-start.6) | collective-permute-done | bytes 602144 | tf_op jit(solution)/shard_map/ppermute | solution.py:222
  34.1 2.6 %pairs_a.1 = f32[2,1,384]{2,1,0:T(1,128)S(1)} custom-call(bf16[392,768]{1,0:T(8,128)(2,1)S(1)} %collective-permute-done.10.refs_0_, bf16[392,768]{1,0:T(8,128)(2,1)S(1)} %collective-permute-done.6.refs_1_, bf16[392,768]{1,0:T(8,128)(2,1)S(1)} %join.1.refs_2_.refs_0_.refs_1_.refs_3_, bf16[392,768]{1,0:T(8,128)(2,1)S(1)} %collective-permute-done.3.refs_3_.refs_2_.refs_4_, ...), custom_call_target="tpu_custom_call" | custom-call | flops 2264924160 | bytes 4128768 | tf_op jit(solution)/shard_map/pairs_a/pallas_call | solution.py:173
  37.9 1.2 %pairs_b.1 = f32[2,1,384]{2,1,0:T(1,128)S(1)} custom-call(bf16[392,768]{1,0:T(8,128)(2,1)S(1)} %collective-permute-done.10.refs_0_, bf16[392,768]{1,0:T(8,128)(2,1)S(1)} %collective-permute-done.6.refs_1_, bf16[392,768]{1,0:T(8,128)(2,1)S(1)} %collective-permute-done.8.refs_6_.refs_2_.refs_8_, bf16[392,768]{1,0:T(8,128)(2,1)S(1)} %collective-permute-done.9.refs_7_.refs_3_.refs_9_), custom_call_target="tpu_custom_call" | custom-call | flops 905969664 | bytes 2359296 | tf_op jit(solution)/shard_map/pairs_b/pallas_call | solution.py:173
  40.2 2.7 %pairs_f.1 = f32[3,1,384]{2,1,0:T(1,128)S(1)} custom-call(bf16[392,768]{1,0:T(8,128)(2,1)S(1)} %collective-permute-done.10.refs_0_, bf16[392,768]{1,0:T(8,128)(2,1)S(1)} %collective-permute-done.6.refs_1_, bf16[392,768]{1,0:T(8,128)(2,1)S(1)} %collective-permute-done.12.refs_2_, bf16[392,768]{1,0:T(8,128)(2,1)S(1)} %join.1.refs_2_.refs_0_.refs_1_.refs_3_, ...), custom_call_target="tpu_custom_call" | custom-call | flops 2264924160 | bytes 6488064 | tf_op jit(solution)/shard_map/pairs_f/pallas_call | solution.py:173
  42.9 3.7 %collective-permute-start.13 = (f32[2,1,384]{2,1,0:T(1,128)S(1)}, f32[2,1,384]{2,1,0:T(1,128)S(1)}, u32[]{:S(2)}, u32[]{:S(2)}) collective-permute-start(f32[2,1,384]{2,1,0:T(1,128)S(1)} %slice_add_fusion), channel_id=1, source_target_pairs={{2,0},{7,1},{4,2},{1,3},{6,4},{3,5},{0,6},{5,7},{10,8},{15,9},{12,... | collective-permute-start | bytes 9224 | tf_op jit(solution)/shard_map/ppermute | solution.py:222
  46.7 1.3 %collective-permute-done.13 = f32[2,1,384]{2,1,0:T(1,128)S(1)} collective-permute-done((f32[2,1,384]{2,1,0:T(1,128)S(1)}, f32[2,1,384]{2,1,0:T(1,128)S(1)}, u32[]{:S(2)}, u32[]{:S(2)}) %collective-permute-start.13) | collective-permute-done | bytes 3104 | tf_op jit(solution)/shard_map/ppermute | solution.py:222
  48.0 2.3 %pairs_own.1 = f32[1,1,384]{2,1,0:T(1,128)S(1)} custom-call(bf16[392,768]{1,0:T(8,128)(2,1)S(1)} %join.1.refs_2_.refs_0_.refs_1_.refs_3_, bf16[392,768]{1,0:T(8,128)(2,1)S(1)} %join.1.refs_2_.refs_0_.refs_1_.refs_3_, bf16[392,768]{1,0:T(8,128)(2,1)S(1)} %collective-permute-done.3.refs_3_.refs_2_.refs_4_, ...), custom_call_target="tpu_custom_call" | custom-call | flops 1811939328 | bytes 5308416 | tf_op jit(solution)/shard_map/pairs_own/pallas_call | solution.py:173
  50.3 1.5 %collective-permute-done.15 = f32[1,384]{1,0:T(1,128)S(1)} collective-permute-done((f32[1,384]{1,0:T(1,128)S(1)}, f32[1,384]{1,0:T(1,128)S(1)}, u32[]{:S(2)}, u32[]{:S(2)}) %collective-permute-start.15) | collective-permute-done | bytes 1568 | tf_op jit(solution)/shard_map/ppermute | solution.py:222
  52.7 2.0 %collective-permute-start.17 = (f32[1,384]{1,0:T(1,128)S(1)}, f32[1,384]{1,0:T(1,128)S(1)}, u32[]{:S(2)}, u32[]{:S(2)}) collective-permute-start(f32[1,384]{1,0:T(1,128)S(1)} %fusion.2.m0_ref), channel_id=1, source_target_pairs={{96,0},{97,1},{98,2},{99,3},{100,4},{101,5},{102,6},{103,7},{104,8... | collective-permute-start | bytes 4616 | tf_op jit(solution)/shard_map/ppermute | solution.py:222
  54.7 1.2 %collective-permute-start.16 = (f32[1,384]{1,0:T(1,128)S(1)}, f32[1,384]{1,0:T(1,128)S(1)}, u32[]{:S(2)}, u32[]{:S(2)}) collective-permute-start(f32[1,384]{1,0:T(1,128)S(1)} %fusion.2.m0_ref), channel_id=1, source_target_pairs={{32,0},{33,1},{34,2},{35,3},{36,4},{37,5},{38,6},{39,7},{40,8},{41... | collective-permute-start | bytes 4616 | tf_op jit(solution)/shard_map/ppermute | solution.py:222
  (25 shorter events, 7.1 us)
Async XLA Ops:
  1.9 7.0 %collective-permute-start = (bf16[104,768]{1,0:T(8,128)(2,1)S(1)}, bf16[104,768]{1,0:T(8,128)(2,1)S(1)}, u32[]{:S(2)}, u32[]{:S(2)}) collective-permute-start(bf16[104,768]{1,0:T(8,128)(2,1)S(1)} %get-tuple-element.16), channel_id=1, source_target_pairs={{96,0},{97,1},{98,2},{99,3},{100,4},{101,5},{102,6},{103,7},{104,8... | collective-permute-start | bytes 479240 | tf_op jit(solution)/shard_map/ppermute | solution.py:222
  3.5 7.0 %collective-permute-start.1 = (bf16[104,768]{1,0:T(8,128)(2,1)S(1)}, bf16[104,768]{1,0:T(8,128)(2,1)S(1)}, u32[]{:S(2)}, u32[]{:S(2)}) collective-permute-start(bf16[104,768]{1,0:T(8,128)(2,1)S(1)} %get-tuple-element.17), channel_id=1, source_target_pairs={{32,0},{33,1},{34,2},{35,3},{36,4},{37,5},{38,6},{39,7},{40,8},{41... | collective-permute-start | bytes 479240 | tf_op jit(solution)/shard_map/ppermute | solution.py:222
  5.2 8.3 %collective-permute-start.2 = (bf16[104,768]{1,0:T(8,128)(2,1)S(1)}, bf16[104,768]{1,0:T(8,128)(2,1)S(1)}, u32[]{:S(2)}, u32[]{:S(2)}) collective-permute-start(bf16[104,768]{1,0:T(8,128)(2,1)S(1)} %get-tuple-element.18), channel_id=1, source_target_pairs={{64,0},{65,1},{66,2},{67,3},{68,4},{69,5},{70,6},{71,7},{72,8},{73... | collective-permute-start | bytes 479240 | tf_op jit(solution)/shard_map/ppermute | solution.py:222
  13.6 3.7 %collective-permute-start.3 = (bf16[392,768]{1,0:T(8,128)(2,1)S(1)}, bf16[392,768]{1,0:T(8,128)(2,1)S(1)}, u32[]{:S(2)}, u32[]{:S(2)}) collective-permute-start(bf16[392,768]{1,0:T(8,128)(2,1)S(1)} %join.1.refs_2_.refs_0_.refs_1_.refs_3_), channel_id=1, source_target_pairs={{1,0},{0,1},{3,2},{2,3},{5,4},{4,5},{7,6},{6,7},{9,8},{8,9},{11,10... | collective-permute-start | bytes 1806344 | tf_op jit(solution)/shard_map/ppermute | solution.py:222
  13.7 11.3 %collective-permute-start.4 = (bf16[392,768]{1,0:T(8,128)(2,1)S(1)}, bf16[392,768]{1,0:T(8,128)(2,1)S(1)}, u32[]{:S(2)}, u32[]{:S(2)}) collective-permute-start(bf16[392,768]{1,0:T(8,128)(2,1)S(1)} %join.1.refs_2_.refs_0_.refs_1_.refs_3_), channel_id=1, source_target_pairs={{24,0},{9,1},{26,2},{11,3},{28,4},{13,5},{30,6},{15,7},{0,8},{17,9... | collective-permute-start | bytes 1806344 | tf_op jit(solution)/shard_map/ppermute | solution.py:222
  15.3 12.0 %collective-permute-start.10 = (bf16[392,768]{1,0:T(8,128)(2,1)S(1)}, bf16[392,768]{1,0:T(8,128)(2,1)S(1)}, u32[]{:S(2)}, u32[]{:S(2)}) collective-permute-start(bf16[392,768]{1,0:T(8,128)(2,1)S(1)} %join.1.refs_2_.refs_0_.refs_1_.refs_3_), channel_id=1, source_target_pairs={{6,0},{3,1},{0,2},{5,3},{2,4},{7,5},{4,6},{1,7},{14,8},{11,9},{8,1... | collective-permute-start | bytes 1806344 | tf_op jit(solution)/shard_map/ppermute | solution.py:222
  17.2 14.2 %collective-permute-start.7 = (bf16[392,768]{1,0:T(8,128)(2,1)S(1)}, bf16[392,768]{1,0:T(8,128)(2,1)S(1)}, u32[]{:S(2)}, u32[]{:S(2)}) collective-permute-start(bf16[392,768]{1,0:T(8,128)(2,1)S(1)} %collective-permute-done.3.refs_3_.refs_2_.refs_4_), channel_id=1, source_target_pairs={{24,0},{9,1},{26,2},{11,3},{28,4},{13,5},{30,6},{15,7},{0,8},{17,9... | collective-permute-start | bytes 1806344 | tf_op jit(solution)/shard_map/ppermute | solution.py:222
  18.8 15.0 %collective-permute-start.6 = (bf16[392,768]{1,0:T(8,128)(2,1)S(1)}, bf16[392,768]{1,0:T(8,128)(2,1)S(1)}, u32[]{:S(2)}, u32[]{:S(2)}) collective-permute-start(bf16[392,768]{1,0:T(8,128)(2,1)S(1)} %collective-permute-done.3.refs_3_.refs_2_.refs_4_), channel_id=1, source_target_pairs={{6,0},{3,1},{0,2},{5,3},{2,4},{7,5},{4,6},{1,7},{14,8},{11,9},{8,1... | collective-permute-start | bytes 1806344 | tf_op jit(solution)/shard_map/ppermute | solution.py:222
  25.0 9.1 %collective-permute-start.5 = (bf16[392,768]{1,0:T(8,128)(2,1)S(1)}, bf16[392,768]{1,0:T(8,128)(2,1)S(1)}, u32[]{:S(2)}, u32[]{:S(2)}) collective-permute-start(bf16[392,768]{1,0:T(8,128)(2,1)S(1)} %collective-permute-done.4.refs_4_.refs_3_.refs_5_), channel_id=1, source_target_pairs={{1,0},{0,1},{3,2},{2,3},{5,4},{4,5},{7,6},{6,7},{9,8},{8,9},{11,10... | collective-permute-start | bytes 1806344 | tf_op jit(solution)/shard_map/ppermute | solution.py:222
  25.0 12.9 %collective-permute-start.9 = (bf16[392,768]{1,0:T(8,128)(2,1)S(1)}, bf16[392,768]{1,0:T(8,128)(2,1)S(1)}, u32[]{:S(2)}, u32[]{:S(2)}) collective-permute-start(bf16[392,768]{1,0:T(8,128)(2,1)S(1)} %collective-permute-done.4.refs_4_.refs_3_.refs_5_), channel_id=1, source_target_pairs={{24,0},{9,1},{26,2},{11,3},{28,4},{13,5},{30,6},{15,7},{0,8},{17,9... | collective-permute-start | bytes 1806344 | tf_op jit(solution)/shard_map/ppermute | solution.py:222
  27.3 12.9 %collective-permute-start.12 = (bf16[392,768]{1,0:T(8,128)(2,1)S(1)}, bf16[392,768]{1,0:T(8,128)(2,1)S(1)}, u32[]{:S(2)}, u32[]{:S(2)}) collective-permute-start(bf16[392,768]{1,0:T(8,128)(2,1)S(1)} %collective-permute-done.10.refs_0_), channel_id=1, source_target_pairs={{6,0},{3,1},{0,2},{5,3},{2,4},{7,5},{4,6},{1,7},{14,8},{11,9},{8,1... | collective-permute-start | bytes 1806344 | tf_op jit(solution)/shard_map/ppermute | solution.py:222
  33.8 4.1 %collective-permute-start.8 = (bf16[392,768]{1,0:T(8,128)(2,1)S(1)}, bf16[392,768]{1,0:T(8,128)(2,1)S(1)}, u32[]{:S(2)}, u32[]{:S(2)}) collective-permute-start(bf16[392,768]{1,0:T(8,128)(2,1)S(1)} %collective-permute-done.7.refs_6_.refs_5_.refs_7_), channel_id=1, source_target_pairs={{1,0},{0,1},{3,2},{2,3},{5,4},{4,5},{7,6},{6,7},{9,8},{8,9},{11,10... | collective-permute-start | bytes 1806344 | tf_op jit(solution)/shard_map/ppermute | solution.py:222
  37.9 2.4 %collective-permute-start.11 = (bf16[392,768]{1,0:T(8,128)(2,1)S(1)}, bf16[392,768]{1,0:T(8,128)(2,1)S(1)}, u32[]{:S(2)}, u32[]{:S(2)}) collective-permute-start(bf16[392,768]{1,0:T(8,128)(2,1)S(1)} %collective-permute-done.9.refs_7_.refs_3_.refs_9_), channel_id=1, source_target_pairs={{1,0},{0,1},{3,2},{2,3},{5,4},{4,5},{7,6},{6,7},{9,8},{8,9},{11,10... | collective-permute-start | bytes 1806344 | tf_op jit(solution)/shard_map/ppermute | solution.py:222
  42.9 5.1 %collective-permute-start.13 = (f32[2,1,384]{2,1,0:T(1,128)S(1)}, f32[2,1,384]{2,1,0:T(1,128)S(1)}, u32[]{:S(2)}, u32[]{:S(2)}) collective-permute-start(f32[2,1,384]{2,1,0:T(1,128)S(1)} %slice_add_fusion), channel_id=1, source_target_pairs={{2,0},{7,1},{4,2},{1,3},{6,4},{3,5},{0,6},{5,7},{10,8},{15,9},{12,... | collective-permute-start | bytes 9224 | tf_op jit(solution)/shard_map/ppermute | solution.py:222
  46.7 5.1 %collective-permute-start.15 = (f32[1,384]{1,0:T(1,128)S(1)}, f32[1,384]{1,0:T(1,128)S(1)}, u32[]{:S(2)}, u32[]{:S(2)}) collective-permute-start(f32[1,384]{1,0:T(1,128)S(1)} %slice_bitcast_fusion), channel_id=1, source_target_pairs={{4,0},{5,1},{6,2},{7,3},{0,4},{1,5},{2,6},{3,7},{12,8},{13,9},{14,... | collective-permute-start | bytes 4616 | tf_op jit(solution)/shard_map/ppermute | solution.py:222
  48.0 3.8 %collective-permute-start.14 = (f32[1,384]{1,0:T(1,128)S(1)}, f32[1,384]{1,0:T(1,128)S(1)}, u32[]{:S(2)}, u32[]{:S(2)}) collective-permute-start(f32[1,384]{1,0:T(1,128)S(1)} %slice_bitcast_fusion.1), channel_id=1, source_target_pairs={{1,0},{0,1},{3,2},{2,3},{5,4},{4,5},{7,6},{6,7},{9,8},{8,9},{11,10... | collective-permute-start | bytes 4616 | tf_op jit(solution)/shard_map/ppermute | solution.py:222
  51.8 5.2 %collective-permute-start.18 = (f32[1,384]{1,0:T(1,128)S(1)}, f32[1,384]{1,0:T(1,128)S(1)}, u32[]{:S(2)}, u32[]{:S(2)}) collective-permute-start(f32[1,384]{1,0:T(1,128)S(1)} %fusion.2.m0_ref), channel_id=1, source_target_pairs={{64,0},{65,1},{66,2},{67,3},{68,4},{69,5},{70,6},{71,7},{72,8},{73... | collective-permute-start | bytes 4616 | tf_op jit(solution)/shard_map/ppermute | solution.py:222
  52.7 4.8 %collective-permute-start.17 = (f32[1,384]{1,0:T(1,128)S(1)}, f32[1,384]{1,0:T(1,128)S(1)}, u32[]{:S(2)}, u32[]{:S(2)}) collective-permute-start(f32[1,384]{1,0:T(1,128)S(1)} %fusion.2.m0_ref), channel_id=1, source_target_pairs={{96,0},{97,1},{98,2},{99,3},{100,4},{101,5},{102,6},{103,7},{104,8... | collective-permute-start | bytes 4616 | tf_op jit(solution)/shard_map/ppermute | solution.py:222
  54.7 3.6 %collective-permute-start.16 = (f32[1,384]{1,0:T(1,128)S(1)}, f32[1,384]{1,0:T(1,128)S(1)}, u32[]{:S(2)}, u32[]{:S(2)}) collective-permute-start(f32[1,384]{1,0:T(1,128)S(1)} %fusion.2.m0_ref), channel_id=1, source_target_pairs={{32,0},{33,1},{34,2},{35,3},{36,4},{37,5},{38,6},{39,7},{40,8},{41... | collective-permute-start | bytes 4616 | tf_op jit(solution)/shard_map/ppermute | solution.py:222

commit v7 on v5

--- a/solution.py
+++ b/solution.py
@@ -247,9 +247,9 @@
             chunks[k] = receive(chunks[k], lambda x, y, z, c, step=step: (x - step, y, z, c))
     own = join(chunks)
 
-    az, ay = near_z(own), near_y(own)
+    ay, az = near_y(own), near_z(own)
     other = swap(own)
-    fz, fy = near_z(az), near_y(ay)
+    fy, fz = near_y(ay), near_z(az)
     bz, by = lax.optimization_barrier((near_z(other), near_y(other)))
     ay2, by2 = swap(ay), swap(by)
     s1 = pair_sums(

time: 59 us -> 59 us (level)
  no operation moved by 1% of the time
where the time goes in v7:
time: 59 us; the launch traced here: 58.9 us
  waiting for transfers between devices  25.3 us (43%)
  starting transfers between devices  22.1 us (37%)
  Pallas kernels  11.4 us (19%)
    ppermute x19, waiting for transfers between devices, receive(): return lax.ppermute(array, AXES, pairs_of(source_of))  25.3 us
    ppermute x19, starting transfers between devices, receive(): return lax.ppermute(array, AXES, pairs_of(source_of))  22.1 us
    pallas_call x4, Pallas kernels, pair_sums(): pl.pallas_call(functools.partial(pairs_kernel, nq, nk, plan), out_shape=j...  8.77 us
    pallas_call x1, Pallas kernels, prepare(): pl.pallas_call(prepare_kernel, out_shape=[chunk] * GROUPS + [jax.ShapeDty...  1.88 us
  transfers between devices with their start and end apart: 19, of which 14 were waited for; matrix products, arithmetic and copies ran while one was open for 0% of the time, Pallas kernels for 10%

profile of v7, /device:TPU:0, one launch (start us, length us, event | category | flops | bytes accessed | tf_op | source)
XLA Modules:
  0.0 58.9 jit_solution(8943443286094764599)
XLA Ops:
  0.0 1.9 %prepare.1 = (bf16[104,768]{1,0:T(8,128)(2,1)S(1)}, bf16[104,768]{1,0:T(8,128)(2,1)S(1)}, bf16[104,768]{1,0:T(8,128)(2,1)S(1)}, bf16[104,768]{1,0:T(8,128)(2,1)S(1)}, f32[1,384]{1,0:T(1,128)S(1)}) custom-call(s32[1]{0:T(128)} %bitcast.x_ref, bf16[384,768]{1,0:T(8,128)(2,1)} %emb_hbm.1, s32[384]{0:T(512)} %ids_hbm.1), custom_call_target="tpu_custom_call" | custom-call | tf_op jit(solution)/shard_map/prepare/pallas_call | solution.py:73
  1.9 1.6 %collective-permute-start = (bf16[104,768]{1,0:T(8,128)(2,1)S(1)}, bf16[104,768]{1,0:T(8,128)(2,1)S(1)}, u32[]{:S(2)}, u32[]{:S(2)}) collective-permute-start(bf16[104,768]{1,0:T(8,128)(2,1)S(1)} %get-tuple-element.16), channel_id=1, source_target_pairs={{96,0},{97,1},{98,2},{99,3},{100,4},{101,5},{102,6},{103,7},{104,8... | collective-permute-start | bytes 479240 | tf_op jit(solution)/shard_map/ppermute | solution.py:222
  3.5 1.7 %collective-permute-start.1 = (bf16[104,768]{1,0:T(8,128)(2,1)S(1)}, bf16[104,768]{1,0:T(8,128)(2,1)S(1)}, u32[]{:S(2)}, u32[]{:S(2)}) collective-permute-start(bf16[104,768]{1,0:T(8,128)(2,1)S(1)} %get-tuple-element.17), channel_id=1, source_target_pairs={{32,0},{33,1},{34,2},{35,3},{36,4},{37,5},{38,6},{39,7},{40,8},{41... | collective-permute-start | bytes 479240 | tf_op jit(solution)/shard_map/ppermute | solution.py:222
  5.2 1.9 %collective-permute-start.2 = (bf16[104,768]{1,0:T(8,128)(2,1)S(1)}, bf16[104,768]{1,0:T(8,128)(2,1)S(1)}, u32[]{:S(2)}, u32[]{:S(2)}) collective-permute-start(bf16[104,768]{1,0:T(8,128)(2,1)S(1)} %get-tuple-element.18), channel_id=1, source_target_pairs={{64,0},{65,1},{66,2},{67,3},{68,4},{69,5},{70,6},{71,7},{72,8},{73... | collective-permute-start | bytes 479240 | tf_op jit(solution)/shard_map/ppermute | solution.py:222
  7.1 1.8 %collective-permute-done.c1_ref = bf16[104,768]{1,0:T(8,128)(2,1)S(1)} collective-permute-done((bf16[104,768]{1,0:T(8,128)(2,1)S(1)}, bf16[104,768]{1,0:T(8,128)(2,1)S(1)}, u32[]{:S(2)}, u32[]{:S(2)}) %collective-permute-start) | collective-permute-done | bytes 159776 | tf_op jit(solution)/shard_map/ppermute | solution.py:222
  8.9 1.7 %collective-permute-done.1.c2_ref = bf16[104,768]{1,0:T(8,128)(2,1)S(1)} collective-permute-done((bf16[104,768]{1,0:T(8,128)(2,1)S(1)}, bf16[104,768]{1,0:T(8,128)(2,1)S(1)}, u32[]{:S(2)}, u32[]{:S(2)}) %collective-permute-start.1) | collective-permute-done | bytes 159776 | tf_op jit(solution)/shard_map/ppermute | solution.py:222
  10.6 2.9 %collective-permute-done.2.c3_ref = bf16[104,768]{1,0:T(8,128)(2,1)S(1)} collective-permute-done((bf16[104,768]{1,0:T(8,128)(2,1)S(1)}, bf16[104,768]{1,0:T(8,128)(2,1)S(1)}, u32[]{:S(2)}, u32[]{:S(2)}) %collective-permute-start.2) | collective-permute-done | bytes 159776 | tf_op jit(solution)/shard_map/ppermute | solution.py:222
  13.7 1.6 %collective-permute-start.4 = (bf16[392,768]{1,0:T(8,128)(2,1)S(1)}, bf16[392,768]{1,0:T(8,128)(2,1)S(1)}, u32[]{:S(2)}, u32[]{:S(2)}) collective-permute-start(bf16[392,768]{1,0:T(8,128)(2,1)S(1)} %join.1.refs_2_.refs_0_.refs_1_.refs_3_), channel_id=1, source_target_pairs={{24,0},{9,1},{26,2},{11,3},{28,4},{13,5},{30,6},{15,7},{0,8},{17,9... | collective-permute-start | bytes 1806344 | tf_op jit(solution)/shard_map/ppermute | solution.py:222
  15.3 1.9 %collective-permute-start.10 = (bf16[392,768]{1,0:T(8,128)(2,1)S(1)}, bf16[392,768]{1,0:T(8,128)(2,1)S(1)}, u32[]{:S(2)}, u32[]{:S(2)}) collective-permute-start(bf16[392,768]{1,0:T(8,128)(2,1)S(1)} %join.1.refs_2_.refs_0_.refs_1_.refs_3_), channel_id=1, source_target_pairs={{6,0},{3,1},{0,2},{5,3},{2,4},{7,5},{4,6},{1,7},{14,8},{11,9},{8,1... | collective-permute-start | bytes 1806344 | tf_op jit(solution)/shard_map/ppermute | solution.py:222
  17.2 1.6 %collective-permute-start.7 = (bf16[392,768]{1,0:T(8,128)(2,1)S(1)}, bf16[392,768]{1,0:T(8,128)(2,1)S(1)}, u32[]{:S(2)}, u32[]{:S(2)}) collective-permute-start(bf16[392,768]{1,0:T(8,128)(2,1)S(1)} %collective-permute-done.3.refs_3_.refs_2_.refs_4_), channel_id=1, source_target_pairs={{24,0},{9,1},{26,2},{11,3},{28,4},{13,5},{30,6},{15,7},{0,8},{17,9... | collective-permute-start | bytes 1806344 | tf_op jit(solution)/shard_map/ppermute | solution.py:222
  18.8 1.9 %collective-permute-start.6 = (bf16[392,768]{1,0:T(8,128)(2,1)S(1)}, bf16[392,768]{1,0:T(8,128)(2,1)S(1)}, u32[]{:S(2)}, u32[]{:S(2)}) collective-permute-start(bf16[392,768]{1,0:T(8,128)(2,1)S(1)} %collective-permute-done.3.refs_3_.refs_2_.refs_4_), channel_id=1, source_target_pairs={{6,0},{3,1},{0,2},{5,3},{2,4},{7,5},{4,6},{1,7},{14,8},{11,9},{8,1... | collective-permute-start | bytes 1806344 | tf_op jit(solution)/shard_map/ppermute | solution.py:222
  20.7 4.2 %collective-permute-done.4.refs_4_.refs_3_.refs_5_ = bf16[392,768]{1,0:T(8,128)(2,1)S(1)} collective-permute-done((bf16[392,768]{1,0:T(8,128)(2,1)S(1)}, bf16[392,768]{1,0:T(8,128)(2,1)S(1)}, u32[]{:S(2)}, u32[]{:S(2)}) %collective-permute-start.4) | collective-permute-done | bytes 602144 | tf_op jit(solution)/shard_map/ppermute | solution.py:222
  25.3 2.0 %collective-permute-done.10.refs_0_ = bf16[392,768]{1,0:T(8,128)(2,1)S(1)} collective-permute-done((bf16[392,768]{1,0:T(8,128)(2,1)S(1)}, bf16[392,768]{1,0:T(8,128)(2,1)S(1)}, u32[]{:S(2)}, u32[]{:S(2)}) %collective-permute-start.10) | collective-permute-done | bytes 602144 | tf_op jit(solution)/shard_map/ppermute | solution.py:222
  27.3 4.1 %collective-permute-done.7.refs_6_.refs_5_.refs_7_ = bf16[392,768]{1,0:T(8,128)(2,1)S(1)} collective-permute-done((bf16[392,768]{1,0:T(8,128)(2,1)S(1)}, bf16[392,768]{1,0:T(8,128)(2,1)S(1)}, u32[]{:S(2)}, u32[]{:S(2)}) %collective-permute-start.7) | collective-permute-done | bytes 602144 | tf_op jit(solution)/shard_map/ppermute | solution.py:222
  31.4 2.4 %collective-permute-done.6.refs_1_ = bf16[392,768]{1,0:T(8,128)(2,1)S(1)} collective-permute-done((bf16[392,768]{1,0:T(8,128)(2,1)S(1)}, bf16[392,768]{1,0:T(8,128)(2,1)S(1)}, u32[]{:S(2)}, u32[]{:S(2)}) %collective-permute-start.6) | collective-permute-done | bytes 602144 | tf_op jit(solution)/shard_map/ppermute | solution.py:222
  34.1 2.6 %pairs_a.1 = f32[2,1,384]{2,1,0:T(1,128)S(1)} custom-call(bf16[392,768]{1,0:T(8,128)(2,1)S(1)} %collective-permute-done.10.refs_0_, bf16[392,768]{1,0:T(8,128)(2,1)S(1)} %collective-permute-done.6.refs_1_, bf16[392,768]{1,0:T(8,128)(2,1)S(1)} %join.1.refs_2_.refs_0_.refs_1_.refs_3_, bf16[392,768]{1,0:T(8,128)(2,1)S(1)} %collective-permute-done.3.refs_3_.refs_2_.refs_4_, ...), custom_call_target="tpu_custom_call" | custom-call | flops 2264924160 | bytes 4128768 | tf_op jit(solution)/shard_map/pairs_a/pallas_call | solution.py:173
  36.7 1.2 %collective-permute-done.9.refs_7_.refs_9_.refs_3_ = bf16[392,768]{1,0:T(8,128)(2,1)S(1)} collective-permute-done((bf16[392,768]{1,0:T(8,128)(2,1)S(1)}, bf16[392,768]{1,0:T(8,128)(2,1)S(1)}, u32[]{:S(2)}, u32[]{:S(2)}) %collective-permute-start.9) | collective-permute-done | bytes 602144 | tf_op jit(solution)/shard_map/ppermute | solution.py:222
  37.9 1.2 %pairs_b.1 = f32[2,1,384]{2,1,0:T(1,128)S(1)} custom-call(bf16[392,768]{1,0:T(8,128)(2,1)S(1)} %collective-permute-done.10.refs_0_, bf16[392,768]{1,0:T(8,128)(2,1)S(1)} %collective-permute-done.6.refs_1_, bf16[392,768]{1,0:T(8,128)(2,1)S(1)} %collective-permute-done.8.refs_6_.refs_8_.refs_2_, bf16[392,768]{1,0:T(8,128)(2,1)S(1)} %collective-permute-done.9.refs_7_.refs_9_.refs_3_), custom_call_target="tpu_custom_call" | custom-call | flops 905969664 | bytes 2359296 | tf_op jit(solution)/shard_map/pairs_b/pallas_call | solution.py:173
  40.2 2.7 %pairs_f.1 = f32[3,1,384]{2,1,0:T(1,128)S(1)} custom-call(bf16[392,768]{1,0:T(8,128)(2,1)S(1)} %collective-permute-done.10.refs_0_, bf16[392,768]{1,0:T(8,128)(2,1)S(1)} %collective-permute-done.6.refs_1_, bf16[392,768]{1,0:T(8,128)(2,1)S(1)} %collective-permute-done.12.refs_2_, bf16[392,768]{1,0:T(8,128)(2,1)S(1)} %join.1.refs_2_.refs_0_.refs_1_.refs_3_, ...), custom_call_target="tpu_custom_call" | custom-call | flops 2264924160 | bytes 6488064 | tf_op jit(solution)/shard_map/pairs_f/pallas_call | solution.py:173
  42.9 3.7 %collective-permute-start.14 = (f32[1,384]{1,0:T(1,128)S(1)}, f32[1,384]{1,0:T(1,128)S(1)}, u32[]{:S(2)}, u32[]{:S(2)}) collective-permute-start(f32[1,384]{1,0:T(1,128)S(1)} %get-tuple-element.23), channel_id=1, source_target_pairs={{2,0},{7,1},{4,2},{1,3},{6,4},{3,5},{0,6},{5,7},{10,8},{15,9},{12,... | collective-permute-start | bytes 4616 | tf_op jit(solution)/shard_map/ppermute | solution.py:222
  46.7 1.3 %collective-permute-start.13 = (f32[1,384]{1,0:T(1,128)S(1)}, f32[1,384]{1,0:T(1,128)S(1)}, u32[]{:S(2)}, u32[]{:S(2)}) collective-permute-start(f32[1,384]{1,0:T(1,128)S(1)} %get-tuple-element.25), channel_id=1, source_target_pairs={{4,0},{5,1},{6,2},{7,3},{0,4},{1,5},{2,6},{3,7},{12,8},{13,9},{14,... | collective-permute-start | bytes 4616 | tf_op jit(solution)/shard_map/ppermute | solution.py:222
  48.0 2.3 %pairs_own.1 = f32[1,1,384]{2,1,0:T(1,128)S(1)} custom-call(bf16[392,768]{1,0:T(8,128)(2,1)S(1)} %join.1.refs_2_.refs_0_.refs_1_.refs_3_, bf16[392,768]{1,0:T(8,128)(2,1)S(1)} %join.1.refs_2_.refs_0_.refs_1_.refs_3_, bf16[392,768]{1,0:T(8,128)(2,1)S(1)} %collective-permute-done.3.refs_3_.refs_2_.refs_4_, ...), custom_call_target="tpu_custom_call" | custom-call | flops 1811939328 | bytes 5308416 | tf_op jit(solution)/shard_map/pairs_own/pallas_call | solution.py:173
  52.6 2.0 %collective-permute-start.17 = (f32[1,384]{1,0:T(1,128)S(1)}, f32[1,384]{1,0:T(1,128)S(1)}, u32[]{:S(2)}, u32[]{:S(2)}) collective-permute-start(f32[1,384]{1,0:T(1,128)S(1)} %fusion.3.m0_ref), channel_id=1, source_target_pairs={{96,0},{97,1},{98,2},{99,3},{100,4},{101,5},{102,6},{103,7},{104,8... | collective-permute-start | bytes 4616 | tf_op jit(solution)/shard_map/ppermute | solution.py:222
  54.6 1.2 %collective-permute-start.16 = (f32[1,384]{1,0:T(1,128)S(1)}, f32[1,384]{1,0:T(1,128)S(1)}, u32[]{:S(2)}, u32[]{:S(2)}) collective-permute-start(f32[1,384]{1,0:T(1,128)S(1)} %fusion.3.m0_ref), channel_id=1, source_target_pairs={{32,0},{33,1},{34,2},{35,3},{36,4},{37,5},{38,6},{39,7},{40,8},{41... | collective-permute-start | bytes 4616 | tf_op jit(solution)/shard_map/ppermute | solution.py:222
  (23 shorter events, 7.3 us)
Async XLA Ops:
  1.9 7.0 %collective-permute-start = (bf16[104,768]{1,0:T(8,128)(2,1)S(1)}, bf16[104,768]{1,0:T(8,128)(2,1)S(1)}, u32[]{:S(2)}, u32[]{:S(2)}) collective-permute-start(bf16[104,768]{1,0:T(8,128)(2,1)S(1)} %get-tuple-element.16), channel_id=1, source_target_pairs={{96,0},{97,1},{98,2},{99,3},{100,4},{101,5},{102,6},{103,7},{104,8... | collective-permute-start | bytes 479240 | tf_op jit(solution)/shard_map/ppermute | solution.py:222
  3.5 7.0 %collective-permute-start.1 = (bf16[104,768]{1,0:T(8,128)(2,1)S(1)}, bf16[104,768]{1,0:T(8,128)(2,1)S(1)}, u32[]{:S(2)}, u32[]{:S(2)}) collective-permute-start(bf16[104,768]{1,0:T(8,128)(2,1)S(1)} %get-tuple-element.17), channel_id=1, source_target_pairs={{32,0},{33,1},{34,2},{35,3},{36,4},{37,5},{38,6},{39,7},{40,8},{41... | collective-permute-start | bytes 479240 | tf_op jit(solution)/shard_map/ppermute | solution.py:222
  5.2 8.3 %collective-permute-start.2 = (bf16[104,768]{1,0:T(8,128)(2,1)S(1)}, bf16[104,768]{1,0:T(8,128)(2,1)S(1)}, u32[]{:S(2)}, u32[]{:S(2)}) collective-permute-start(bf16[104,768]{1,0:T(8,128)(2,1)S(1)} %get-tuple-element.18), channel_id=1, source_target_pairs={{64,0},{65,1},{66,2},{67,3},{68,4},{69,5},{70,6},{71,7},{72,8},{73... | collective-permute-start | bytes 479240 | tf_op jit(solution)/shard_map/ppermute | solution.py:222
  13.6 3.7 %collective-permute-start.3 = (bf16[392,768]{1,0:T(8,128)(2,1)S(1)}, bf16[392,768]{1,0:T(8,128)(2,1)S(1)}, u32[]{:S(2)}, u32[]{:S(2)}) collective-permute-start(bf16[392,768]{1,0:T(8,128)(2,1)S(1)} %join.1.refs_2_.refs_0_.refs_1_.refs_3_), channel_id=1, source_target_pairs={{1,0},{0,1},{3,2},{2,3},{5,4},{4,5},{7,6},{6,7},{9,8},{8,9},{11,10... | collective-permute-start | bytes 1806344 | tf_op jit(solution)/shard_map/ppermute | solution.py:222
  13.7 11.3 %collective-permute-start.4 = (bf16[392,768]{1,0:T(8,128)(2,1)S(1)}, bf16[392,768]{1,0:T(8,128)(2,1)S(1)}, u32[]{:S(2)}, u32[]{:S(2)}) collective-permute-start(bf16[392,768]{1,0:T(8,128)(2,1)S(1)} %join.1.refs_2_.refs_0_.refs_1_.refs_3_), channel_id=1, source_target_pairs={{24,0},{9,1},{26,2},{11,3},{28,4},{13,5},{30,6},{15,7},{0,8},{17,9... | collective-permute-start | bytes 1806344 | tf_op jit(solution)/shard_map/ppermute | solution.py:222
  15.3 12.0 %collective-permute-start.10 = (bf16[392,768]{1,0:T(8,128)(2,1)S(1)}, bf16[392,768]{1,0:T(8,128)(2,1)S(1)}, u32[]{:S(2)}, u32[]{:S(2)}) collective-permute-start(bf16[392,768]{1,0:T(8,128)(2,1)S(1)} %join.1.refs_2_.refs_0_.refs_1_.refs_3_), channel_id=1, source_target_pairs={{6,0},{3,1},{0,2},{5,3},{2,4},{7,5},{4,6},{1,7},{14,8},{11,9},{8,1... | collective-permute-start | bytes 1806344 | tf_op jit(solution)/shard_map/ppermute | solution.py:222
  17.2 14.2 %collective-permute-start.7 = (bf16[392,768]{1,0:T(8,128)(2,1)S(1)}, bf16[392,768]{1,0:T(8,128)(2,1)S(1)}, u32[]{:S(2)}, u32[]{:S(2)}) collective-permute-start(bf16[392,768]{1,0:T(8,128)(2,1)S(1)} %collective-permute-done.3.refs_3_.refs_2_.refs_4_), channel_id=1, source_target_pairs={{24,0},{9,1},{26,2},{11,3},{28,4},{13,5},{30,6},{15,7},{0,8},{17,9... | collective-permute-start | bytes 1806344 | tf_op jit(solution)/shard_map/ppermute | solution.py:222
  18.8 15.0 %collective-permute-start.6 = (bf16[392,768]{1,0:T(8,128)(2,1)S(1)}, bf16[392,768]{1,0:T(8,128)(2,1)S(1)}, u32[]{:S(2)}, u32[]{:S(2)}) collective-permute-start(bf16[392,768]{1,0:T(8,128)(2,1)S(1)} %collective-permute-done.3.refs_3_.refs_2_.refs_4_), channel_id=1, source_target_pairs={{6,0},{3,1},{0,2},{5,3},{2,4},{7,5},{4,6},{1,7},{14,8},{11,9},{8,1... | collective-permute-start | bytes 1806344 | tf_op jit(solution)/shard_map/ppermute | solution.py:222
  25.0 9.1 %collective-permute-start.5 = (bf16[392,768]{1,0:T(8,128)(2,1)S(1)}, bf16[392,768]{1,0:T(8,128)(2,1)S(1)}, u32[]{:S(2)}, u32[]{:S(2)}) collective-permute-start(bf16[392,768]{1,0:T(8,128)(2,1)S(1)} %collective-permute-done.4.refs_4_.refs_3_.refs_5_), channel_id=1, source_target_pairs={{1,0},{0,1},{3,2},{2,3},{5,4},{4,5},{7,6},{6,7},{9,8},{8,9},{11,10... | collective-permute-start | bytes 1806344 | tf_op jit(solution)/shard_map/ppermute | solution.py:222
  25.0 12.9 %collective-permute-start.9 = (bf16[392,768]{1,0:T(8,128)(2,1)S(1)}, bf16[392,768]{1,0:T(8,128)(2,1)S(1)}, u32[]{:S(2)}, u32[]{:S(2)}) collective-permute-start(bf16[392,768]{1,0:T(8,128)(2,1)S(1)} %collective-permute-done.4.refs_4_.refs_3_.refs_5_), channel_id=1, source_target_pairs={{24,0},{9,1},{26,2},{11,3},{28,4},{13,5},{30,6},{15,7},{0,8},{17,9... | collective-permute-start | bytes 1806344 | tf_op jit(solution)/shard_map/ppermute | solution.py:222
  27.3 12.9 %collective-permute-start.12 = (bf16[392,768]{1,0:T(8,128)(2,1)S(1)}, bf16[392,768]{1,0:T(8,128)(2,1)S(1)}, u32[]{:S(2)}, u32[]{:S(2)}) collective-permute-start(bf16[392,768]{1,0:T(8,128)(2,1)S(1)} %collective-permute-done.10.refs_0_), channel_id=1, source_target_pairs={{6,0},{3,1},{0,2},{5,3},{2,4},{7,5},{4,6},{1,7},{14,8},{11,9},{8,1... | collective-permute-start | bytes 1806344 | tf_op jit(solution)/shard_map/ppermute | solution.py:222
  33.8 4.1 %collective-permute-start.8 = (bf16[392,768]{1,0:T(8,128)(2,1)S(1)}, bf16[392,768]{1,0:T(8,128)(2,1)S(1)}, u32[]{:S(2)}, u32[]{:S(2)}) collective-permute-start(bf16[392,768]{1,0:T(8,128)(2,1)S(1)} %collective-permute-done.7.refs_6_.refs_5_.refs_7_), channel_id=1, source_target_pairs={{1,0},{0,1},{3,2},{2,3},{5,4},{4,5},{7,6},{6,7},{9,8},{8,9},{11,10... | collective-permute-start | bytes 1806344 | tf_op jit(solution)/shard_map/ppermute | solution.py:222
  37.9 2.4 %collective-permute-start.11 = (bf16[392,768]{1,0:T(8,128)(2,1)S(1)}, bf16[392,768]{1,0:T(8,128)(2,1)S(1)}, u32[]{:S(2)}, u32[]{:S(2)}) collective-permute-start(bf16[392,768]{1,0:T(8,128)(2,1)S(1)} %collective-permute-done.9.refs_7_.refs_9_.refs_3_), channel_id=1, source_target_pairs={{1,0},{0,1},{3,2},{2,3},{5,4},{4,5},{7,6},{6,7},{9,8},{8,9},{11,10... | collective-permute-start | bytes 1806344 | tf_op jit(solution)/shard_map/ppermute | solution.py:222
  42.9 7.4 %collective-permute-start.14 = (f32[1,384]{1,0:T(1,128)S(1)}, f32[1,384]{1,0:T(1,128)S(1)}, u32[]{:S(2)}, u32[]{:S(2)}) collective-permute-start(f32[1,384]{1,0:T(1,128)S(1)} %get-tuple-element.23), channel_id=1, source_target_pairs={{2,0},{7,1},{4,2},{1,3},{6,4},{3,5},{0,6},{5,7},{10,8},{15,9},{12,... | collective-permute-start | bytes 4616 | tf_op jit(solution)/shard_map/ppermute | solution.py:222
  46.7 4.2 %collective-permute-start.15 = (f32[1,384]{1,0:T(1,128)S(1)}, f32[1,384]{1,0:T(1,128)S(1)}, u32[]{:S(2)}, u32[]{:S(2)}) collective-permute-start(f32[1,384]{1,0:T(1,128)S(1)} %get-tuple-element.24), channel_id=1, source_target_pairs={{7,0},{2,1},{1,2},{4,3},{3,4},{6,5},{5,6},{0,7},{15,8},{10,9},{9,1... | collective-permute-start | bytes 4616 | tf_op jit(solution)/shard_map/ppermute | solution.py:222
  46.7 5.1 %collective-permute-start.13 = (f32[1,384]{1,0:T(1,128)S(1)}, f32[1,384]{1,0:T(1,128)S(1)}, u32[]{:S(2)}, u32[]{:S(2)}) collective-permute-start(f32[1,384]{1,0:T(1,128)S(1)} %get-tuple-element.25), channel_id=1, source_target_pairs={{4,0},{5,1},{6,2},{7,3},{0,4},{1,5},{2,6},{3,7},{12,8},{13,9},{14,... | collective-permute-start | bytes 4616 | tf_op jit(solution)/shard_map/ppermute | solution.py:222
  51.8 5.1 %collective-permute-start.18 = (f32[1,384]{1,0:T(1,128)S(1)}, f32[1,384]{1,0:T(1,128)S(1)}, u32[]{:S(2)}, u32[]{:S(2)}) collective-permute-start(f32[1,384]{1,0:T(1,128)S(1)} %fusion.3.m0_ref), channel_id=1, source_target_pairs={{64,0},{65,1},{66,2},{67,3},{68,4},{69,5},{70,6},{71,7},{72,8},{73... | collective-permute-start | bytes 4616 | tf_op jit(solution)/shard_map/ppermute | solution.py:222
  52.6 4.8 %collective-permute-start.17 = (f32[1,384]{1,0:T(1,128)S(1)}, f32[1,384]{1,0:T(1,128)S(1)}, u32[]{:S(2)}, u32[]{:S(2)}) collective-permute-start(f32[1,384]{1,0:T(1,128)S(1)} %fusion.3.m0_ref), channel_id=1, source_target_pairs={{96,0},{97,1},{98,2},{99,3},{100,4},{101,5},{102,6},{103,7},{104,8... | collective-permute-start | bytes 4616 | tf_op jit(solution)/shard_map/ppermute | solution.py:222
  54.6 3.6 %collective-permute-start.16 = (f32[1,384]{1,0:T(1,128)S(1)}, f32[1,384]{1,0:T(1,128)S(1)}, u32[]{:S(2)}, u32[]{:S(2)}) collective-permute-start(f32[1,384]{1,0:T(1,128)S(1)} %fusion.3.m0_ref), channel_id=1, source_target_pairs={{32,0},{33,1},{34,2},{35,3},{36,4},{37,5},{38,6},{39,7},{40,8},{41... | collective-permute-start | bytes 4616 | tf_op jit(solution)/shard_map/ppermute | solution.py:222
